TPU v7x, 32 devices: a whole 2x2x4 slice. The times are simulated.
32 devices in a mesh: dp: 8 (over z, core), seq: 4 (over y, x).
Axes of the slice: x: 2, y: 2, z: 4, core: 2. Of those that a mesh axis runs over, the one named last changes fastest.
Arguments:
- tokens: bfloat16 [16, 2048, 1024], P('dp', 'seq'), may hold values from -6 to 6
- cotangent: bfloat16 [16, 2048, 1024], P('dp', 'seq'), may hold values from -6 to 6
- lengths: int32 [16], P('dp'), may hold values from 1 to 2048, 20480 in all
- species: int32 [16], P('dp'), may hold values from 0 to 7
- ln1_gain: bfloat16 [1024], P(('dp', 'seq')), may hold values from 0.5 to 1.5
- ln1_bias: bfloat16 [1024], P(('dp', 'seq')), may hold values from -3 to 3
- w_query: bfloat16 [1024, 1024], P(('dp', 'seq')), may hold values from -0.1875 to 0.1875
- w_key: bfloat16 [1024, 1024], P(('dp', 'seq')), may hold values from -0.1875 to 0.1875
- w_value: bfloat16 [1024, 1024], P(('dp', 'seq')), may hold values from -0.1875 to 0.1875
- w_out: bfloat16 [1024, 1024], P(('dp', 'seq')), may hold values from -1.5 to 1.5
- ln2_gain: bfloat16 [1024], P(('dp', 'seq')), may hold values from 0.5 to 1.5
- ln2_bias: bfloat16 [1024], P(('dp', 'seq')), may hold values from -3 to 3
- w_gate: bfloat16 [1024, 4096], P(('dp', 'seq')), may hold values from -0.1875 to 0.1875
- w_up: bfloat16 [1024, 4096], P(('dp', 'seq')), may hold values from -0.1875 to 0.1875
- w_down: bfloat16 [4096, 1024], P(('dp', 'seq')), may hold values from -0.09375 to 0.09375
Outputs:
- output: float32 [16, 2048, 1024], P('dp', 'seq')
- grad_tokens: float32 [16, 2048, 1024], P('dp', 'seq')
- grad_ln1_gain: float32 [1024], P(('dp', 'seq'))
- grad_ln1_bias: float32 [1024], P(('dp', 'seq'))
- grad_w_query: float32 [1024, 1024], P(('dp', 'seq'))
- grad_w_key: float32 [1024, 1024], P(('dp', 'seq'))
- grad_w_value: float32 [1024, 1024], P(('dp', 'seq'))
- grad_w_out: float32 [1024, 1024], P(('dp', 'seq'))
- grad_ln2_gain: float32 [1024], P(('dp', 'seq'))
- grad_ln2_bias: float32 [1024], P(('dp', 'seq'))
- grad_w_gate: float32 [1024, 4096], P(('dp', 'seq'))
- grad_w_up: float32 [1024, 4096], P(('dp', 'seq'))
- grad_w_down: float32 [4096, 1024], P(('dp', 'seq'))
Inputs may be any that keep to these rules, and one draw needn't show every extreme that they name: The lengths of all windows sum to 16 * 2048 * 5 // 8 and the longest is exactly 2048.
All inputs are finite; a program needn't handle non-finite values. No bound on the sum of `lengths` on one device may be relied on, other than what follows from the above.
Results may differ from a plain program's by a relative error of at most 0.015.
Values may be sent and summed in bfloat16 or wider, within the bound.
No kernel may reach another device: no remote copies, remote signals or barrier semaphores. Data moves between devices by JAX's collectives and lax.ppermute only.
A program may use at most 256 MiB of HBM per device.

v0:
```python
import jax
import jax.numpy as jnp
from jax import lax
from jax.sharding import PartitionSpec as P

HEAD_DIM = 64
SPECIES = 8


EPS = 1e-05
heads_together = 4


def layer_norm(value, gain, bias):
    mean_v = jnp.mean(value, axis=-1, keepdims=True)
    centered = value - mean_v
    var_v = jnp.mean(centered * centered, axis=-1, keepdims=True)
    inverse = lax.rsqrt(var_v + EPS)
    normal = centered * inverse
    return (normal * gain + bias, normal, inverse)


def norm_back(grad, normal, inverse, gain):
    scaled = grad * gain
    centered = scaled - jnp.mean(scaled, axis=-1, keepdims=True)
    return inverse * (centered - normal * jnp.mean(scaled * normal, axis=-1, keepdims=True))


def rotary(value, cosine, sine):
    half = value.shape[-1] // 2
    first = value[..., :half]
    second = value[..., half:]
    cos_wide = cosine[None, :, None, :]
    sin_wide = sine[None, :, None, :]
    return jnp.concatenate(
        [first * cos_wide - second * sin_wide, second * cos_wide + first * sin_wide], axis=-1
    )


def to_groups(value, heads):
    wins, rows, width = value.shape
    groups = heads // heads_together
    split = value.reshape(wins, rows, groups, heads_together, width // heads)
    return split.transpose(0, 2, 1, 3, 4).reshape(
        wins * groups, rows, heads_together, width // heads
    )


def from_groups(value, wins):
    items, rows, per_group, dim = value.shape
    groups = items // wins
    joined = value.reshape(wins, groups, rows, per_group, dim).transpose(0, 2, 1, 3, 4)
    return joined.reshape(wins, rows, groups * per_group * dim)


def scores_of(query, key, length, factor):
    raw = jnp.einsum("thd,khd->htk", query, key, preferred_element_type=jnp.float32)
    valid = jnp.arange(key.shape[0]) < length
    return jnp.where(valid[None, None, :], raw * factor, -1e30)


def angles_of(positions):
    half = HEAD_DIM // 2
    freq = 10000.0 ** (-2.0 * jnp.arange(half, dtype=jnp.float32) / HEAD_DIM)
    angle = positions.astype(jnp.float32)[:, None] * freq[None, :]
    return (jnp.cos(angle), jnp.sin(angle))


def body(
    tokens,
    cotangent,
    lengths,
    species,
    ln1_gain,
    ln1_bias,
    w_query,
    w_key,
    w_value,
    w_out,
    ln2_gain,
    ln2_bias,
    w_gate,
    w_up,
    w_down,
):
    wins, rows, width = tokens.shape
    heads = width // HEAD_DIM
    groups = heads // heads_together
    factor = HEAD_DIM ** (-0.5)
    species_ids = jnp.arange(SPECIES)
    onehot = (species[:, None] == species_ids[None, :]).astype(jnp.float32)
    counts = lax.psum(jnp.sum(onehot * lengths[:, None].astype(jnp.float32), axis=0), "dp")
    window_weight = SPECIES * jnp.sum(onehot * counts[None, :], axis=1) / jnp.sum(counts)
    weights = (
        lax.all_gather(ln1_gain, ("dp", "seq"), axis=0, tiled=True),
        lax.all_gather(ln1_bias, ("dp", "seq"), axis=0, tiled=True),
        lax.all_gather(w_query, ("dp", "seq"), axis=0, tiled=True),
        lax.all_gather(w_key, ("dp", "seq"), axis=0, tiled=True),
        lax.all_gather(w_value, ("dp", "seq"), axis=0, tiled=True),
        lax.all_gather(w_out, ("dp", "seq"), axis=0, tiled=True),
        lax.all_gather(ln2_gain, ("dp", "seq"), axis=0, tiled=True),
        lax.all_gather(ln2_bias, ("dp", "seq"), axis=0, tiled=True),
        lax.all_gather(w_gate, ("dp", "seq"), axis=0, tiled=True),
        lax.all_gather(w_up, ("dp", "seq"), axis=0, tiled=True),
        lax.all_gather(w_down, ("dp", "seq"), axis=0, tiled=True),
    )
    gain_one, bias_one, query_w, key_w, value_w, out_w, gain_two, bias_two, gate_w, up_w, down_w = (
        weights
    )
    positions = lax.axis_index("seq") * rows + jnp.arange(rows)
    cosine, sine = angles_of(positions)
    row_scale = jnp.where(positions[None, :] < lengths[:, None], window_weight[:, None], 0.0)
    inputs = tokens.astype(jnp.float32)
    normed, normal_one, inverse_one = layer_norm(
        inputs, gain_one.astype(jnp.float32), bias_one.astype(jnp.float32)
    )
    normed_low = normed.astype(jnp.bfloat16)

    def project(weight):
        product = jnp.einsum("wtd,de->wte", normed_low, weight, preferred_element_type=jnp.float32)
        return product.reshape(wins, rows, heads, HEAD_DIM)

    query = rotary(project(query_w), cosine, sine).reshape(wins, rows, width).astype(jnp.bfloat16)
    key = rotary(project(key_w), cosine, sine).reshape(wins, rows, width).astype(jnp.bfloat16)
    value = project(value_w).reshape(wins, rows, width).astype(jnp.bfloat16)

    def attend_item(items):
        query_g, key_g, value_g, length = items
        scores = scores_of(query_g, key_g, length, factor)
        top = jnp.max(scores, axis=-1, keepdims=True)
        lse = top + jnp.log(jnp.sum(jnp.exp(scores - top), axis=-1, keepdims=True))
        probs = jnp.exp(scores - lse).astype(jnp.bfloat16)
        return (jnp.einsum("htk,khd->thd", probs, value_g, preferred_element_type=jnp.float32), lse)

    def attend_back(items):
        query_g, key_g, value_g, length, lse, grad_g = items
        scores = scores_of(query_g, key_g, length, factor)
        probs = jnp.exp(scores - lse)
        probs_low = probs.astype(jnp.bfloat16)
        grad_value = jnp.einsum(
            "htk,thd->khd", probs_low, grad_g, preferred_element_type=jnp.float32
        )
        grad_probs = jnp.einsum("thd,khd->htk", grad_g, value_g, preferred_element_type=jnp.float32)
        inner = jnp.sum(probs * grad_probs, axis=-1, keepdims=True)
        grad_scores = (probs * (grad_probs - inner)).astype(jnp.bfloat16)
        grad_query = factor * jnp.einsum(
            "htk,khd->thd", grad_scores, key_g, preferred_element_type=jnp.float32
        )
        grad_key = factor * jnp.einsum(
            "htk,thd->khd", grad_scores, query_g, preferred_element_type=jnp.float32
        )
        return (grad_query, grad_key, grad_value)

    key_all, value_all = (
        lax.all_gather(key, "seq", axis=1, tiled=True),
        lax.all_gather(value, "seq", axis=1, tiled=True),
    )
    item_lengths = jnp.repeat(lengths, groups)
    mixed_items, lse_items = lax.map(
        attend_item,
        (
            to_groups(query, heads),
            to_groups(key_all, heads),
            to_groups(value_all, heads),
            item_lengths,
        ),
    )
    mixed = from_groups(mixed_items, wins).astype(jnp.bfloat16)
    middle = inputs + jnp.einsum("wtd,de->wte", mixed, out_w, preferred_element_type=jnp.float32)
    normed_two, normal_two, inverse_two = layer_norm(
        middle, gain_two.astype(jnp.float32), bias_two.astype(jnp.float32)
    )
    normed_two_low = normed_two.astype(jnp.bfloat16)
    gate = jnp.einsum("wtd,df->wtf", normed_two_low, gate_w, preferred_element_type=jnp.float32)
    upper = jnp.einsum("wtd,df->wtf", normed_two_low, up_w, preferred_element_type=jnp.float32)
    sigma = jax.nn.sigmoid(gate)
    hidden = (gate * sigma * upper).astype(jnp.bfloat16)
    output = middle + jnp.einsum("wtf,fd->wtd", hidden, down_w, preferred_element_type=jnp.float32)
    weights_back = (
        lax.all_gather(ln1_gain, ("dp", "seq"), axis=0, tiled=True),
        lax.all_gather(ln1_bias, ("dp", "seq"), axis=0, tiled=True),
        lax.all_gather(w_query, ("dp", "seq"), axis=0, tiled=True),
        lax.all_gather(w_key, ("dp", "seq"), axis=0, tiled=True),
        lax.all_gather(w_value, ("dp", "seq"), axis=0, tiled=True),
        lax.all_gather(w_out, ("dp", "seq"), axis=0, tiled=True),
        lax.all_gather(ln2_gain, ("dp", "seq"), axis=0, tiled=True),
        lax.all_gather(ln2_bias, ("dp", "seq"), axis=0, tiled=True),
        lax.all_gather(w_gate, ("dp", "seq"), axis=0, tiled=True),
        lax.all_gather(w_up, ("dp", "seq"), axis=0, tiled=True),
        lax.all_gather(w_down, ("dp", "seq"), axis=0, tiled=True),
    )
    gain_one, bias_one, query_w, key_w, value_w, out_w, gain_two, bias_two, gate_w, up_w, down_w = (
        weights_back
    )
    grad_out = cotangent.astype(jnp.float32) * row_scale[:, :, None]
    grad_low = grad_out.astype(jnp.bfloat16)
    grad_down = jnp.einsum("wtf,wtd->fd", hidden, grad_low, preferred_element_type=jnp.float32)
    grad_hidden = jnp.einsum("wtd,fd->wtf", grad_low, down_w, preferred_element_type=jnp.float32)
    grad_up = (grad_hidden * gate * sigma).astype(jnp.bfloat16)
    grad_gate = (grad_hidden * upper * sigma * (1.0 + gate * (1.0 - sigma))).astype(jnp.bfloat16)
    grad_gate_w = jnp.einsum(
        "wtd,wtf->df", normed_two_low, grad_gate, preferred_element_type=jnp.float32
    )
    grad_up_w = jnp.einsum(
        "wtd,wtf->df", normed_two_low, grad_up, preferred_element_type=jnp.float32
    )
    grad_normed_two = jnp.einsum(
        "wtf,df->wtd", grad_gate, gate_w, preferred_element_type=jnp.float32
    )
    grad_normed_two = grad_normed_two + jnp.einsum(
        "wtf,df->wtd", grad_up, up_w, preferred_element_type=jnp.float32
    )
    grad_gain_two = jnp.sum(grad_normed_two * normal_two, axis=(0, 1))
    grad_bias_two = jnp.sum(grad_normed_two, axis=(0, 1))
    grad_middle = grad_out + norm_back(
        grad_normed_two, normal_two, inverse_two, gain_two.astype(jnp.float32)
    )
    grad_middle_low = grad_middle.astype(jnp.bfloat16)
    grad_out_w = jnp.einsum(
        "wtd,wte->de", mixed, grad_middle_low, preferred_element_type=jnp.float32
    )
    grad_mixed = jnp.einsum(
        "wte,de->wtd", grad_middle_low, out_w, preferred_element_type=jnp.float32
    ).astype(jnp.bfloat16)
    grad_q_items, grad_k_items, grad_v_items = lax.map(
        attend_back,
        (
            to_groups(query, heads),
            to_groups(key_all, heads),
            to_groups(value_all, heads),
            item_lengths,
            lse_items,
            to_groups(grad_mixed, heads),
        ),
    )
    grad_query = from_groups(grad_q_items, wins)
    grad_key_part = from_groups(grad_k_items, wins)
    grad_value_part = from_groups(grad_v_items, wins)
    grad_key_sum, grad_value_sum = (
        lax.psum_scatter(
            grad_key_part.astype(jnp.bfloat16), "seq", scatter_dimension=1, tiled=True
        ).astype(jnp.float32),
        lax.psum_scatter(
            grad_value_part.astype(jnp.bfloat16), "seq", scatter_dimension=1, tiled=True
        ).astype(jnp.float32),
    )
    grad_q_low = (
        rotary(grad_query.reshape(wins, rows, heads, HEAD_DIM), cosine, -sine)
        .reshape(wins, rows, width)
        .astype(jnp.bfloat16)
    )
    grad_k_low = (
        rotary(grad_key_sum.reshape(wins, rows, heads, HEAD_DIM), cosine, -sine)
        .reshape(wins, rows, width)
        .astype(jnp.bfloat16)
    )
    grad_v_low = grad_value_sum.astype(jnp.bfloat16)
    grad_query_w = jnp.einsum(
        "wtd,wte->de", normed_low, grad_q_low, preferred_element_type=jnp.float32
    )
    grad_key_w = jnp.einsum(
        "wtd,wte->de", normed_low, grad_k_low, preferred_element_type=jnp.float32
    )
    grad_value_w = jnp.einsum(
        "wtd,wte->de", normed_low, grad_v_low, preferred_element_type=jnp.float32
    )
    grad_normed = jnp.einsum("wte,de->wtd", grad_q_low, query_w, preferred_element_type=jnp.float32)
    grad_normed = grad_normed + jnp.einsum(
        "wte,de->wtd", grad_k_low, key_w, preferred_element_type=jnp.float32
    )
    grad_normed = grad_normed + jnp.einsum(
        "wte,de->wtd", grad_v_low, value_w, preferred_element_type=jnp.float32
    )
    grad_gain_one = jnp.sum(grad_normed * normal_one, axis=(0, 1))
    grad_bias_one = jnp.sum(grad_normed, axis=(0, 1))
    grad_inputs = grad_middle + norm_back(
        grad_normed, normal_one, inverse_one, gain_one.astype(jnp.float32)
    )
    summed = (
        lax.psum_scatter(grad_gain_one, ("dp", "seq"), scatter_dimension=0, tiled=True),
        lax.psum_scatter(grad_bias_one, ("dp", "seq"), scatter_dimension=0, tiled=True),
        lax.psum_scatter(grad_query_w, ("dp", "seq"), scatter_dimension=0, tiled=True),
        lax.psum_scatter(grad_key_w, ("dp", "seq"), scatter_dimension=0, tiled=True),
        lax.psum_scatter(grad_value_w, ("dp", "seq"), scatter_dimension=0, tiled=True),
        lax.psum_scatter(grad_out_w, ("dp", "seq"), scatter_dimension=0, tiled=True),
        lax.psum_scatter(grad_gain_two, ("dp", "seq"), scatter_dimension=0, tiled=True),
        lax.psum_scatter(grad_bias_two, ("dp", "seq"), scatter_dimension=0, tiled=True),
        lax.psum_scatter(grad_gate_w, ("dp", "seq"), scatter_dimension=0, tiled=True),
        lax.psum_scatter(grad_up_w, ("dp", "seq"), scatter_dimension=0, tiled=True),
        lax.psum_scatter(grad_down, ("dp", "seq"), scatter_dimension=0, tiled=True),
    )
    return (
        output,
        grad_inputs,
        summed[0],
        summed[1],
        summed[2],
        summed[3],
        summed[4],
        summed[5],
        summed[6],
        summed[7],
        summed[8],
        summed[9],
        summed[10],
    )


def solution(mesh):
    return jax.shard_map(
        body,
        mesh=mesh,
        in_specs=(
            P("dp", "seq", None),
            P("dp", "seq", None),
            P("dp"),
            P("dp"),
            P(("dp", "seq")),
            P(("dp", "seq")),
            P(("dp", "seq"), None),
            P(("dp", "seq"), None),
            P(("dp", "seq"), None),
            P(("dp", "seq"), None),
            P(("dp", "seq")),
            P(("dp", "seq")),
            P(("dp", "seq"), None),
            P(("dp", "seq"), None),
            P(("dp", "seq"), None),
        ),
        out_specs=(
            P("dp", "seq", None),
            P("dp", "seq", None),
            P(("dp", "seq")),
            P(("dp", "seq")),
            P(("dp", "seq"), None),
            P(("dp", "seq"), None),
            P(("dp", "seq"), None),
            P(("dp", "seq"), None),
            P(("dp", "seq")),
            P(("dp", "seq")),
            P(("dp", "seq"), None),
            P(("dp", "seq"), None),
            P(("dp", "seq"), None),
        ),
        check_vma=False,
    )
```

profile of v0, /device:TPU:0, one launch (start us, length us, event | category | flops | bytes accessed | tf_op | source)
XLA Modules:
  0.0 2916.9 jit_solution(1059704391594096941)
XLA Ops:
  13.4 42.2 %all-reduce.9 = (bf16[1024]{0:T(1024)(128)(2,1)S(1)}, bf16[1024]{0:T(1024)(128)(2,1)S(1)}, bf16[1024]{0:T(1024)(128)(2,1)S(1)}, bf16[1024]{0:T(1024)(128)(2,1)S(1)}) all-reduce(bf16[1024]{0:T(1024)(128)(2,1)S(1)} %dynamic-update-slice.1, bf16[1024]{0:T(1024)(128)(2,1)S(1)} %dynamic-update-slice, ...), channel_id=1, replica_groups=mesh['dp'=8,'seq'=4] {'dp','seq'}, use_global_device_ids=true, to_apply=%add.1 | all-reduce | flops 4096 | bytes 16384
  76.7 51.6 %all-gather.16.cloned.1.call-done = bf16[1024,1024]{1,0:T(8,128)(2,1)} async-done(((bf16[32,1024]{1,0:T(8,128)(2,1)}), bf16[1024,1024]{1,0:T(8,128)(2,1)}) %all-gather.16.cloned.1.call-update) | async-done | bytes 2097168 | tf_op jit(solution)/shard_map/all_gather | solution.py:98
  134.6 51.9 %all-gather.14.cloned.1.call-done = bf16[1024,1024]{1,0:T(8,128)(2,1)} async-done(((bf16[32,1024]{1,0:T(8,128)(2,1)}), bf16[1024,1024]{1,0:T(8,128)(2,1)}) %all-gather.14.cloned.1.call-update) | async-done | bytes 2097168 | tf_op jit(solution)/shard_map/all_gather | solution.py:97
  224.0 41.7 %all-gather.26.cloned.1.call-done = bf16[4096,1024]{1,0:T(8,128)(2,1)} async-done(((bf16[128,1024]{1,0:T(8,128)(2,1)}), bf16[4096,1024]{1,0:T(8,128)(2,1)}) %all-gather.26.cloned.1.call-update) | async-done | bytes 8388624 | tf_op jit(solution)/shard_map/all_gather | solution.py:105
  280.2 74.0 %all-gather.12.cloned.1.call-done = bf16[2,2048,1024]{2,1,0:T(8,128)(2,1)} async-done(((bf16[2,512,1024]{2,1,0:T(8,128)(2,1)}), bf16[2,2048,1024]{2,1,0:T(8,128)(2,1)}) %all-gather.12.cloned.1.call-update) | async-done | bytes 8388624 | tf_op jit(solution)/shard_map/all_gather | solution.py:156
  366.3 77.1 %all-gather.18.cloned.1.call-done = bf16[2,2048,1024]{1,2,0:T(8,128)(2,1)} async-done(((bf16[2,512,1024]{1,2,0:T(8,128)(2,1)}), bf16[2,2048,1024]{1,2,0:T(8,128)(2,1)}) %all-gather.18.cloned.1.call-update) | async-done | bytes 8388624 | tf_op jit(solution)/shard_map/all_gather | solution.py:155
  443.4 121.9 %while.28 = (s32[]{:T(128)}, bf16[8,512,4,64]{1,3,2,0:T(8,128)(2,1)}, f32[8,4,512,1]{2,1,3,0:T(4,128)}, bf16[8,2048,4,64]{1,3,2,0:T(8,128)(2,1)}, s32[8]{0:T(128...) while((s32[]{:T(128)}, bf16[8,512,4,64]{1,3,2,0:T(8,128)(2,1)}, ...), condition=%wide.region_5.6_spmd.clone, body=%wide.region_2.5_spmd.sunk.clone | while | flops 1119879168 | bytes 53291112 | solution.py:159
  596.6 64.6 %all-gather.22.cloned.1.call-done = bf16[1024,4096]{1,0:T(8,128)(2,1)} async-done(((bf16[32,4096]{1,0:T(8,128)(2,1)}), bf16[1024,4096]{1,0:T(8,128)(2,1)}) %all-gather.22.cloned.1.call-update) | async-done | bytes 8388624 | tf_op jit(solution)/shard_map/all_gather | solution.py:103
  661.2 27.9 multiply_convert_fusion.2
  704.5 16.2 multiply_reduce_fusion.1
  731.0 351.8 %while.29 = (s32[]{:T(128)}, f32[8,512,4,64]{1,3,2,0:T(8,128)}, bf16[8,2048,4,64]{1,3,2,0:T(8,128)(2,1)}, bf16[8,2048,4,64]{1,3,2,0:T(8,128)(2,1)}, bf16[8,2048,...) while((s32[]{:T(128)}, f32[8,512,4,64]{1,3,2,0:T(8,128)}, ...), condition=%wide.region_16.17_spmd.clone, body=%wide.region_14.16_spmd.sunk.clone | while | flops 2747924480 | bytes 134812800 | solution.py:225
  1091.4 76.5 %reduce-scatter.10.cloned.1.call-done = bf16[2,512,1024]{1,2,0:T(8,128)(2,1)} async-done(((bf16[2,2048,1024]{1,2,0:T(8,128)(2,1)}), bf16[2,512,1024]{1,2,0:T(8,128)(2,1)}) %reduce-scatter.10.cloned.1.call-update) | async-done | bytes 2097168 | tf_op jit(solution)/shard_map/reduce_scatter | solution.py:240
  1187.9 69.8 %reduce-scatter.12.cloned.1.call-done = bf16[2,512,1024]{1,2,0:T(8,128)(2,1)} async-done(((bf16[2,2048,1024]{1,2,0:T(8,128)(2,1)}), bf16[2,512,1024]{1,2,0:T(8,128)(2,1)}) %reduce-scatter.12.cloned.1.call-update) | async-done | bytes 2097168 | tf_op jit(solution)/shard_map/reduce_scatter | solution.py:243
  1264.2 16.3 convolution_bitcast_fusion.2
  1280.5 16.2 convolution_bitcast_fusion.1
  1297.4 16.4 convolution_bitcast_fusion
  1313.9 16.0 fusion.83
  1340.5 39.9 %all-reduce.8 = (f32[1024]{0:T(1024)S(1)}, f32[1024]{0:T(1024)S(1)}, f32[1024]{0:T(1024)S(1)}, f32[1024]{0:T(1024)S(1)}) all-reduce(f32[1024]{0:T(1024)S(1)} %get-tuple-element.163, f32[1024]{0:T(1024)S(1)} %get-tuple-element.168, f32[1024]{0:T(1024)S(1)} %copy-done.29, ...), channel_id=4, replica_groups=mesh['dp'=8,'seq'=4] {'dp','seq'}, use_global_device_ids=true, to_apply=%region_22.23.clone | all-reduce | flops 4096 | bytes 32768
  1401.9 142.2 %reduce-scatter.14.cloned.1.call-done = f32[32,1024]{1,0:T(8,128)} async-done(((f32[1024,1024]{1,0:T(8,128)}), f32[32,1024]{1,0:T(8,128)}) %reduce-scatter.14.cloned.1.call-update) | async-done | bytes 131088 | tf_op jit(solution)/shard_map/reduce_scatter | solution.py:282
  1544.1 142.1 %reduce-scatter.16.cloned.1.call-done = f32[32,1024]{1,0:T(8,128)} async-done(((f32[1024,1024]{1,0:T(8,128)}), f32[32,1024]{1,0:T(8,128)}) %reduce-scatter.16.cloned.1.call-update) | async-done | bytes 131088 | tf_op jit(solution)/shard_map/reduce_scatter | solution.py:283
  1686.2 142.0 %reduce-scatter.18.cloned.1.call-done = f32[32,1024]{1,0:T(8,128)} async-done(((f32[1024,1024]{1,0:T(8,128)}), f32[32,1024]{1,0:T(8,128)}) %reduce-scatter.18.cloned.1.call-update) | async-done | bytes 131088 | tf_op jit(solution)/shard_map/reduce_scatter | solution.py:284
  1828.2 358.0 %reduce-scatter.22.cloned.1.call-done = f32[32,4096]{1,0:T(8,128)} async-done(((f32[1024,4096]{1,0:T(8,128)}), f32[32,4096]{1,0:T(8,128)}) %reduce-scatter.22.cloned.1.call-update) | async-done | bytes 524304 | tf_op jit(solution)/shard_map/reduce_scatter | solution.py:288
  2186.2 361.8 %reduce-scatter.24.cloned.1.call-done = f32[32,4096]{1,0:T(8,128)} async-done(((f32[1024,4096]{1,0:T(8,128)}), f32[32,4096]{1,0:T(8,128)}) %reduce-scatter.24.cloned.1.call-update) | async-done | bytes 524304 | tf_op jit(solution)/shard_map/reduce_scatter | solution.py:289
  2548.1 361.8 %reduce-scatter.26.cloned.1.call-done = f32[128,1024]{1,0:T(8,128)} async-done(((f32[4096,1024]{1,0:T(8,128)}), f32[128,1024]{1,0:T(8,128)}) %reduce-scatter.26.cloned.1.call-update) | async-done | bytes 524304 | tf_op jit(solution)/shard_map/reduce_scatter | solution.py:290
  (315 shorter events, 694.8 us)
Async XLA Ops:
  7.2 63.0 %all-gather.10.cloned.1.call-start = ((), (), s32[]{:S(2)}) async-start(), calls=%async_computation.9 | async-start | bytes 2162688 | tf_op jit(solution)/shard_map/all_gather | solution.py:99
  7.9 120.4 %all-gather.16.cloned.1.call-start = ((), (), s32[]{:S(2)}) async-start(), calls=%async_computation.12 | async-start | bytes 2162688 | tf_op jit(solution)/shard_map/all_gather | solution.py:98
  8.7 177.8 %all-gather.14.cloned.1.call-start = ((), (), s32[]{:S(2)}) async-start(), calls=%async_computation.11 | async-start | bytes 2162688 | tf_op jit(solution)/shard_map/all_gather | solution.py:97
  9.4 256.3 %all-gather.26.cloned.1.call-start = ((), (), s32[]{:S(2)}) async-start(), calls=%async_computation.17 | async-start | bytes 8650752 | tf_op jit(solution)/shard_map/all_gather | solution.py:105
  10.0 344.2 %all-gather.12.cloned.1.call-start = ((), (), s32[]{:S(2)}) async-start(), calls=%async_computation.10 | async-start | bytes 10485760 | tf_op jit(solution)/shard_map/all_gather | solution.py:156
  55.6 130.9 %copy-start.27 = (f32[1024]{0:T(1024)}, f32[1024]{0:T(1024)S(1)}, u32[]{:S(2)}) copy-start(f32[1024]{0:T(1024)S(1)} %convert_element_type.124) | copy-start | bytes 12292
  55.6 130.9 %copy-start.20 = (f32[1024]{0:T(1024)}, f32[1024]{0:T(1024)S(1)}, u32[]{:S(2)}) copy-start(f32[1024]{0:T(1024)S(1)} %convert_element_type.123) | copy-start | bytes 12292
  57.5 128.9 %copy-start.18 = (f32[2,512]{1,0:T(2,128)}, f32[2,512]{1,0:T(2,128)S(1)}, u32[]{:S(2)}) copy-start(f32[2,512]{1,0:T(2,128)S(1)} %broadcast_multiply_fusion.5) | copy-start | bytes 12292
  59.8 126.6 %copy-start.22 = (f32[2,512]{1,0:T(2,128)}, f32[2,512]{1,0:T(2,128)S(1)}, u32[]{:S(2)}) copy-start(f32[2,512]{1,0:T(2,128)S(1)} %add_rsqrt_fusion.1) | copy-start | bytes 12292
  75.5 367.9 %all-gather.18.cloned.1.call-start = ((), (), s32[]{:S(2)}) async-start(), calls=%async_computation.13 | async-start | bytes 10485760 | tf_op jit(solution)/shard_map/all_gather | solution.py:155
  76.7 114.3 %copy-start.15 = (f32[512,32]{0,1:T(8,128)}, f32[512,32]{0,1:T(8,128)S(1)}, u32[]{:S(2)}) copy-start(f32[512,32]{0,1:T(8,128)S(1)} %get-tuple-element.237) | copy-start | bytes 196612
  194.0 371.3 %all-gather.20.cloned.1.call-start = ((), (), s32[]{:S(2)}) async-start(), calls=%async_computation.14 | async-start | bytes 2162688 | tf_op jit(solution)/shard_map/all_gather | solution.py:100
  194.7 387.4 %all-gather.24.cloned.1.call-start = ((), (), s32[]{:S(2)}) async-start(), calls=%async_computation.16 | async-start | bytes 8650752 | tf_op jit(solution)/shard_map/all_gather | solution.py:104
  195.5 465.7 %all-gather.22.cloned.1.call-start = ((), (), s32[]{:S(2)}) async-start(), calls=%async_computation.15 | async-start | bytes 8650752 | tf_op jit(solution)/shard_map/all_gather | solution.py:103
  196.2 971.7 %reduce-scatter.10.cloned.1.call-start = ((), (), s32[]{:S(2)}) async-start(), calls=%async_computation.18 | async-start | bytes 10485760 | tf_op jit(solution)/shard_map/reduce_scatter | solution.py:240
  573.5 87.7 %copy-start.7 = (bf16[2,512,1024]{2,1,0:T(8,128)(2,1)}, bf16[2,512,1024]{2,1,0:T(8,128)(2,1)S(1)}, u32[]{:S(2)}) copy-start(bf16[2,512,1024]{2,1,0:T(8,128)(2,1)S(1)} %add_convert_fusion) | copy-start | bytes 6291460
  1082.8 174.9 %reduce-scatter.12.cloned.1.call-start = ((), (), s32[]{:S(2)}) async-start(), calls=%async_computation.19 | async-start | bytes 10485760 | tf_op jit(solution)/shard_map/reduce_scatter | solution.py:243
  1083.5 318.4 %reduce-scatter.20.cloned.1.call-start = ((), (), s32[]{:S(2)}) async-start(), calls=%async_computation.23 | async-start | bytes 4325376 | tf_op jit(solution)/shard_map/reduce_scatter | solution.py:285
  1091.0 453.2 %reduce-scatter.14.cloned.1.call-start = ((), (), s32[]{:S(2)}) async-start(), calls=%async_computation.20 | async-start | bytes 4325376 | tf_op jit(solution)/shard_map/reduce_scatter | solution.py:282
  1180.3 505.9 %reduce-scatter.16.cloned.1.call-start = ((), (), s32[]{:S(2)}) async-start(), calls=%async_computation.21 | async-start | bytes 4325376 | tf_op jit(solution)/shard_map/reduce_scatter | solution.py:283
  1187.9 640.4 %reduce-scatter.18.cloned.1.call-start = ((), (), s32[]{:S(2)}) async-start(), calls=%async_computation.22 | async-start | bytes 4325376 | tf_op jit(solution)/shard_map/reduce_scatter | solution.py:284
  1264.0 922.3 %reduce-scatter.22.cloned.1.call-start = ((), (), s32[]{:S(2)}) async-start(), calls=%async_computation.24 | async-start | bytes 17301504 | tf_op jit(solution)/shard_map/reduce_scatter | solution.py:288
  1280.5 1267.6 %reduce-scatter.24.cloned.1.call-start = ((), (), s32[]{:S(2)}) async-start(), calls=%async_computation.25 | async-start | bytes 17301504 | tf_op jit(solution)/shard_map/reduce_scatter | solution.py:289
  1296.8 1613.1 %reduce-scatter.26.cloned.1.call-start = ((), (), s32[]{:S(2)}) async-start(), calls=%async_computation.26 | async-start | bytes 17301504 | tf_op jit(solution)/shard_map/reduce_scatter | solution.py:290
  (34 other events, 469.2 us)
Sparse Core Ops, SparseCore 0:
  10.9 59.2 all-gather.9
  73.0 55.2 all-gather.15
  131.2 55.2 all-gather.13
  189.2 76.4 all-gather.25
  267.9 86.1 all-gather.11
  355.9 87.4 all-gather.17
  446.2 56.4 all-gather.19
  505.6 76.4 all-gather.23
  585.0 76.1 all-gather.21
  1082.9 84.9 reduce-scatter.9
  1171.2 86.3 reduce-scatter.11
  1260.4 141.4 reduce-scatter.19
  1404.8 139.3 reduce-scatter.13
  1546.9 139.3 reduce-scatter.15
  1688.9 139.2 reduce-scatter.17
  1831.0 355.2 reduce-scatter.21
  2189.0 359.0 reduce-scatter.23
  2550.8 358.9 reduce-scatter.25
where the time goes:
time: 2920 us
  waiting for transfers between devices  2050 us (70%)
  matrix products  539 us (18%)
  other arithmetic  157 us (5%)
  blocking collectives  97.9 us (3%)
  local copies, waits for them, and re-layouts  52.4 us (2%)
    reduce_scatter x1, waiting for transfers between devices, body(): lax.psum_scatter(grad_up_w, ('dp', 'seq'), scatter_dimension=0, tiled=True)  362 us
    reduce_scatter x1, waiting for transfers between devices, body(): lax.psum_scatter(grad_down, ('dp', 'seq'), scatter_dimension=0, tiled=True)  362 us
    reduce_scatter x1, waiting for transfers between devices, body(): lax.psum_scatter(grad_gate_w, ('dp', 'seq'), scatter_dimension=0, tiled=T...  358 us
    reduce_scatter x1, waiting for transfers between devices, body(): lax.psum_scatter(grad_query_w, ('dp', 'seq'), scatter_dimension=0, tiled=...  142 us
    reduce_scatter x1, waiting for transfers between devices, body(): lax.psum_scatter(grad_key_w, ('dp', 'seq'), scatter_dimension=0, tiled=True)  142 us
    reduce_scatter x1, waiting for transfers between devices, body(): lax.psum_scatter(grad_value_w, ('dp', 'seq'), scatter_dimension=0, tiled=...  142 us
    convert_element_type x8, other arithmetic, attend_back(): grad_scores = (probs * (grad_probs - inner)).astype(jnp.bfloat16)  85.2 us
    unnamed x2, blocking collectives  82 us
  transfers between devices with their start and end apart: 18, of which 17 were waited for; matrix products, arithmetic and copies ran while one was open for 11% of the time, Pallas kernels for 0%

commit v1 on v0

v1 whole, which is shorter than its diff:
```python
import functools

import jax
import jax.numpy as jnp
from jax import lax
from jax.experimental import pallas as pl
from jax.experimental.pallas import tpu as pltpu
from jax.sharding import PartitionSpec as P

HEAD_DIM = 64
SPECIES = 8
EPS = 1e-05
LOG2E = 1.4426950408889634
BOTH = ("dp", "seq")
F32 = jnp.float32
BF16 = jnp.bfloat16
QUERIES = 512
KEYS = 512
VMEM = 60 * 2**20

NN = (((1,), (0,)), ((), ()))
NT = (((1,), (1,)), ((), ()))


def dot(a, b, dims=NN):
    return lax.dot_general(a, b, dims, preferred_element_type=F32)


def attend_kernel(len_ref, q_ref, k_ref, v_ref, o_ref, l_ref, vt_ref):
    length = len_ref[pl.program_id(0)]
    lane = lax.broadcasted_iota(jnp.int32, (1, 128), 1)
    rows = q_ref.shape[2]

    @pl.when(pl.program_id(2) == 0)
    def _():
        vt_ref[...] = v_ref[0, 0].T

    q2 = q_ref[0, 0] * BF16(0.125)

    def run(n):
        k2 = k_ref[0, 0, :n]
        outs = []
        for h in range(2):
            qh = jnp.where((lane // 64) == h, q2, BF16(0))
            s = dot(k2, qh, NT)
            row = lax.broadcasted_iota(jnp.int32, (KEYS, rows), 0) + (n - KEYS)
            last = jnp.where(row < length, s[n - KEYS :], -1e30)
            s = jnp.concatenate([s[: n - KEYS], last], 0) if n > KEYS else last
            m = jnp.max(s, axis=0, keepdims=True)
            p = jnp.exp2((s - m) * LOG2E)
            total = jnp.sum(p, axis=0, keepdims=True)
            o = dot(vt_ref[h * 64 : h * 64 + 64, :n], p.astype(BF16))
            outs.append(o / total)
            l_ref[0, 0, h : h + 1] = m + jnp.log(total)
        o_ref[0] = jnp.concatenate(outs, 0).T.astype(BF16)

    blocks = (length + KEYS - 1) // KEYS
    for i in range(k_ref.shape[2] // KEYS):
        pl.when(blocks == i + 1)(functools.partial(run, KEYS * (i + 1)))


def attend(lengths, qkv):
    three, wins, span, width = qkv.shape
    pairs = width // 128
    rows = min(QUERIES, span)

    def whole(which):
        return pl.BlockSpec((1, 1, span, 128), lambda w, h, i, _: (which, w, 0, h))

    return pl.pallas_call(
        attend_kernel,
        grid_spec=pltpu.PrefetchScalarGridSpec(
            num_scalar_prefetch=1,
            grid=(wins, pairs, span // rows),
            in_specs=[
                pl.BlockSpec((1, 1, rows, 128), lambda w, h, i, _: (0, w, i, h)),
                whole(1),
                whole(2),
            ],
            out_specs=[
                pl.BlockSpec((1, rows, 128), lambda w, h, i, _: (w, i, h)),
                pl.BlockSpec((1, 1, 2, rows), lambda w, h, i, _: (w, h, 0, i)),
            ],
            scratch_shapes=[pltpu.VMEM((128, span), BF16)],
        ),
        out_shape=[
            jax.ShapeDtypeStruct((wins, span, width), BF16),
            jax.ShapeDtypeStruct((wins, pairs, 2, span), F32),
        ],
        compiler_params=pltpu.CompilerParams(vmem_limit_bytes=VMEM),
        cost_estimate=pl.CostEstimate(
            flops=4 * wins * span * span * width * 4,
            bytes_accessed=8 * wins * span * width,
            transcendentals=wins * span * span * width // 64,
        ),
        name="attend",
    )(lengths, qkv, qkv, qkv)


def attend_back_kernel(
    len_ref, q_ref, k_ref, v_ref, o_ref, g_ref, l_ref, d_ref, kt_ref, dq_ref, dk_ref, dv_ref
):
    step = pl.program_id(2)
    length = len_ref[pl.program_id(0)]
    rows = q_ref.shape[2]
    lane = lax.broadcasted_iota(jnp.int32, (1, 128), 1)

    @pl.when(step == 0)
    def _():
        kt_ref[...] = (k_ref[0, 0] * BF16(0.125)).T
        dk_ref[...] = jnp.zeros_like(dk_ref)
        dv_ref[...] = jnp.zeros_like(dv_ref)

    here = pl.ds(pl.multiple_of(step * rows, rows), rows)

    @pl.when(step * rows >= length)
    def _():
        dq_ref[here] = jnp.zeros((rows, 128), BF16)

    @pl.when(step * rows < length)
    def _():
        q2 = q_ref[0, 0] * BF16(0.125)
        g2 = g_ref[0]
        products = (g2.astype(F32) * o_ref[0].astype(F32)).T
        qs, gs, ls, ds = [], [], [], []
        for h in range(2):
            mine = (lane // 64) == h
            qs.append(jnp.where(mine, q2, BF16(0)))
            gs.append(jnp.where(mine, g2, BF16(0)))
            ls.append(l_ref[0, 0, h : h + 1] * LOG2E)
            ds.append(jnp.sum(products[h * 64 : h * 64 + 64], axis=0, keepdims=True))
        qc = jnp.concatenate(qs, 0)
        gc = jnp.concatenate(gs, 0)
        lc = jnp.concatenate(ls, 1)
        dc = jnp.concatenate(ds, 1)

        def chunk(c, acc, masked):
            base = c * KEYS
            sl = pl.ds(pl.multiple_of(base, KEYS), KEYS)
            k2 = k_ref[0, 0, sl]
            v2 = v_ref[0, 0, sl]
            p = jnp.exp2(dot(k2, qc, NT) * LOG2E - lc)
            if masked:
                row = lax.broadcasted_iota(jnp.int32, (KEYS, 1), 0) + base
                p = jnp.where(row < length, p, 0.0)
            gp = dot(v2, gc, NT)
            gs_low = (p * (gp - dc)).astype(BF16)
            dv_ref[sl] += dot(p.astype(BF16), gc)
            dk_ref[sl] += dot(gs_low, qc)
            return tuple(
                acc[h] + dot(kt_ref[h * 64 : h * 64 + 64, sl], gs_low[:, h * rows : (h + 1) * rows])
                for h in range(2)
            )

        acc = (jnp.zeros((64, rows), F32),) * 2
        full = length // KEYS
        acc = lax.fori_loop(0, full, lambda c, a: chunk(c, a, False), acc)
        acc = lax.cond(full * KEYS < length, lambda a: chunk(full, a, True), lambda a: a, acc)
        dq_ref[here] = jnp.concatenate(acc, 0).T.astype(BF16)

    @pl.when(step == pl.num_programs(2) - 1)
    def _():
        d_ref[0, 0] = dq_ref[...]
        d_ref[1, 0] = dk_ref[...].astype(BF16)
        d_ref[2, 0] = dv_ref[...].astype(BF16)


def attend_back(lengths, qkv, mixed, grad, lse):
    three, wins, span, width = qkv.shape
    pairs = width // 128
    rows = min(QUERIES, span)
    block = pl.BlockSpec((1, rows, 128), lambda w, h, i, _: (w, i, h))

    def whole(which):
        return pl.BlockSpec((1, 1, span, 128), lambda w, h, i, _: (which, w, 0, h))

    return pl.pallas_call(
        attend_back_kernel,
        grid_spec=pltpu.PrefetchScalarGridSpec(
            num_scalar_prefetch=1,
            grid=(wins, pairs, span // rows),
            in_specs=[
                pl.BlockSpec((1, 1, rows, 128), lambda w, h, i, _: (0, w, i, h)),
                whole(1),
                whole(2),
                block,
                block,
                pl.BlockSpec((1, 1, 2, rows), lambda w, h, i, _: (w, h, 0, i)),
            ],
            out_specs=pl.BlockSpec((3, 1, span, 128), lambda w, h, i, _: (0, w, 0, h)),
            scratch_shapes=[
                pltpu.VMEM((128, span), BF16),
                pltpu.VMEM((span, 128), BF16),
                pltpu.VMEM((span, 128), F32),
                pltpu.VMEM((span, 128), F32),
            ],
        ),
        out_shape=jax.ShapeDtypeStruct((3, wins, span, width), BF16),
        compiler_params=pltpu.CompilerParams(vmem_limit_bytes=VMEM),
        cost_estimate=pl.CostEstimate(
            flops=10 * wins * span * span * width * 3,
            bytes_accessed=16 * wins * span * width,
            transcendentals=wins * span * span * width // 64,
        ),
        name="attend_back",
    )(lengths, qkv, qkv, qkv, mixed, grad, lse)


def normalise(value):
    centered = value - jnp.mean(value, axis=-1, keepdims=True)
    inverse = lax.rsqrt(jnp.mean(centered * centered, axis=-1, keepdims=True) + EPS)
    return centered * inverse, inverse


def norm_back(grad, normal, inverse, gain):
    scaled = grad * gain
    centered = scaled - jnp.mean(scaled, axis=-1, keepdims=True)
    return inverse * (centered - normal * jnp.mean(scaled * normal, axis=-1, keepdims=True))


def rotary(value, cosine, sine):
    half = HEAD_DIM // 2
    rows, width = value.shape[-2:]
    split = value.reshape(value.shape[:-1] + (width // HEAD_DIM, HEAD_DIM))
    first, second = split[..., :half], split[..., half:]
    cos_wide, sin_wide = cosine[:, None, :], sine[:, None, :]
    turned = jnp.concatenate(
        [first * cos_wide - second * sin_wide, second * cos_wide + first * sin_wide], axis=-1
    )
    return turned.reshape(value.shape)


def angles_of(positions):
    half = HEAD_DIM // 2
    freq = 10000.0 ** (-2.0 * jnp.arange(half, dtype=F32) / HEAD_DIM)
    angle = positions.astype(F32)[:, None] * freq[None, :]
    return (jnp.cos(angle), jnp.sin(angle))


class Links:
    def __init__(self, mesh):
        self.dp, self.seq = mesh.shape["dp"], mesh.shape["seq"]
        self.count = self.dp * self.seq
        self.bits = self.count.bit_length() - 1
        self.core = self.seq.bit_length() - 1
        self.seq_bits = list(range(self.core))
        self.dp_bits = list(range(self.core, self.bits))
        self.chips = self.seq_bits + self.dp_bits[1:]

    def me(self):
        return lax.axis_index("dp") * self.seq + lax.axis_index("seq")

    def swap(self, value, bit):
        pairs = [(i, i ^ (1 << bit)) for i in range(self.count)]
        return lax.ppermute(value, BOTH, pairs)

    def orders(self, turn):
        turn = turn % len(self.chips)
        return [self.core] + self.chips[turn:] + self.chips[:turn]

    def scatter_sum(self, value, order, wire):
        blocks = value.reshape((2,) * self.bits + (value.shape[0] // self.count,) + value.shape[1:])
        axes = list(range(self.bits - 1, -1, -1))
        me = self.me()
        for bit in order:
            at = axes.index(bit)
            own = (me >> bit) & 1
            away = lax.dynamic_index_in_dim(blocks, 1 - own, at, keepdims=False).astype(wire)
            kept = lax.dynamic_index_in_dim(blocks, own, at, keepdims=False)
            blocks = kept.astype(F32) + self.swap(away, bit).astype(F32)
            axes.pop(at)
        return blocks

    def window_sum(self, value):
        for bit in self.dp_bits:
            value = value + self.swap(value, bit)
        return value


def to_heads(value):
    return lax.all_to_all(value, "seq", split_axis=3, concat_axis=2, tiled=True)


def to_positions(value):
    return lax.all_to_all(value, "seq", split_axis=2, concat_axis=3, tiled=True)


def body(
    links,
    tokens,
    cotangent,
    lengths,
    species,
    ln1_gain,
    ln1_bias,
    w_query,
    w_key,
    w_value,
    w_out,
    ln2_gain,
    ln2_bias,
    w_gate,
    w_up,
    w_down,
):
    wins, rows, width = tokens.shape
    flat = wins * rows
    ff = w_gate.shape[1]
    species_ids = jnp.arange(SPECIES)
    onehot = (species[:, None] == species_ids[None, :]).astype(F32)
    counts = links.window_sum(jnp.sum(onehot * lengths[:, None].astype(F32), axis=0))
    window_weight = SPECIES * jnp.sum(onehot * counts[None, :], axis=1) / jnp.sum(counts)

    def gathered(value):
        return lax.all_gather(value, BOTH, axis=0, tiled=True)

    small = jnp.stack([ln1_gain, ln1_bias, ln2_gain, ln2_bias], axis=1)
    small = jnp.pad(small, ((0, 0), (0, 124)))
    first = gathered(jnp.concatenate([w_query, w_key, w_value, small], axis=1))
    second = gathered(jnp.concatenate([w_out, w_gate, w_up], axis=1))
    down_w = gathered(w_down)
    qkv_w = first[:, : 3 * width]
    gain_one, bias_one, gain_two, bias_two = (
        first[:, 3 * width : 3 * width + 4].T.astype(F32).reshape(4, 1, width)
    )
    out_w = second[:, :width]
    both_w = second[:, width:]

    positions = lax.axis_index("seq") * rows + jnp.arange(rows)
    cosine, sine = angles_of(positions)
    row_scale = jnp.where(positions[None, :] < lengths[:, None], window_weight[:, None], 0.0)
    row_scale = row_scale.reshape(flat, 1)
    inputs = tokens.astype(F32).reshape(flat, width)
    normal_one, inverse_one = normalise(inputs)
    normed_low = (normal_one * gain_one + bias_one).astype(BF16)

    qkv = dot(normed_low, qkv_w).reshape(wins, rows, 3, width)
    query = rotary(qkv[:, :, 0], cosine, sine).astype(BF16)
    key = rotary(qkv[:, :, 1], cosine, sine).astype(BF16)
    value = qkv[:, :, 2].astype(BF16)

    qkv_heads = to_heads(jnp.stack([query, key, value]))
    mixed_heads, lse = attend(lengths, qkv_heads)
    mixed = to_positions(mixed_heads[None])[0].reshape(flat, width)
    middle = inputs + dot(mixed, out_w)
    normal_two, inverse_two = normalise(middle)
    normed_two_low = (normal_two * gain_two + bias_two).astype(BF16)
    both = dot(normed_two_low, both_w)
    gate, upper = both[:, :ff], both[:, ff:]
    sigma = jax.nn.sigmoid(gate)
    hidden = (gate * sigma * upper).astype(BF16)
    output = middle + dot(hidden, down_w)

    grad_out = cotangent.astype(F32).reshape(flat, width) * row_scale
    grad_low = grad_out.astype(BF16)
    grad_down = dot(hidden.T, grad_low).astype(BF16)
    sum_down = links.scatter_sum(grad_down, links.orders(0), BF16)
    grad_hidden = dot(grad_low, down_w, NT)
    grad_up = (grad_hidden * gate * sigma).astype(BF16)
    grad_gate = (grad_hidden * upper * sigma * (1.0 + gate * (1.0 - sigma))).astype(BF16)
    normed_two_t = normed_two_low.T
    sum_gate = links.scatter_sum(dot(normed_two_t, grad_gate).astype(BF16), links.orders(1), BF16)
    sum_up = links.scatter_sum(dot(normed_two_t, grad_up).astype(BF16), links.orders(2), BF16)
    grad_normed_two = dot(grad_gate, both_w[:, :ff], NT) + dot(grad_up, both_w[:, ff:], NT)
    grad_gain_two = jnp.sum(grad_normed_two * normal_two, axis=0)
    grad_bias_two = jnp.sum(grad_normed_two, axis=0)
    grad_middle = grad_out + norm_back(grad_normed_two, normal_two, inverse_two, gain_two)
    grad_middle_low = grad_middle.astype(BF16)
    grad_mixed = dot(grad_middle_low, out_w, NT).astype(BF16)
    grad_heads = to_heads(grad_mixed.reshape(1, wins, rows, width))[0]
    sum_out = links.scatter_sum(
        dot(mixed.T, grad_middle_low).astype(BF16), links.orders(0), BF16
    )

    grad_qkv = to_positions(attend_back(lengths, qkv_heads, mixed_heads, grad_heads, lse))
    grad_q_low = rotary(grad_qkv[0].astype(F32), cosine, -sine).astype(BF16).reshape(flat, width)
    grad_k_low = rotary(grad_qkv[1].astype(F32), cosine, -sine).astype(BF16).reshape(flat, width)
    grad_v_low = grad_qkv[2].reshape(flat, width)
    low = jnp.concatenate([grad_q_low, grad_k_low, grad_v_low], axis=1)
    sum_qkv = links.scatter_sum(dot(normed_low.T, low).astype(BF16), links.orders(1), BF16)
    grad_normed = dot(low, qkv_w, NT)
    grad_gain_one = jnp.sum(grad_normed * normal_one, axis=0)
    grad_bias_one = jnp.sum(grad_normed, axis=0)
    grad_inputs = grad_middle + norm_back(grad_normed, normal_one, inverse_one, gain_one)
    vectors = jnp.stack([grad_gain_one, grad_bias_one, grad_gain_two, grad_bias_two])
    vectors = vectors.reshape(4, links.count, width // links.count).transpose(1, 0, 2)
    vectors = links.scatter_sum(vectors.reshape(links.count * 4, -1), links.orders(0), F32)
    return (
        output.reshape(wins, rows, width),
        grad_inputs.reshape(wins, rows, width),
        vectors[0],
        vectors[1],
        sum_qkv[:, :width],
        sum_qkv[:, width : 2 * width],
        sum_qkv[:, 2 * width :],
        sum_out,
        vectors[2],
        vectors[3],
        sum_gate,
        sum_up,
        sum_down,
    )


def solution(mesh):
    token = P("dp", "seq", None)
    vector = P(BOTH)
    matrix = P(BOTH, None)
    return jax.shard_map(
        functools.partial(body, Links(mesh)),
        mesh=mesh,
        in_specs=(
            (token, token, P("dp"), P("dp"), vector, vector)
            + (matrix,) * 4
            + (vector, vector)
            + (matrix,) * 3
        ),
        out_specs=(
            (token, token, vector, vector) + (matrix,) * 4 + (vector, vector) + (matrix,) * 3
        ),
        check_vma=False,
    )
```

time: 2920 us -> 976 us (0.33)
  waiting for transfers between devices: 2050 us -> 293 us
  matrix products: 539 us -> 183 us
  local copies, waits for them, and re-layouts: 52.4 us -> 189 us
  Pallas kernels: 0 us -> 108 us
  starting transfers between devices: 1.68 us -> 107 us
  blocking collectives: 97.9 us -> 0 us
  other arithmetic: 157 us -> 78.4 us
    reduce_scatter x9 -> x0, waiting for transfers between devices: 1670 us -> none  [the longest x1 362 us: body(): lax.psum_scatter(grad_up_w, ('dp', 'seq'), scatter_dimension=0, tiled=True)]
    dot_general x77 -> x14, matrix products: 539 us -> 183 us  [dot(): return lax.dot_general(a, b, dims, preferred_element_type=F32)]
    all_gather x9 -> x3, waiting for transfers between devices: 380 us -> 69.4 us  [gathered(): return lax.all_gather(value, BOTH, axis=0, tiled=True)]
    ppermute x0 -> x33, waiting for transfers between devices: none -> 139 us  [swap(): return lax.ppermute(value, BOTH, pairs)]
    pallas_call x0 -> x2, Pallas kernels: none -> 108 us  [the longest x1 62.8 us: attend_back(): pl.pallas_call(attend_back_kernel, grid_spec=pltpu.PrefetchScalarGridSpec...]
    ppermute x0 -> x33, starting transfers between devices: none -> 87.1 us  [swap(): return lax.ppermute(value, BOTH, pairs)]
    all_to_all x0 -> x4, waiting for transfers between devices: none -> 83.9 us  [the longest x2 83.9 us: to_heads(): return lax.all_to_all(value, 'seq', split_axis=3, concat_axis=2, tiled=True)]
    unnamed x2 -> x0, blocking collectives: 82 us -> none
  transfers between devices with their start and end apart: 18 -> 40, of which waited for: 17 -> 19; matrix products, arithmetic and copies ran while one was open for 11% -> 40% of each run, Pallas kernels for 0% -> 11%
where the time goes in v1:
time: 976 us; the launch traced here: 974 us
  waiting for transfers between devices  293 us (30%)
  local copies, waits for them, and re-layouts  189 us (19%)
  matrix products  183 us (19%)
  Pallas kernels  108 us (11%)
  starting transfers between devices  107 us (11%)
  other arithmetic  78.4 us (8%)
  between operations  15.3 us (2%)
    dot_general x14, matrix products, dot(): return lax.dot_general(a, b, dims, preferred_element_type=F32)  183 us
    ppermute x33, waiting for transfers between devices, swap(): return lax.ppermute(value, BOTH, pairs)  139 us
    ppermute x33, starting transfers between devices, swap(): return lax.ppermute(value, BOTH, pairs)  87.1 us
    all_to_all x2, waiting for transfers between devices, to_heads(): return lax.all_to_all(value, 'seq', split_axis=3, concat_axis=2, tiled=True)  83.9 us
    all_gather x3, waiting for transfers between devices, gathered(): return lax.all_gather(value, BOTH, axis=0, tiled=True)  69.4 us
    pallas_call x1, Pallas kernels, attend_back(): pl.pallas_call(attend_back_kernel, grid_spec=pltpu.PrefetchScalarGridSpec...  62.8 us
    pallas_call x1, Pallas kernels, attend(): pl.pallas_call(attend_kernel, grid_spec=pltpu.PrefetchScalarGridSpec(num_...  44.7 us
    add x30, other arithmetic, scatter_sum(): blocks = kept.astype(F32) + self.swap(away, bit).astype(F32)  33.9 us
  transfers between devices with their start and end apart: 40, of which 19 were waited for; matrix products, arithmetic and copies ran while one was open for 40% of the time, Pallas kernels for 11%

profile of v1, /device:TPU:0, one launch (start us, length us, event | category | flops | bytes accessed | tf_op | source)
XLA Modules:
  0.0 973.7 jit_solution(11224525506451739733)
XLA Ops:
  15.4 69.4 %all-gather.4.cloned.1.call-done = bf16[1024,3200]{1,0:T(8,128)(2,1)} async-done(((bf16[32,3200]{1,0:T(8,128)(2,1)}), bf16[1024,3200]{1,0:T(8,128)(2,1)}) %all-gather.4.cloned.1.call-update) | async-done | bytes 6553616 | tf_op jit(solution)/shard_map/all_gather | solution.py:315
  153.4 16.4 %copy.187 = bf16[3,2,512,1024]{2,1,0,3:T(2,128)(2,1)} copy(bf16[3,2,512,1024]{3,2,1,0:T(8,128)(2,1)} %pad_maximum_fusion) | data formatting | bytes 12582912 | tf_op jit(solution)/shard_map/stack | solution.py:342
  175.8 79.2 %all-to-all-done = bf16[3,2,512,1024]{2,1,0,3:T(2,128)(2,1)} async-done(((bf16[3,2,512,1024]{2,1,0,3:T(2,128)(2,1)}), bf16[3,2,512,1024]{2,1,0,3:T(2,128)(2,1)}, u32[]{:S(2)}, u32[]{:S(2)}) %all-to-all-start) | async-done | bytes 6291488 | tf_op jit(solution)/shard_map/all_to_all | solution.py:281
  255.1 16.0 %copy.188 = bf16[3,2,512,4,256]{4,2,3,1,0:T(8,128)(2,1)} copy(bf16[3,2,512,4,256]{2,1,0,4,3:T(2,128)(2,1)} %bitcast.16) | data formatting | bytes 12582912 | tf_op jit(solution)/shard_map/all_to_all | solution.py:281
  271.1 44.7 %attend.1 = (bf16[2,2048,256]{2,1,0:T(8,128)(2,1)}, f32[2,2,2,2048]{3,2,1,0:T(2,128)}) custom-call(s32[2]{0:T(128)} %len_ref.3, bf16[3,2,2048,256]{3,2,1,0:T(8,128)(2,1)} %bitcast.298, bf16[3,2,2048,256]{3,2,1,0:T(8,128)(2,1)} %bitcast.299, bf16[3,2,2048,256]{3,2,1,0:T(8,128)(2,1)} %bitcast.300), custom_call_target="tpu_custom_call" | custom-call | flops 34359738368 | bytes 8388608 | tf_op jit(solution)/shard_map/attend/pallas_call | solution.py:70
  326.4 12.1 %collective-permute-start = (f32[8]{0:T(128)S(1)}, f32[8]{0:T(128)S(1)}, u32[]{:S(2)}, u32[]{:S(2)}) collective-permute-start(f32[8]{0:T(128)S(1)} %select_reduce_fusion.1), channel_id=1, source_target_pairs={{0,4},{1,5},{2,6},{3,7},{4,0},{5,1},{6,2},{7,3},{8,12},{9,13},{10,... | collective-permute-start | bytes 104 | tf_op jit(solution)/shard_map/ppermute | solution.py:255
  371.0 26.0 %fusion = f32[1024,8192]{1,0:T(8,128)} fusion(bf16[1024,9216]{1,0:T(8,128)(2,1)} %all-gather.6.cloned.1.call-done, f32[1024,1024]{1,0:T(8,128)S(1)} %get-tuple-element.79, f32[1024]{0:T(1024)S(1)} %get-tuple-element.26, f32[1024]{0:T(1024)S(1)} %get-tuple-element.25, f32[1024]{0:T(1024)S(1)} %add_rsqrt_fusion, f32[1024]{0:T(1024)S(1)} %broadcast_multiply_fusion.4), kind=kOutput, calls=%fused_computation | convolution fusion | flops 17185112064 | bytes 54542336 | tf_op jit(solution)/shard_map/dot_general | solution.py:26
  397.0 28.2 %multiply_convert_fusion.1 = (bf16[1024,4096]{1,0:T(8,128)(2,1)}, bf16[1024,4096]{1,0:T(8,128)(2,1)}, bf16[1024,4096]{1,0:T(8,128)(2,1)}) fusion(f32[1024,8192]{1,0:T(8,128)} %fusion, bf16[1024,1024]{1,0:T(8,128)(2,1)S(1)} %copy-done.21, bf16[4096,1024]{1,0:T(8,128)(2,1)} %all-gather.8.cloned.1.call-done), kind=kOutput, calls=%fused_computation.3 | convolution fusion | flops 8657043456 | bytes 69206016 | tf_op jit(solution)/shard_map/dot_general | solution.py:26
  425.1 12.9 %convolution_convert_fusion = bf16[4096,1024]{1,0:T(8,128)(2,1)S(1)} fusion(bf16[1024,4096]{1,0:T(8,128)(2,1)} %get-tuple-element.33, bf16[1024,1024]{1,0:T(8,128)(2,1)} %fusion.9), kind=kOutput, calls=%fused_computation.13 | convolution fusion | flops 8594128896 | bytes 18874368 | tf_op jit(solution)/shard_map/dot_general | solution.py:26
  445.1 15.5 %convolution_convert_fusion.1 = bf16[1024,4096]{1,0:T(8,128)(2,1)} fusion(bf16[1024,4096]{1,0:T(8,128)(2,1)} %get-tuple-element.32, f32[1024,1024]{1,0:T(8,128)S(1)} %copy-done.5, f32[1024]{0:T(1024)S(1)} %get-tuple-element.26, f32[1024]{0:T(1024)S(1)} %get-tuple-element.25, f32[1024]{0:T(1024)S(1)} %add_rsqrt_fusion, f32[1024]{0:T(1024)S(1)} %broadcast_multiply_fusion.4), kind=kOutput, calls=%fused_computation.14 | convolution fusion | flops 8599371776 | bytes 20987904 | tf_op jit(solution)/shard_map/dot_general | solution.py:26
  460.6 12.2 %convolution_convert_fusion.2 = bf16[1024,4096]{1,0:T(8,128)(2,1)} fusion(bf16[1024,4096]{1,0:T(8,128)(2,1)S(1)} %bitcast.329, f32[1024,1024]{1,0:T(8,128)S(1)} %copy-done.5, f32[1024]{0:T(1024)S(1)} %get-tuple-element.26, f32[1024]{0:T(1024)S(1)} %get-tuple-element.25, f32[1024]{0:T(1024)S(1)} %add_rsqrt_fusion, f32[1024]{0:T(1024)S(1)} %broadcast_multiply_fusion.4), kind=kOutput, calls=%fused_computation.15 | convolution fusion | flops 8599371776 | bytes 20987904 | tf_op jit(solution)/shard_map/dot_general | solution.py:26
  472.8 12.8 %fusion.2 = f32[1024,1024]{1,0:T(8,128)S(1)} fusion(bf16[1024,4096]{1,0:T(8,128)(2,1)} %get-tuple-element.32, bf16[1024,9216]{1,0:T(8,128)(2,1)} %all-gather.6.cloned.1.call-done), kind=kOutput, calls=%fused_computation.6 | convolution fusion | flops 8589934592 | bytes 20971520 | tf_op jit(solution)/shard_map/dot_general | solution.py:26
  485.7 16.3 %multiply_reduce_fusion = (f32[1024]{0:T(1024)S(1)}, f32[1024]{0:T(1024)S(1)}, f32[1024]{0:T(1024)S(1)}, f32[1024]{0:T(1024)S(1)}, f32[1024,1024]{1,0:T(8,128)}) fusion(f32[1024,1024]{1,0:T(8,128)S(1)} %copy-done.5, f32[1024]{0:T(1024)S(1)} %add_rsqrt_fusion, f32[1024]{0:T(1024)S(1)} %broadcast_multiply_fusion.4, f32[1024]{0:T(1024)S(1)} %get-tuple-element.25, ...), kind=kOutput, calls=%fused_computation.60 | convolution fusion | flops 8600416256 | bytes 29388800 | tf_op jit(solution)/shard_map/dot_general | solution.py:26
  546.5 15.6 %convolution_add_fusion = f32[1024,1024]{1,0:T(8,128)} fusion(f32[1024,1024]{1,0:T(8,128)} %copy-done.4, bf16[1024,4096]{1,0:T(8,128)(2,1)} %get-tuple-element.33, bf16[4096,1024]{1,0:T(8,128)(2,1)} %all-gather.8.cloned.1.call-done), kind=kOutput, calls=%fused_computation.103 | convolution fusion | flops 8590983168 | bytes 25165824 | tf_op jit(solution)/shard_map/dot_general | solution.py:26
  576.1 62.8 %attend_back.1 = bf16[3,2,2048,256]{3,2,1,0:T(8,128)(2,1)} custom-call(s32[2]{0:T(128)} %len_ref.3, bf16[3,2,2048,256]{3,2,1,0:T(8,128)(2,1)} %bitcast.301, bf16[3,2,2048,256]{3,2,1,0:T(8,128)(2,1)} %bitcast.302, bf16[3,2,2048,256]{3,2,1,0:T(8,128)(2,1)} %bitcast.303, bf16[2,2048,256]{2,1,0:T(8,128)(2,1)} %get-tuple-element.15.o_ref, ...), custom_call_target="tpu_custom_call" | custom-call | flops 64424509440 | bytes 16777216 | tf_op jit(solution)/shard_map/attend_back/pallas_call | solution.py:177
  638.9 12.7 %copy.194 = bf16[3,2,2048,256]{3,1,0,2:T(2,128)(2,1)} copy(bf16[3,2,2048,256]{3,2,1,0:T(8,128)(2,1)} %attend_back.1) | data formatting | bytes 12582912 | tf_op jit(solution)/shard_map/attend_back/pallas_call | solution.py:177
  671.7 23.5 %collective-permute-start.24 = (bf16[2,2,2,32,4096]{4,3,1,2,0:T(8,128)(2,1)}, bf16[2,2,2,32,4096]{4,3,1,2,0:T(8,128)(2,1)}, u32[]{:S(2)}, u32[]{:S(2)}) collective-permute-start(bf16[2,2,2,32,4096]{4,3,1,2,0:T(8,128)(2,1)} %fusion.32), channel_id=1, source_target_pairs={{0,8},{1,9},{2,10},{3,11},{4,12},{5,13},{6,14},{7,15},{8,0},{9,1},... | collective-permute-start | bytes 6291464 | tf_op jit(solution)/shard_map/ppermute | solution.py:255
  706.8 47.4 %collective-permute-done.29 = bf16[2,2,2,128,1024]{4,3,0,1,2:T(8,128)(2,1)} collective-permute-done((bf16[2,2,2,128,1024]{4,3,0,1,2:T(8,128)(2,1)}, bf16[2,2,2,128,1024]{4,3,0,1,2:T(8,128)(2,1)}, u32[]{:S(2)}, u32[]{:S(2)}) %collective-permute-start.29) | collective-permute-done | bytes 2097184 | tf_op jit(solution)/shard_map/ppermute | solution.py:255
  774.0 17.2 %collective-permute-start.20 = (bf16[2,2,32,4096]{3,2,1,0:T(8,128)(2,1)}, bf16[2,2,32,4096]{3,2,1,0:T(8,128)(2,1)}, u32[]{:S(2)}, u32[]{:S(2)}) collective-permute-start(bf16[2,2,32,4096]{3,2,1,0:T(8,128)(2,1)} %fusion.45), channel_id=1, source_target_pairs={{0,8},{1,9},{2,10},{3,11},{4,12},{5,13},{6,14},{7,15},{8,0},{9,1},... | collective-permute-start | bytes 3145736 | tf_op jit(solution)/shard_map/ppermute | solution.py:255
  833.3 14.4 %fusion.25 = (f32[1024]{0:T(1024)S(1)}, f32[1024]{0:T(1024)S(1)}, f32[1024]{0:T(1024)S(1)}, f32[1024]{0:T(1024)S(1)}, bf16[1024,1024]{1,0:T(8,128)(2,1)}, /*index=5*/f32[1024,1024]{1,0:T(8,128)}) fusion(bf16[2,512,1024]{2,1,0:T(8,128)(2,1)S(1)} %copy-done.1, f32[1024]{0:T(1024)S(1)} %bitcast.321, f32[1024]{0:T(1024)S(1)} %bitcast.319, ...), kind=kOutput, calls=%fused_computation.51 | convolution fusion | flops 6456078336 | bytes 21004288 | tf_op jit(solution)/shard_map/dot_general | solution.py:26
  885.2 11.7 %collective-permute-done.31 = bf16[2,128,1024]{2,1,0:T(8,128)(2,1)S(1)} collective-permute-done((bf16[2,128,1024]{2,1,0:T(8,128)(2,1)S(1)}, bf16[2,128,1024]{2,1,0:T(8,128)(2,1)S(1)}, u32[]{:S(2)}, u32[]{:S(2)}) %collective-permute-start.31) | collective-permute-done | bytes 524320 | tf_op jit(solution)/shard_map/ppermute | solution.py:255
  901.0 13.0 %collective-permute-done.21 = bf16[2,32,4096]{2,1,0:T(8,128)(2,1)S(1)} collective-permute-done((bf16[2,32,4096]{2,1,0:T(8,128)(2,1)S(1)}, bf16[2,32,4096]{2,1,0:T(8,128)(2,1)S(1)}, u32[]{:S(2)}, u32[]{:S(2)}) %collective-permute-start.21) | collective-permute-done | bytes 524320 | tf_op jit(solution)/shard_map/ppermute | solution.py:255
  915.2 13.8 %collective-permute-done.9 = bf16[2,2,2,32,3072]{4,3,2,0,1:T(8,128)(2,1)S(1)} collective-permute-done((bf16[2,2,2,32,3072]{4,3,2,0,1:T(8,128)(2,1)S(1)}, bf16[2,2,2,32,3072]{4,3,2,0,1:T(8,128)(2,1)S(1)}, u32[]{:S(2)}, u32[]{:S(2)}) %collective-permute-start.9) | collective-permute-done | bytes 1572896 | tf_op jit(solution)/shard_map/ppermute | solution.py:255
  932.7 13.0 %collective-permute-done.10 = bf16[2,2,32,3072]{3,2,1,0:T(8,128)(2,1)S(1)} collective-permute-done((bf16[2,2,32,3072]{3,2,1,0:T(8,128)(2,1)S(1)}, bf16[2,2,32,3072]{3,2,1,0:T(8,128)(2,1)S(1)}, u32[]{:S(2)}, u32[]{:S(2)}) %collective-permute-start.10) | collective-permute-done | bytes 786464 | tf_op jit(solution)/shard_map/ppermute | solution.py:255
  (305 shorter events, 351.6 us)
Async XLA Ops:
  7.2 77.6 %all-gather.4.cloned.1.call-start = ((), (), s32[]{:S(2)}) async-start(), calls=%async_computation.4 | async-start | bytes 6758400 | tf_op jit(solution)/shard_map/all_gather | solution.py:315
  9.8 354.5 %all-gather.6.cloned.1.call-start = ((), (), s32[]{:S(2)}) async-start(), calls=%async_computation.5 | async-start | bytes 19464192 | tf_op jit(solution)/shard_map/all_gather | solution.py:315
  169.8 85.2 %all-to-all-start = ((bf16[3,2,512,1024]{2,1,0,3:T(2,128)(2,1)}), bf16[3,2,512,1024]{2,1,0,3:T(2,128)(2,1)}, u32[]{:S(2)}, u32[]{:S(2)}) async-start(bf16[3,2,512,1024]{2,1,0,3:T(2,128)(2,1)} %copy.187), calls=%async_computation | async-start | bytes 12582912 | tf_op jit(solution)/shard_map/all_to_all | solution.py:281
  175.1 221.9 %all-gather.8.cloned.1.call-start = ((), (), s32[]{:S(2)}) async-start(), calls=%async_computation.6 | async-start | bytes 8650752 | tf_op jit(solution)/shard_map/all_gather | solution.py:315
  321.7 37.6 %all-to-all-start.1 = ((bf16[1,2,2048,256]{3,1,0,2:T(2,128)(2,1)}), bf16[1,2,2048,256]{3,1,0,2:T(2,128)(2,1)}, u32[]{:S(2)}, u32[]{:S(2)}) async-start(bf16[1,2,2048,256]{3,1,0,2:T(2,128)(2,1)} %copy.189), calls=%async_computation.1 | async-start | bytes 4194304 | tf_op jit(solution)/shard_map/all_to_all | solution.py:285
  444.4 212.8 %collective-permute-start.28 = (bf16[2,2,2,2,128,1024]{5,4,0,1,2,3:T(8,128)(2,1)}, bf16[2,2,2,2,128,1024]{5,4,0,1,2,3:T(8,128)(2,1)}, u32[]{:S(2)}, u32[]{:S(2)}) collective-permute-start(bf16[2,2,2,2,128,1024]{5,4,0,1,2,3:T(8,128)(2,1)} %bitcast.272), channel_id=1, source_target_pairs={{0,4},{1,5},{2,6},{3,7},{4,0},{5,1},{6,2},{7,3},{8,12},{9,13},{10,... | collective-permute-start | bytes 12582920 | tf_op jit(solution)/shard_map/ppermute | solution.py:255
  517.1 149.3 %collective-permute-start.23 = (bf16[2,2,2,2,32,4096]{5,4,2,3,0,1:T(8,128)(2,1)}, bf16[2,2,2,2,32,4096]{5,4,2,3,0,1:T(8,128)(2,1)}, u32[]{:S(2)}, u32[]{:S(2)}) collective-permute-start(bf16[2,2,2,2,32,4096]{5,4,2,3,0,1:T(8,128)(2,1)} %bitcast.273), channel_id=1, source_target_pairs={{0,4},{1,5},{2,6},{3,7},{4,0},{5,1},{6,2},{7,3},{8,12},{9,13},{10,... | collective-permute-start | bytes 12582920 | tf_op jit(solution)/shard_map/ppermute | solution.py:255
  526.1 169.0 %collective-permute-start.18 = (bf16[2,2,2,2,32,4096]{5,4,3,0,1,2:T(8,128)(2,1)}, bf16[2,2,2,2,32,4096]{5,4,3,0,1,2:T(8,128)(2,1)}, u32[]{:S(2)}, u32[]{:S(2)}) collective-permute-start(bf16[2,2,2,2,32,4096]{5,4,3,0,1,2:T(8,128)(2,1)} %bitcast.274), channel_id=1, source_target_pairs={{0,4},{1,5},{2,6},{3,7},{4,0},{5,1},{6,2},{7,3},{8,12},{9,13},{10,... | collective-permute-start | bytes 12582920 | tf_op jit(solution)/shard_map/ppermute | solution.py:255
  537.8 30.2 %all-to-all-start.2 = ((bf16[1,2,512,1024]{2,1,0,3:T(2,128)(2,1)}), bf16[1,2,512,1024]{2,1,0,3:T(2,128)(2,1)S(1)}, u32[]{:S(2)}, u32[]{:S(2)}) async-start(bf16[1,2,512,1024]{2,1,0,3:T(2,128)(2,1)} %copy.191), calls=%async_computation.2 | async-start | bytes 4194304 | tf_op jit(solution)/shard_map/all_to_all | solution.py:281
  574.0 83.1 %collective-permute-start.16 = (bf16[2,32,1024]{2,1,0:T(8,128)(2,1)S(1)}, bf16[2,32,1024]{2,1,0:T(8,128)(2,1)S(1)}, u32[]{:S(2)}, u32[]{:S(2)}) collective-permute-start(bf16[2,32,1024]{2,1,0:T(8,128)(2,1)S(1)} %fusion.63), channel_id=1, source_target_pairs={{0,8},{1,9},{2,10},{3,11},{4,12},{5,13},{6,14},{7,15},{8,0},{9,1},... | collective-permute-start | bytes 393224 | tf_op jit(solution)/shard_map/ppermute | solution.py:255
  651.6 139.5 %all-to-all-start.3 = ((bf16[3,2,2048,256]{3,1,0,2:T(2,128)(2,1)}), bf16[3,2,2048,256]{3,1,0,2:T(2,128)(2,1)}, u32[]{:S(2)}, u32[]{:S(2)}) async-start(bf16[3,2,2048,256]{3,1,0,2:T(2,128)(2,1)} %copy.194), calls=%async_computation.3 | async-start | bytes 12582912 | tf_op jit(solution)/shard_map/all_to_all | solution.py:285
  657.1 49.0 %collective-permute-start.17 = (bf16[32,1024]{1,0:T(8,128)(2,1)S(1)}, bf16[32,1024]{1,0:T(8,128)(2,1)S(1)}, u32[]{:S(2)}, u32[]{:S(2)}) collective-permute-start(bf16[32,1024]{1,0:T(8,128)(2,1)S(1)} %fusion.64), channel_id=1, source_target_pairs={{0,16},{1,17},{2,18},{3,19},{4,20},{5,21},{6,22},{7,23},{8,24},{9,... | collective-permute-start | bytes 196616 | tf_op jit(solution)/shard_map/ppermute | solution.py:255
  664.4 89.8 %collective-permute-start.29 = (bf16[2,2,2,128,1024]{4,3,0,1,2:T(8,128)(2,1)}, bf16[2,2,2,128,1024]{4,3,0,1,2:T(8,128)(2,1)}, u32[]{:S(2)}, u32[]{:S(2)}) collective-permute-start(bf16[2,2,2,128,1024]{4,3,0,1,2:T(8,128)(2,1)} %fusion.33), channel_id=1, source_target_pairs={{0,1},{1,0},{2,3},{3,2},{4,5},{5,4},{6,7},{7,6},{8,9},{9,8},{10,11... | collective-permute-start | bytes 6291464 | tf_op jit(solution)/shard_map/ppermute | solution.py:255
  671.7 88.7 %collective-permute-start.24 = (bf16[2,2,2,32,4096]{4,3,1,2,0:T(8,128)(2,1)}, bf16[2,2,2,32,4096]{4,3,1,2,0:T(8,128)(2,1)}, u32[]{:S(2)}, u32[]{:S(2)}) collective-permute-start(bf16[2,2,2,32,4096]{4,3,1,2,0:T(8,128)(2,1)} %fusion.32), channel_id=1, source_target_pairs={{0,8},{1,9},{2,10},{3,11},{4,12},{5,13},{6,14},{7,15},{8,0},{9,1},... | collective-permute-start | bytes 6291464 | tf_op jit(solution)/shard_map/ppermute | solution.py:255
  704.6 66.3 %collective-permute-start.19 = (bf16[2,2,2,32,4096]{4,3,2,0,1:T(8,128)(2,1)S(1)}, bf16[2,2,2,32,4096]{4,3,2,0,1:T(8,128)(2,1)S(1)}, u32[]{:S(2)}, u32[]{:S(2)}) collective-permute-start(bf16[2,2,2,32,4096]{4,3,2,0,1:T(8,128)(2,1)S(1)} %fusion.31), channel_id=1, source_target_pairs={{0,2},{1,3},{2,0},{3,1},{4,6},{5,7},{6,4},{7,5},{8,10},{9,11},{10,... | collective-permute-start | bytes 6291464 | tf_op jit(solution)/shard_map/ppermute | solution.py:255
  758.9 118.8 %collective-permute-start.30 = (bf16[2,2,128,1024]{3,2,0,1:T(8,128)(2,1)S(1)}, bf16[2,2,128,1024]{3,2,0,1:T(8,128)(2,1)}, u32[]{:S(2)}, u32[]{:S(2)}) collective-permute-start(bf16[2,2,128,1024]{3,2,0,1:T(8,128)(2,1)S(1)} %fusion.47), channel_id=1, source_target_pairs={{0,2},{1,3},{2,0},{3,1},{4,6},{5,7},{6,4},{7,5},{8,10},{9,11},{10,... | collective-permute-start | bytes 3145736 | tf_op jit(solution)/shard_map/ppermute | solution.py:255
  763.8 115.9 %collective-permute-start.25 = (bf16[2,2,32,4096]{3,2,0,1:T(8,128)(2,1)}, bf16[2,2,32,4096]{3,2,0,1:T(8,128)(2,1)}, u32[]{:S(2)}, u32[]{:S(2)}) collective-permute-start(bf16[2,2,32,4096]{3,2,0,1:T(8,128)(2,1)} %fusion.46), channel_id=1, source_target_pairs={{0,16},{1,17},{2,18},{3,19},{4,20},{5,21},{6,22},{7,23},{8,24},{9,... | collective-permute-start | bytes 3145736 | tf_op jit(solution)/shard_map/ppermute | solution.py:255
  774.0 107.8 %collective-permute-start.20 = (bf16[2,2,32,4096]{3,2,1,0:T(8,128)(2,1)}, bf16[2,2,32,4096]{3,2,1,0:T(8,128)(2,1)}, u32[]{:S(2)}, u32[]{:S(2)}) collective-permute-start(bf16[2,2,32,4096]{3,2,1,0:T(8,128)(2,1)} %fusion.45), channel_id=1, source_target_pairs={{0,8},{1,9},{2,10},{3,11},{4,12},{5,13},{6,14},{7,15},{8,0},{9,1},... | collective-permute-start | bytes 3145736 | tf_op jit(solution)/shard_map/ppermute | solution.py:255
  862.6 34.7 %collective-permute-start.8 = (bf16[2,2,2,2,32,3072]{5,4,3,0,1,2:T(8,128)(2,1)S(1)}, bf16[2,2,2,2,32,3072]{5,4,3,0,1,2:T(8,128)(2,1)S(1)}, u32[]{:S(2)}, u32[]{:S(2)}) collective-permute-start(bf16[2,2,2,2,32,3072]{5,4,3,0,1,2:T(8,128)(2,1)S(1)} %bitcast.307), channel_id=1, source_target_pairs={{0,4},{1,5},{2,6},{3,7},{4,0},{5,1},{6,2},{7,3},{8,12},{9,13},{10,... | collective-permute-start | bytes 9437192 | tf_op jit(solution)/shard_map/ppermute | solution.py:255
  883.4 30.6 %collective-permute-start.21 = (bf16[2,32,4096]{2,1,0:T(8,128)(2,1)S(1)}, bf16[2,32,4096]{2,1,0:T(8,128)(2,1)S(1)}, u32[]{:S(2)}, u32[]{:S(2)}) collective-permute-start(bf16[2,32,4096]{2,1,0:T(8,128)(2,1)S(1)} %fusion.52), channel_id=1, source_target_pairs={{0,16},{1,17},{2,18},{3,19},{4,20},{5,21},{6,22},{7,23},{8,24},{9,... | collective-permute-start | bytes 1572872 | tf_op jit(solution)/shard_map/ppermute | solution.py:255
  897.1 65.1 %collective-permute-start.32 = (bf16[128,1024]{1,0:T(8,128)(2,1)S(1)}, bf16[128,1024]{1,0:T(8,128)(2,1)S(1)}, u32[]{:S(2)}, u32[]{:S(2)}) collective-permute-start(bf16[128,1024]{1,0:T(8,128)(2,1)S(1)} %fusion.60), channel_id=1, source_target_pairs={{0,16},{1,17},{2,18},{3,19},{4,20},{5,21},{6,22},{7,23},{8,24},{9,... | collective-permute-start | bytes 786440 | tf_op jit(solution)/shard_map/ppermute | solution.py:255
  898.8 30.2 %collective-permute-start.9 = (bf16[2,2,2,32,3072]{4,3,2,0,1:T(8,128)(2,1)S(1)}, bf16[2,2,2,32,3072]{4,3,2,0,1:T(8,128)(2,1)S(1)}, u32[]{:S(2)}, u32[]{:S(2)}) collective-permute-start(bf16[2,2,2,32,3072]{4,3,2,0,1:T(8,128)(2,1)S(1)} %fusion.44), channel_id=1, source_target_pairs={{0,2},{1,3},{2,0},{3,1},{4,6},{5,7},{6,4},{7,5},{8,10},{9,11},{10,... | collective-permute-start | bytes 4718600 | tf_op jit(solution)/shard_map/ppermute | solution.py:255
  899.1 32.7 %collective-permute-start.27 = (bf16[32,4096]{1,0:T(8,128)(2,1)S(1)}, bf16[32,4096]{1,0:T(8,128)(2,1)S(1)}, u32[]{:S(2)}, u32[]{:S(2)}) collective-permute-start(bf16[32,4096]{1,0:T(8,128)(2,1)S(1)} %fusion.59), channel_id=1, source_target_pairs={{0,2},{1,3},{2,0},{3,1},{4,6},{5,7},{6,4},{7,5},{8,10},{9,11},{10,... | collective-permute-start | bytes 786440 | tf_op jit(solution)/shard_map/ppermute | solution.py:255
  914.2 31.9 %collective-permute-start.22 = (bf16[32,4096]{1,0:T(8,128)(2,1)S(1)}, bf16[32,4096]{1,0:T(8,128)(2,1)S(1)}, u32[]{:S(2)}, u32[]{:S(2)}) collective-permute-start(bf16[32,4096]{1,0:T(8,128)(2,1)S(1)} %fusion.58), channel_id=1, source_target_pairs={{0,1},{1,0},{2,3},{3,2},{4,5},{5,4},{6,7},{7,6},{8,9},{9,8},{10,11... | collective-permute-start | bytes 786440 | tf_op jit(solution)/shard_map/ppermute | solution.py:255
  (58 other events, 648.9 us)
Sparse Core Ops, SparseCore 0:
  11.5 73.2 all-gather.3
  87.7 166.1 all-gather.5
  256.7 80.8 all-gather.7

commit v2 on v1

v2 whole, which is shorter than its diff:
```python
import functools

import jax
import jax.numpy as jnp
from jax import lax
from jax.experimental import pallas as pl
from jax.experimental.pallas import tpu as pltpu
from jax.sharding import PartitionSpec as P

HEAD_DIM = 64
SPECIES = 8
EPS = 1e-05
LOG2E = 1.4426950408889634
BOTH = ("dp", "seq")
F32 = jnp.float32
BF16 = jnp.bfloat16
FF_BLOCK = 512
FEED_ROWS = 512
PARTS = 2
ROW_UNIT = 32
VMEM = 60 * 2**20

NN = (((1,), (0,)), ((), ()))
NT = (((1,), (1,)), ((), ()))


def dot(a, b, dims=NN):
    return lax.dot_general(a, b, dims, preferred_element_type=F32)


def shape(dims, dtype):
    return jax.ShapeDtypeStruct(dims, dtype)


def params():
    return pltpu.CompilerParams(vmem_limit_bytes=VMEM)


def cost(flops, moved, exps=0):
    return pl.CostEstimate(flops=flops, bytes_accessed=moved, transcendentals=exps)


def normalise(value):
    centered = value - jnp.mean(value, axis=-1, keepdims=True)
    inverse = lax.rsqrt(jnp.mean(centered * centered, axis=-1, keepdims=True) + EPS)
    return centered * inverse, inverse


def norm_back(grad, normal, inverse, gain):
    scaled = grad * gain
    centered = scaled - jnp.mean(scaled, axis=-1, keepdims=True)
    return inverse * (centered - normal * jnp.mean(scaled * normal, axis=-1, keepdims=True))


def turn(value, cosine, early, late):
    return value * cosine + pltpu.roll(value, 96, 1) * early + pltpu.roll(value, 32, 1) * late


def tables(positions):
    half = HEAD_DIM // 2
    freq = 10000.0 ** (-2.0 * jnp.arange(half, dtype=F32) / HEAD_DIM)
    angle = positions.astype(F32)[:, None] * freq[None, :]
    cosine, sine = jnp.cos(angle), jnp.sin(angle)
    zero = jnp.zeros_like(sine)
    return (
        jnp.concatenate([cosine] * 4, axis=1),
        jnp.concatenate([-sine, zero, -sine, zero], axis=1),
        jnp.concatenate([zero, sine, zero, sine], axis=1),
    )


def arrange_kernel(base_ref, *refs):
    for k, ref in enumerate(refs[:-1]):
        refs[-1][base_ref[0] ^ k] = ref[...]


def arrange(base, blocks):
    rows, width = blocks[0].shape
    return pl.pallas_call(
        arrange_kernel,
        grid_spec=pltpu.PrefetchScalarGridSpec(
            num_scalar_prefetch=1,
            grid=(1,),
            in_specs=[pl.BlockSpec((rows, width), lambda i, _: (0, 0))] * len(blocks),
            out_specs=pl.BlockSpec((len(blocks), rows, width), lambda i, _: (0, 0, 0)),
        ),
        out_shape=shape((len(blocks), rows, width), blocks[0].dtype),
        compiler_params=params(),
        cost_estimate=cost(0, 16 * rows * width),
        name="arrange",
    )(base, *blocks).reshape(len(blocks) * rows, width)


def settle_kernel(base_ref, *refs):
    blocks, added, out_ref = refs[:4], refs[4:-1], refs[-1]
    here = pl.program_id(0)

    for k, ref in enumerate(blocks):

        @pl.when((base_ref[0] ^ k) == here)
        def _(ref=ref):
            value = ref[...].astype(F32)
            out_ref[0] = value + added[0][0].astype(F32) if added else value


def settle(base, blocks, added):
    rows, width = blocks[0].shape
    block = pl.BlockSpec((1, rows, width), lambda i, _: (i, 0, 0))
    return pl.pallas_call(
        settle_kernel,
        grid_spec=pltpu.PrefetchScalarGridSpec(
            num_scalar_prefetch=1,
            grid=(4,),
            in_specs=[pl.BlockSpec((rows, width), lambda i, _: (0, 0))] * 4
            + [block] * len(added),
            out_specs=block,
        ),
        out_shape=shape((4, rows, width), F32),
        compiler_params=params(),
        cost_estimate=cost(0, 32 * rows * width),
        name="settle",
    )(base, *blocks, *[a.reshape(4, rows, width) for a in added])


def project_kernel(at_ref, x_ref, w_ref, vec_ref, c_ref, e_ref, l_ref, send_ref, n_ref):
    which = pl.program_id(0)
    _, rows, lanes = send_ref.shape

    @pl.when(which == 0)
    def _():
        normal, _ = normalise(x_ref[...].astype(F32))
        n_ref[...] = (normal * vec_ref[0:1] + vec_ref[1:2]).astype(BF16)

    product = dot(n_ref[...], w_ref[0])
    cosine, early, late = c_ref[...], e_ref[...], l_ref[...]

    def put(rotate):
        for at in range(0, lanes, 128):
            piece = product[:, at : at + 128]
            if rotate:
                piece = turn(piece, cosine, early, late)
            send_ref[0, :, at : at + 128] = piece.astype(BF16)

    pl.when(which < 2)(lambda: put(True))
    pl.when(which == 2)(lambda: put(False))


def project(at, tokens, weights, vectors, table, lanes):
    rows, width = tokens.shape
    wide = pl.BlockSpec((rows, 128), lambda j, _: (0, 0))
    return pl.pallas_call(
        project_kernel,
        grid_spec=pltpu.PrefetchScalarGridSpec(
            num_scalar_prefetch=1,
            grid=(3,),
            in_specs=[
                pl.BlockSpec((rows, width), lambda j, _: (0, 0)),
                pl.BlockSpec((1, width, lanes), lambda j, at: (j, 0, at[0])),
                pl.BlockSpec((4, width), lambda j, _: (0, 0)),
                wide,
                wide,
                wide,
            ],
            out_specs=[
                pl.BlockSpec((1, rows, lanes), lambda j, _: (j, 0, 0)),
                pl.BlockSpec((rows, width), lambda j, _: (0, 0)),
            ],
        ),
        out_shape=[shape((3, rows, lanes), BF16), shape((rows, width), BF16)],
        compiler_params=params(),
        cost_estimate=cost(6 * rows * width * lanes, 6 * rows * lanes + 6 * width * lanes),
        name="project",
    )(at, tokens, weights, vectors, *table)


def attend_kernel(info_ref, *refs, team):
    q_refs, k_refs, v_refs = refs[:team], refs[team : 2 * team], refs[2 * team : 3 * team]
    o_refs, (l_ref, vt_ref) = refs[3 * team : 4 * team], refs[4 * team :]
    length, side, upper = info_ref[0], info_ref[1], info_ref[2]
    lane = lax.broadcasted_iota(jnp.int32, (1, 128), 1)
    block = q_refs[0].shape[0]
    keys, ups = 2 * block, team // 2
    up = pl.program_id(2)

    def chunk(arrays, p, b):
        rows = slice(b * block, (b + 1) * block)
        return jnp.concatenate([arrays[2 * p][rows], arrays[2 * p + 1][rows]], axis=0)

    @pl.when((pl.program_id(1) == 0) & (up == 0))
    def _():
        for p in range(ups):
            for b in range(4):
                at = (4 * p + b) * keys
                vt_ref[:, at : at + keys] = chunk(v_refs, p, b).T

    q2 = jnp.concatenate([q_refs[0][...], q_refs[1][...]], axis=0)
    for p in range(1, ups):
        other = jnp.concatenate([q_refs[2 * p][...], q_refs[2 * p + 1][...]], axis=0)
        q2 = jnp.where(up == p, other, q2)
    q2 = q2 * BF16(0.125)

    def positions(p, b):
        row = lax.broadcasted_iota(jnp.int32, (keys, keys), 0)
        return row ^ (side * block) | (4 * (upper ^ p) + b) * keys

    def run(chunks):
        k2 = jnp.concatenate([chunk(k_refs, c // 4, c % 4) for c in range(chunks)], axis=0)
        n = chunks * keys
        outs = []
        for h in range(2):
            qh = jnp.where((lane // 64) == h, q2, BF16(0))
            s = dot(k2, qh, NT)
            if ups == 1:
                last = jnp.where(positions(0, chunks - 1) < length, s[n - keys :], -1e30)
                s = jnp.concatenate([s[: n - keys], last], 0) if chunks > 1 else last
            else:
                valid = [positions(c // 4, c % 4) < length for c in range(chunks)]
                s = jnp.concatenate(
                    [jnp.where(v, s[c * keys : (c + 1) * keys], -1e30) for c, v in enumerate(valid)],
                    axis=0,
                )
            m = jnp.max(s, axis=0, keepdims=True)
            p = jnp.exp2((s - m) * LOG2E)
            all_p = jnp.sum(p, axis=0, keepdims=True)
            o = dot(vt_ref[h * 64 : h * 64 + 64, :n], p.astype(BF16))
            outs.append(o / all_p)
            l_ref[0, h : h + 1] = m + jnp.log(all_p)
        result = jnp.concatenate(outs, 0).T.astype(BF16)
        for p in range(ups):

            @pl.when(up == p)
            def _(p=p):
                o_refs[2 * p][...] = result[:block]
                o_refs[2 * p + 1][...] = result[block:]

    if ups == 1:
        blocks = (length + keys - 1) // keys
        for i in range(4):
            pl.when(blocks == i + 1)(functools.partial(run, i + 1))
    else:
        run(4 * ups)


def attend(info, qkv):
    team = len(qkv)
    _, rows, lanes = qkv[0].shape
    span, pairs, ups = team * rows, lanes // 128, team // 2
    block = rows // 4

    def whole(which):
        return [pl.BlockSpec((None, rows, 128), lambda h, b, u, _: (which, 0, h))] * team

    return pl.pallas_call(
        functools.partial(attend_kernel, team=team),
        grid_spec=pltpu.PrefetchScalarGridSpec(
            num_scalar_prefetch=1,
            grid=(pairs, 4, ups),
            in_specs=[pl.BlockSpec((None, block, 128), lambda h, b, u, _: (0, b, h))] * team
            + whole(1)
            + whole(2),
            out_specs=[pl.BlockSpec((block, 128), lambda h, b, u, _: (b, h))] * team
            + [pl.BlockSpec((1, 2, 2 * block), lambda h, b, u, _: (h, 0, b * ups + u))],
            scratch_shapes=[pltpu.VMEM((128, span), BF16)],
        ),
        out_shape=[shape((rows, lanes), BF16)] * team + [shape((pairs, 2, span), F32)],
        compiler_params=params(),
        cost_estimate=cost(16 * span * span * lanes, 8 * span * lanes, span * span * lanes // 64),
        name="attend",
    )(info, *qkv, *qkv, *qkv)


def attend_back_kernel(info_ref, *refs, team):
    q_refs, k_refs, v_refs, o_refs, g_refs = (refs[i * team : (i + 1) * team] for i in range(5))
    l_ref, d_refs = refs[5 * team], refs[5 * team + 1 : 6 * team + 1]
    kt_ref, dk_ref, dv_ref = refs[6 * team + 1 :]
    length, side, upper = info_ref[0], info_ref[1], info_ref[2]
    lane = lax.broadcasted_iota(jnp.int32, (1, 128), 1)
    block = q_refs[0].shape[0]
    keys, ups = 2 * block, team // 2
    b, up = pl.program_id(1), pl.program_id(2)
    first = (4 * (upper ^ up) + b) * keys

    def chunk(arrays, p, c):
        rows = pl.ds(pl.multiple_of(c * block, block), block)
        return jnp.concatenate([arrays[2 * p][rows], arrays[2 * p + 1][rows]], axis=0)

    def queries(arrays):
        value = jnp.concatenate([arrays[0][...], arrays[1][...]], axis=0)
        for p in range(1, ups):
            other = jnp.concatenate([arrays[2 * p][...], arrays[2 * p + 1][...]], axis=0)
            value = jnp.where(up == p, other, value)
        return value

    @pl.when((b == 0) & (up == 0))
    def _():
        for p in range(ups):
            for c in range(4):
                at = (4 * p + c) * keys
                kt_ref[:, at : at + keys] = (chunk(k_refs, p, c) * BF16(0.125)).T
        dk_ref[...] = jnp.zeros_like(dk_ref)
        dv_ref[...] = jnp.zeros_like(dv_ref)

    here = pl.ds(pl.multiple_of(b * block, block), block)

    def put(value):
        for p in range(ups):

            @pl.when(up == p)
            def _(p=p):
                d_refs[2 * p][0, here] = value[:block]
                d_refs[2 * p + 1][0, here] = value[block:]

    @pl.when(first >= length)
    def _():
        put(jnp.zeros((keys, 128), BF16))

    @pl.when(first < length)
    def _():
        q2 = queries(q_refs) * BF16(0.125)
        g2 = queries(g_refs)
        products = (g2.astype(F32) * queries(o_refs).astype(F32)).T
        qs, gs, ls, ds = [], [], [], []
        for h in range(2):
            mine = (lane // 64) == h
            qs.append(jnp.where(mine, q2, BF16(0)))
            gs.append(jnp.where(mine, g2, BF16(0)))
            ls.append(l_ref[0, h : h + 1] * LOG2E)
            ds.append(jnp.sum(products[h * 64 : h * 64 + 64], axis=0, keepdims=True))
        qc = jnp.concatenate(qs, 0)
        gc = jnp.concatenate(gs, 0)
        lc = jnp.concatenate(ls, 1)
        dc = jnp.concatenate(ds, 1)
        acc = (jnp.zeros((64, keys), F32),) * 2
        for p in range(ups):
            start = 4 * (upper ^ p) * keys

            def step(c, acc, masked, p=p, start=start):
                sl = pl.ds(pl.multiple_of((4 * p + c) * keys, keys), keys)
                k2 = chunk(k_refs, p, c)
                v2 = chunk(v_refs, p, c)
                prob = jnp.exp2(dot(k2, qc, NT) * LOG2E - lc)
                if masked:
                    row = lax.broadcasted_iota(jnp.int32, (keys, 1), 0)
                    row = row ^ (side * block) | (start + c * keys)
                    prob = jnp.where(row < length, prob, 0.0)
                gp = dot(v2, gc, NT)
                gs_low = (prob * (gp - dc)).astype(BF16)
                dv_ref[sl] += dot(prob.astype(BF16), gc)
                dk_ref[sl] += dot(gs_low, qc)
                return tuple(
                    acc[h]
                    + dot(kt_ref[h * 64 : h * 64 + 64, sl], gs_low[:, h * keys : (h + 1) * keys])
                    for h in range(2)
                )

            valid = jnp.clip(length - start, 0, 4 * keys)
            full = valid // keys
            acc = lax.fori_loop(0, full, lambda c, a: step(c, a, False), acc)
            acc = lax.cond(
                full * keys < valid, lambda a: step(full, a, True), lambda a: a, acc
            )
        put(jnp.concatenate(acc, 0).T.astype(BF16))

    @pl.when((b == 3) & (up == ups - 1))
    def _():
        for p in range(ups):
            for c in range(4):
                at = (4 * p + c) * keys
                for t, ref in ((1, dk_ref), (2, dv_ref)):
                    for m in range(2):
                        rows = slice(c * block, (c + 1) * block)
                        piece = ref[at + m * block : at + (m + 1) * block]
                        d_refs[2 * p + m][t, rows] = piece.astype(BF16)


def attend_back(info, qkv, mixed, grad, lse, part):
    team = len(qkv)
    _, rows, lanes = qkv[0].shape
    span, pairs, ups = team * rows, lanes // 128 // PARTS, team // 2
    block = rows // 4
    spot = pl.BlockSpec((block, 128), lambda h, b, u, _: (b, part * pairs + h))

    def whole(which):
        return [
            pl.BlockSpec((None, rows, 128), lambda h, b, u, _: (which, 0, part * pairs + h))
        ] * team

    return pl.pallas_call(
        functools.partial(attend_back_kernel, team=team),
        grid_spec=pltpu.PrefetchScalarGridSpec(
            num_scalar_prefetch=1,
            grid=(pairs, 4, ups),
            in_specs=[
                pl.BlockSpec((None, block, 128), lambda h, b, u, _: (0, b, part * pairs + h))
            ]
            * team
            + whole(1)
            + whole(2)
            + [spot] * (2 * team)
            + [
                pl.BlockSpec(
                    (1, 2, 2 * block), lambda h, b, u, _: (part * pairs + h, 0, b * ups + u)
                )
            ],
            out_specs=[pl.BlockSpec((3, rows, 128), lambda h, b, u, _: (0, 0, h))] * team,
            scratch_shapes=[
                pltpu.VMEM((128, span), BF16),
                pltpu.VMEM((span, 128), F32),
                pltpu.VMEM((span, 128), F32),
            ],
        ),
        out_shape=[shape((3, rows, pairs * 128), BF16)] * team,
        compiler_params=params(),
        cost_estimate=cost(
            30 * span * span * pairs * 128, 16 * span * pairs * 128, 2 * span * span * pairs
        ),
        name="attend_back",
    )(info, *qkv, *qkv, *qkv, *mixed, *grad, lse)


def feed_kernel(
    at_ref, x_ref, cot_ref, scale_ref, vec_ref, wo_ref, wg_ref, wu_ref, wd_ref, *refs, team
):
    mix_refs, send_refs = refs[:team], refs[team : 2 * team]
    (
        delta_ref, gm_ref, gml_ref, n_ref, gl_ref, hid_ref, gg_ref, gu_ref, sum_ref, rows_ref,
        acc_ref, normal_ref, inv_ref,
    ) = refs[2 * team :]
    step = pl.program_id(1)
    lanes = mix_refs[0].shape[1]

    def whole(ref):
        return ref[...].reshape(-1, ref.shape[-1])

    def spot(m):
        return pl.ds(pl.multiple_of((at_ref[0] ^ m) * lanes, lanes), lanes)

    @pl.when(step == 0)
    def _():
        for m in range(team):
            rows_ref[:, spot(m)] = mix_refs[m][...]
        added = dot(rows_ref[...], whole(wo_ref))
        acc_ref[...] = added
        normal, inverse = normalise(x_ref[...].astype(F32) + added)
        normal_ref[...] = normal
        inv_ref[...] = inverse
        n_ref[...] = (normal * vec_ref[2:3] + vec_ref[3:4]).astype(BF16)
        gl_ref[...] = (cot_ref[...].astype(F32) * scale_ref[...]).astype(BF16)
        gm_ref[...] = jnp.zeros_like(gm_ref)

    wg, wu, wd = whole(wg_ref), whole(wu_ref), whole(wd_ref)
    normed = n_ref[...]
    gate = dot(normed, wg)
    upper = dot(normed, wu)
    sigma = jax.nn.sigmoid(gate)
    silu = gate * sigma
    hidden = (silu * upper).astype(BF16)
    hid_ref[...] = hidden
    grad_hidden = dot(gl_ref[...], wd, NT)
    grad_up = (grad_hidden * silu).astype(BF16)
    grad_gate = (grad_hidden * upper * sigma * (1.0 + gate * (1.0 - sigma))).astype(BF16)
    gu_ref[...] = grad_up
    gg_ref[...] = grad_gate
    acc_ref[...] += dot(hidden, wd)
    gm_ref[...] += dot(grad_gate, wg, NT) + dot(grad_up, wu, NT)

    @pl.when(step == pl.num_programs(1) - 1)
    def _():
        delta_ref[...] = acc_ref[...].astype(BF16)
        grad = gm_ref[...]
        normal = normal_ref[...]

        @pl.when(pl.program_id(0) == 0)
        def _():
            sum_ref[...] = jnp.zeros_like(sum_ref)

        sum_ref[0:1] += jnp.sum(grad * normal, axis=0, keepdims=True)
        sum_ref[1:2] += jnp.sum(grad, axis=0, keepdims=True)
        total_grad = cot_ref[...].astype(F32) * scale_ref[...] + norm_back(
            grad, normal, inv_ref[...], vec_ref[2:3]
        )
        gm_ref[...] = total_grad
        low = total_grad.astype(BF16)
        gml_ref[...] = low
        acc_ref[...] = dot(low, whole(wo_ref), NT)
        for m in range(team):
            send_refs[m][...] = acc_ref[:, spot(m)].astype(BF16)


def feed(at, tokens, cotangent, scale, mixed, vectors, weights):
    team = len(mixed)
    rows, width = tokens.shape
    lanes = width // team
    units = weights.shape[0]
    tall = 4 * ROW_UNIT
    ff = units * tall
    columns = width // FF_BLOCK
    each = min(FEED_ROWS, rows)
    const = pl.BlockSpec((each, width), lambda i, j, _: (i, 0))
    block = pl.BlockSpec((each, FF_BLOCK), lambda i, j, _: (i, j))
    mix = pl.BlockSpec((each, lanes), lambda i, j, _: (i, 0))

    def part(first):
        return pl.BlockSpec(
            (units, ROW_UNIT, FF_BLOCK), lambda i, j, _: (0, first + j // columns, j % columns)
        )

    return pl.pallas_call(
        functools.partial(feed_kernel, team=team),
        grid_spec=pltpu.PrefetchScalarGridSpec(
            num_scalar_prefetch=1,
            grid=(rows // each, ff // FF_BLOCK),
            in_specs=[
                const,
                const,
                pl.BlockSpec((each, 1), lambda i, j, _: (i, 0)),
                pl.BlockSpec((4, width), lambda i, j, _: (0, 0)),
                pl.BlockSpec((units, ROW_UNIT, width), lambda i, j, _: (0, 4, 0)),
                part(5),
                part(9),
                pl.BlockSpec((FF_BLOCK // tall, tall, width), lambda i, j, _: (j, 0, 0)),
            ]
            + [mix] * team,
            out_specs=[mix] * team
            + [const, const, const, const, const, block, block, block]
            + [pl.BlockSpec((2, width), lambda i, j, _: (0, 0)), const],
            scratch_shapes=[
                pltpu.VMEM((each, width), F32),
                pltpu.VMEM((each, width), F32),
                pltpu.VMEM((each, 1), F32),
            ],
        ),
        out_shape=[shape((rows, lanes), BF16)] * team
        + [
            shape((rows, width), BF16),
            shape((rows, width), F32),
            shape((rows, width), BF16),
            shape((rows, width), BF16),
            shape((rows, width), BF16),
            shape((rows, ff), BF16),
            shape((rows, ff), BF16),
            shape((rows, ff), BF16),
            shape((2, width), F32),
            shape((rows, width), BF16),
        ],
        compiler_params=params(),
        cost_estimate=cost(
            12 * rows * width * ff + 4 * rows * width * width,
            12 * width * ff + 6 * rows * ff + 30 * rows * width,
            rows * ff,
        ),
        name="feed",
    )(at, tokens, cotangent, scale, vectors, weights, weights, weights, weights, *mixed)


def weight_kernel(core_ref, a_ref, b_ref, own_ref, away_ref, at_ref, *, size):
    rows, tall = a_ref.shape
    core = core_ref[0]
    outs = (own_ref, away_ref)

    @pl.when(pl.program_id(1) == 0)
    def _():
        for side in range(2):
            half = core if side == 0 else 1 - core
            for c in range(tall // (2 * size)):
                start = pl.multiple_of((2 * c + half) * size, 128)
                at_ref[side, c * size : (c + 1) * size] = a_ref[:, pl.ds(start, size)].T

    wide = own_ref.shape[-1]
    for side in range(2):
        outs[side][...] = dot(at_ref[side], b_ref[...].reshape(rows, wide)).astype(BF16)


def weight_grad(core, a, b, chunk):
    rows, tall = a.shape
    stacked = b.ndim == 3
    wide = b.shape[0] * b.shape[2] if stacked else b.shape[1]
    if chunk < 128:
        a = a.reshape(rows, tall // (2 * chunk), 2, chunk).swapaxes(1, 2).reshape(rows, tall)
        chunk = tall // 2
    columns = b.shape[2] if stacked else min(1024, wide)
    block = max(1024, 2 * chunk)
    if stacked:
        right = pl.BlockSpec((1, rows, columns), lambda i, j, _: (j, 0, 0))
    else:
        right = pl.BlockSpec((rows, columns), lambda i, j, _: (0, j))
    out = pl.BlockSpec((block // 2, columns), lambda i, j, _: (i, j))
    return pl.pallas_call(
        functools.partial(weight_kernel, size=chunk),
        grid_spec=pltpu.PrefetchScalarGridSpec(
            num_scalar_prefetch=1,
            grid=(tall // block, wide // columns),
            in_specs=[pl.BlockSpec((rows, block), lambda i, j, _: (0, i)), right],
            out_specs=[out, out],
            scratch_shapes=[pltpu.VMEM((2, block // 2, rows), BF16)],
        ),
        out_shape=[shape((tall // 2, wide), BF16)] * 2,
        compiler_params=params(),
        cost_estimate=cost(2 * rows * tall * wide, 2 * (rows * tall + rows * wide + tall * wide)),
        name="weight_grad",
    )(core, a, b)


def unturn_kernel(at_ref, c_ref, e_ref, l_ref, *refs):
    blocks, out_ref = refs[:-1], refs[-1]
    cosine, early, late = c_ref[...], e_ref[...], l_ref[...]
    which = pl.program_id(0)
    lanes = blocks[0].shape[-1]
    for m, ref in enumerate(blocks):
        for at in range(0, lanes, 128):
            spot = pl.ds(pl.multiple_of((at_ref[0] ^ m) * lanes + at, 128), 128)

            @pl.when(which < 2)
            def _(ref=ref, at=at, spot=spot):
                piece = turn(ref[0, :, at : at + 128].astype(F32), cosine, -early, -late)
                out_ref[0, :, spot] = piece.astype(BF16)

            @pl.when(which == 2)
            def _(ref=ref, at=at, spot=spot):
                out_ref[0, :, spot] = ref[0, :, at : at + 128]


def unturn(at, blocks, table):
    _, rows, lanes = blocks[0].shape
    wide = pl.BlockSpec((rows, 128), lambda j, _: (0, 0))
    team = len(blocks)
    return pl.pallas_call(
        unturn_kernel,
        grid_spec=pltpu.PrefetchScalarGridSpec(
            num_scalar_prefetch=1,
            grid=(3,),
            in_specs=[wide] * 3 + [pl.BlockSpec((1, rows, lanes), lambda j, _: (j, 0, 0))] * team,
            out_specs=pl.BlockSpec((1, rows, team * lanes), lambda j, _: (j, 0, 0)),
        ),
        out_shape=shape((3, rows, team * lanes), BF16),
        compiler_params=params(),
        cost_estimate=cost(0, 12 * rows * team * lanes),
        name="unturn",
    )(at, *table, *blocks)


def project_back_kernel(x_ref, gm_ref, vec_ref, w_ref, low_ref, *refs, part, lanes, first, last):
    which = pl.program_id(0)
    acc_ref = refs[-1]

    @pl.when(which == 0)
    def _():
        acc_ref[...] = jnp.zeros_like(acc_ref) if first else refs[0][...]

    width = w_ref.shape[-1]
    weight = jnp.concatenate(
        [
            w_ref[0, :, at : at + lanes]
            for at in range(part * lanes, width, PARTS * lanes)
        ],
        axis=1,
    )
    acc_ref[...] += dot(low_ref[0], weight, NT)

    if last:
        out_ref, sum_ref = refs[-3:-1]

        @pl.when(which == 2)
        def _():
            grad = acc_ref[...]
            normal, inverse = normalise(x_ref[...].astype(F32))
            sum_ref[0:1] = jnp.sum(grad * normal, axis=0, keepdims=True)
            sum_ref[1:2] = jnp.sum(grad, axis=0, keepdims=True)
            grad = gm_ref[...] + norm_back(grad, normal, inverse, vec_ref[0:1])
            out_ref[...] = grad.astype(BF16)


def project_back(tokens, grad_middle, vectors, weights, low, part, team, partial):
    rows, width = tokens.shape
    wide = low.shape[-1]
    last = part == PARTS - 1
    const = pl.BlockSpec((rows, width), lambda j: (0, 0))
    return pl.pallas_call(
        functools.partial(
            project_back_kernel, part=part, lanes=wide // team, first=not partial, last=last
        ),
        grid=(3,),
        in_specs=[
            const,
            const,
            pl.BlockSpec((4, width), lambda j: (0, 0)),
            pl.BlockSpec((1, width, width), lambda j: (j, 0, 0)),
            pl.BlockSpec((1, rows, wide), lambda j: (j, 0, 0)),
        ]
        + [const] * len(partial),
        out_specs=[const, pl.BlockSpec((2, width), lambda j: (0, 0))] if last else [const],
        out_shape=(
            [shape((rows, width), BF16), shape((2, width), F32)]
            if last
            else [shape((rows, width), F32)]
        ),
        scratch_shapes=[pltpu.VMEM((rows, width), F32)] if last else [],
        compiler_params=params(),
        cost_estimate=cost(6 * rows * width * wide, 18 * rows * width + 6 * width * width),
        name="project_back",
    )(tokens, grad_middle, vectors, weights, low, *partial)


def place_kernel(me_ref, *refs, masks):
    count = len(masks)
    halves, (wide_ref, small_ref, sem) = refs[: 2 * count], refs[2 * count :]
    me = me_ref[0]
    for wait in (False, True):
        for t in range(count):
            half = len(masks[t]) // 2
            for j, mask in enumerate(masks[t]):
                source = halves[2 * t + j // half].at[j % half]
                place = wide_ref.at[t, me ^ mask] if t < count - 1 else small_ref.at[me ^ mask]
                copy = pltpu.make_async_copy(source, place, sem.at[t, j])
                copy.wait() if wait else copy.start()


class Chain:
    def __init__(self, links, own, away, rounds, wire=BF16):
        self.links, self.rounds, self.wire = links, [list(r) for r in rounds], wire
        self.axes = [b for b in range(links.bits - 1, -1, -1) if b != links.core]
        self.dims = (2,) * len(self.axes) + (own.shape[0] * 2 // links.count,) + own.shape[1:]
        self.terms = [own.reshape(self.dims), links.swap(away, 1 << links.core).reshape(self.dims)]

    def pick(self, mask):
        me, parts, axes = self.links.me() ^ mask, self.terms, list(self.axes)
        for bit in self.rounds[0]:
            at = axes.index(bit)
            parts = [
                lax.dynamic_index_in_dim(p, (me >> bit) & 1, at, keepdims=False) for p in parts
            ]
            axes.pop(at)
        return parts

    def split(self):
        self.masks = [0]
        for bit in self.rounds[0]:
            self.masks += [m | 1 << bit for m in self.masks]
        sent = [total(self.pick(m)).astype(self.wire) for m in self.masks[1:]]
        self.kept = self.pick(0)
        return sent

    def swap(self, sent):
        return [self.links.swap(v, m) for v, m in zip(sent, self.masks[1:])]

    def take(self, received):
        for bit in self.rounds.pop(0):
            self.axes.remove(bit)
        self.terms = self.kept + list(received)

    def result(self):
        return total(self.terms)


def total(terms):
    return functools.reduce(jnp.add, [t.astype(F32) for t in terms])


def tie(values, *others):
    return lax.optimization_barrier((values, others))[0]


def beside(chains, work, *values):
    chains = [c for c in chains if c.rounds]
    sent = [c.split() for c in chains]
    values, sent = lax.optimization_barrier((values, sent))
    received = [c.swap(v) for c, v in zip(chains, sent)]
    result = work(*values)
    for c, r in zip(chains, tie(received, jax.tree.leaves(result))):
        c.take(r)
    return result


class Links:
    def __init__(self, mesh):
        self.dp, self.seq = mesh.shape["dp"], mesh.shape["seq"]
        self.count = self.dp * self.seq
        self.bits = self.count.bit_length() - 1
        self.core = self.seq.bit_length() - 1
        seq_bits = list(range(self.core))
        dp_bits = list(range(self.core + 1, self.bits))
        self.dp_bits = [self.core] + dp_bits
        first, last = dp_bits[:1], dp_bits[1:]
        self.seq_first = [[seq_bits[0]], seq_bits[1:], dp_bits]
        self.seq_last = [[seq_bits[-1]], seq_bits[:-1], dp_bits]
        self.dp_first = [first, [seq_bits[0]], seq_bits[1:] + last]
        self.dp_last = [first, [seq_bits[-1]], seq_bits[:-1] + last]
        self.direct = [seq_bits, dp_bits]
        self.direct_back = [dp_bits, seq_bits]
        self.orders = [
            seq_bits + dp_bits,
            seq_bits[::-1] + dp_bits,
            dp_bits[:1] + seq_bits + dp_bits[1:],
            dp_bits[:1] + seq_bits[::-1] + dp_bits[1:],
        ]

        self.team_bits = [self.core] + seq_bits[2:]
        self.team = 2 ** len(self.team_bits)

    def bit(self, which):
        return (self.me() >> which) & 1

    def route(self, k):
        pairs = []
        for i in range(self.count):
            core, y, x = (i >> self.core) & 1, (i >> 1) & 1, i & 1
            rest = i & ~((1 << self.core) | 3)
            pairs.append((i, rest | (y ^ (k >> 1)) << self.core | core << 1 | (x ^ (k & 1))))
        return pairs

    def to_team(self, value):
        wins, rows, width = value.shape
        blocks = value.reshape(wins * 2, rows // 2, width)
        place = 2 * self.bit(0) + self.bit(1)
        received = []
        for k in range(4):
            away = lax.dynamic_index_in_dim(
                blocks, place ^ (2 * (k & 1) + (k >> 1)), 0, keepdims=False
            )
            received.append(lax.ppermute(away, BOTH, self.route(k)))
        return received

    def from_team(self, value):
        rows, width = value.shape
        blocks = value.reshape(4, rows // 4, width)
        base = self.base()
        received = []
        for k in range(4):
            away = lax.dynamic_index_in_dim(blocks, base ^ k, 0, keepdims=False)
            back = [(j, i) for i, j in self.route(k)]
            received.append(lax.ppermute(away, BOTH, back))
        return [received[k] for k in (0, 2, 1, 3)]

    def base(self):
        return 2 * self.bit(self.core) + self.bit(0)

    def member(self):
        return sum(self.bit(b) << i for i, b in enumerate(self.team_bits))

    def exchange(self, values):
        masks = [
            sum(1 << b for i, b in enumerate(self.team_bits) if m >> i & 1)
            for m in range(self.team)
        ]
        return [v if m == 0 else self.swap(v, masks[m]) for m, v in enumerate(values)]

    def me(self):
        return lax.axis_index("dp") * self.seq + lax.axis_index("seq")

    def swap(self, value, mask):
        return lax.ppermute(value, BOTH, [(i, i ^ mask) for i in range(self.count)])

    def chip_sum(self, own, away):
        both = total([own, self.swap(away, 1 << self.core)]).astype(BF16)
        groups = [
            [d * self.seq + s for d in range(c, self.dp, 2) for s in range(self.seq)]
            for c in range(2)
        ]
        summed = lax.psum_scatter(
            both, BOTH, scatter_dimension=0, axis_index_groups=groups, tiled=True
        )
        return summed.astype(F32)

    def own(self):
        return jnp.reshape(lax.axis_index("dp") % 2, (1,))

    def gather(self, values, orders):
        args, masks, early = [], [], []
        for value, order in zip(values, orders):
            order = order[::-1] + [self.core]
            held, mask = value[None], [0]
            for bit in order:
                got = self.swap(held, 1 << bit)
                if bit == order[-3]:
                    early.append(got)
                mask = mask + [m | 1 << bit for m in mask]
                if bit == self.core:
                    args += [held, got]
                else:
                    held = jnp.concatenate([held, got], axis=0)
            masks.append(mask)
        wide = (len(values) - 1, self.count) + values[0].shape
        narrow = (self.count,) + values[-1].shape
        placed = pl.pallas_call(
            functools.partial(place_kernel, masks=masks),
            grid_spec=pltpu.PrefetchScalarGridSpec(
                num_scalar_prefetch=1,
                grid=(1,),
                in_specs=[pl.BlockSpec(memory_space=pl.ANY)] * len(args),
                out_specs=[
                    pl.BlockSpec(wide, lambda i, _: (0, 0, 0, 0)),
                    pl.BlockSpec(narrow, lambda i, _: (0, 0, 0)),
                ],
                scratch_shapes=[pltpu.SemaphoreType.DMA((len(values), self.count))],
            ),
            out_shape=[shape(wide, BF16), shape(narrow, BF16)],
            compiler_params=params(),
            name="place",
        )(jnp.reshape(self.me(), (1,)), *args)
        return placed, early

    def window_sum(self, value):
        for bit in self.dp_bits:
            value = value + self.swap(value, 1 << bit)
        return value


def packed(w_down, w_out, w_gate, w_up, width):
    parts = [w_down, w_out]
    for weight in (w_gate, w_up):
        parts += [weight[:, c : c + width] for c in range(0, weight.shape[1], width)]
    return jnp.concatenate(parts, axis=0)


def regrouped(gathered, each, width):
    if each == ROW_UNIT:
        return gathered
    tall = 4 * each
    down = gathered[:, :tall].reshape(-1, 4 * ROW_UNIT, width)
    parts = [down]
    for at in range(tall, gathered.shape[1], each):
        parts.append(gathered[:, at : at + each].reshape(-1, ROW_UNIT, width))
    return jnp.concatenate(parts, axis=1)


def body(
    links,
    tokens,
    cotangent,
    lengths,
    species,
    ln1_gain,
    ln1_bias,
    w_query,
    w_key,
    w_value,
    w_out,
    ln2_gain,
    ln2_bias,
    w_gate,
    w_up,
    w_down,
):
    wins, rows, width = tokens.shape
    each = w_query.shape[0]
    team = links.team
    lanes = width // team
    share = wins * rows
    scalar = functools.partial(jnp.reshape, shape=(1,))
    member = links.member()
    base = scalar(links.base())

    small = jnp.stack([ln1_gain, ln1_bias, ln2_gain, ln2_bias], axis=1)
    small = jnp.pad(small, ((0, 0), (0, 124)))
    local = [w_query, w_key, w_value, small]
    moved = links.to_team(tokens)
    told = jnp.stack([lengths, species])
    told = jnp.stack([told, links.swap(told, 1 << links.core)])
    (qkv_w, small), early = links.gather(local, links.orders)
    mine = tie(packed(w_down, w_out, w_gate, w_up, width), early)
    weights = regrouped(lax.all_gather(mine, BOTH, axis=0), each, width)
    qkv_w = qkv_w.reshape(3, width, width)
    vectors = small.reshape(width, 128)[:, :4].T.astype(F32)

    told = lax.dynamic_index_in_dim(told, links.bit(1) ^ links.bit(links.core), 0, keepdims=False)
    told = lax.dynamic_index_in_dim(told, links.bit(0), 1, keepdims=False)
    length, kind = told[0], told[1]
    upper = member >> 1
    half = rows // 2
    block = (4 * upper + jnp.arange(4))[:, None] * rows + links.bit(links.core) * half
    positions = (block + jnp.arange(half)[None, :]).reshape(share)
    table = tables(positions)
    info = jnp.stack([length, member & 1, upper])

    rows_in = arrange(base, moved)
    projected = []
    for m in range(team)[::-1]:
        projected.append(project(scalar(member ^ m), rows_in, qkv_w, vectors, table, lanes))
    projected = projected[::-1]
    normed_one = projected[0][1]
    cot_moved = links.to_team(tie(cotangent, [p[0] for p in projected[1:]]))
    species_ids = jnp.arange(SPECIES)
    onehot = (species[:, None] == species_ids[None, :]).astype(F32)
    counts = jnp.sum(onehot * lengths[:, None].astype(F32), axis=0)
    counts = links.window_sum(tie(counts, projected[-1][0]))
    window_weight = SPECIES * jnp.sum((kind == species_ids) * counts) / jnp.sum(counts)
    row_scale = jnp.where(positions < length, window_weight, 0.0)[:, None]

    qkv = links.exchange([p[0] for p in projected])
    *mixed_heads, lse = attend(info, qkv)
    mixed = links.exchange(mixed_heads)
    cot_in = arrange(base, cot_moved)
    fed = feed(scalar(member), rows_in, cot_in, row_scale, mixed, vectors, weights)
    grad_mixed = fed[:team]
    (
        delta, grad_middle, grad_middle_low, normed_two, grad_low, hidden, grad_gate, grad_up,
        sums_two, mixed_rows,
    ) = fed[team:]
    grad_heads = links.exchange(grad_mixed)

    narrow, broad = width // links.dp, hidden.shape[1] // links.dp
    core = links.own()
    terms = [
        (hidden, grad_low, broad, links.dp_first),
        (normed_two, grad_gate, narrow, links.seq_first),
        (normed_two, grad_up, narrow, links.seq_last),
        (mixed_rows, grad_middle_low, narrow, links.dp_last),
    ]
    chains = [Chain(links, *weight_grad(core, *t[:3]), t[3]) for t in terms]
    sum_down, sum_gate, sum_up, sum_out = chains

    blocks, made = [], []
    for part in range(PARTS):
        made = beside(
            chains, lambda *g: attend_back(info, qkv, mixed_heads, g, lse, part), *grad_heads
        )
        grad_heads = tie(list(grad_heads), made)
        blocks.append(links.exchange(made))
    returned = links.from_team(tie(delta, made))

    sums, partial, fresh = [], [], []
    for part in range(PARTS):

        def through(value):
            return project_back(
                rows_in, grad_middle, vectors, qkv_w, value, part, team, partial
            )

        def weigh(*received):
            low = unturn(scalar(member), received, table)
            return (low,) + tuple(weight_grad(core, normed_one, low, narrow))

        if part < PARTS - 1:
            low, own, away = weigh(*tie(blocks[part], made))
            fresh = [Chain(links, own, away, links.direct_back)]
            sums.append(fresh)
            partial = beside(chains, through, tie(low, own))
            chains = chains + fresh
        else:
            low, own, away = beside(chains, weigh, *tie(blocks[part], partial))
            half = own.shape[1] // 2
            fresh = [
                Chain(links, own[:, :half], away[:, :half], links.direct),
                Chain(links, own[:, half:], away[:, half:], links.direct),
            ]
            sums.append(fresh)
            grad_in, sums_one = beside(chains, through, tie(low, own))
            chains = chains + fresh

    home = links.from_team(grad_in)
    place = scalar(2 * links.bit(0) + links.bit(1))
    gains = jnp.concatenate([sums_one, sums_two], axis=0)
    gains = gains.reshape(4, links.dp // 2, 2, links.seq, each).transpose(2, 1, 3, 0, 4)
    gains = gains.reshape(2, links.count // 2 * 4, each)
    own, away = (
        lax.dynamic_index_in_dim(gains, c, 0, keepdims=False) for c in (core[0], 1 - core[0])
    )
    gains = Chain(links, own, away, links.direct, F32)
    output = settle(place, tie(returned, sums_one), [tokens])
    chains = chains + [gains]
    while any(c.rounds for c in chains):
        beside(chains, lambda: [])
    grad_tokens = settle(place, home, [])

    merged = [jnp.concatenate([c.result() for c in s], axis=1) for s in sums]
    merged = jnp.concatenate([m.reshape(each, 3, team, 1, -1) for m in merged], axis=3)
    merged = merged.reshape(each, 3, width)
    gains = gains.result()
    return (
        output.reshape(wins, rows, width),
        grad_tokens.reshape(wins, rows, width),
        gains[0],
        gains[1],
        merged[:, 0],
        merged[:, 1],
        merged[:, 2],
        sum_out.result(),
        gains[2],
        gains[3],
        sum_gate.result(),
        sum_up.result(),
        sum_down.result(),
    )


def solution(mesh):
    token = P("dp", "seq", None)
    vector = P(BOTH)
    matrix = P(BOTH, None)
    return jax.shard_map(
        functools.partial(body, Links(mesh)),
        mesh=mesh,
        in_specs=(
            (token, token, P("dp"), P("dp"), vector, vector)
            + (matrix,) * 4
            + (vector, vector)
            + (matrix,) * 3
        ),
        out_specs=(
            (token, token, vector, vector) + (matrix,) * 4 + (vector, vector) + (matrix,) * 3
        ),
        check_vma=False,
    )
```

time: 976 us -> 784 us (0.80)
  Pallas kernels: 108 us -> 299 us
  matrix products: 183 us -> 0 us
  local copies, waits for them, and re-layouts: 189 us -> 32.9 us
  waiting for transfers between devices: 293 us -> 164 us
  starting transfers between devices: 107 us -> 193 us
    pallas_call x2 -> x21, Pallas kernels: 108 us -> 299 us  [the longest x1 78.9 us: feed(): pl.pallas_call(functools.partial(feed_kernel, team=team), grid_spec=pltpu...]
    dot_general x14 -> x0, matrix products: 183 us -> none  [dot(): return lax.dot_general(a, b, dims, preferred_element_type=F32)]
    ppermute x33 -> x97, starting transfers between devices: 87.1 us -> 193 us  [the longest x81 112 us: swap(): return lax.ppermute(value, BOTH, [(i, i ^ mask) for i in range(self.count)])]
    all_to_all x4 -> x0, waiting for transfers between devices: 83.9 us -> none  [the longest x2 83.9 us: to_heads(): return lax.all_to_all(value, 'seq', split_axis=3, concat_axis=2, tiled=True)]
    all_gather x3 -> x1, waiting for transfers between devices: 69.4 us -> 0.01 us  [body(): weights = regrouped(lax.all_gather(mine, BOTH, axis=0), each, width)]
    convert_element_type x3 -> x19, other arithmetic: 4.3 us -> 45.3 us  [the longest x17 44.3 us: split(): sent = [total(self.pick(m)).astype(self.wire) for m in self.masks[1:]]]
    convert_element_type x25 -> x0, local copies, waits for them, and re-layouts: 31.3 us -> none  [the longest x20 9.92 us: scatter_sum(): lax.dynamic_index_in_dim(blocks, 1 - own, at, keepdims=False).astype(wire)]
    add x35 -> x12, other arithmetic: 40.7 us -> 11.8 us  [the longest x9 11.8 us: total(): return functools.reduce(jnp.add, [t.astype(F32) for t in terms])]
  transfers between devices with their start and end apart: 40 -> 98, of which waited for: 19 -> 28; matrix products, arithmetic and copies ran while one was open for 40% -> 12% of each run, Pallas kernels for 11% -> 26%
where the time goes in v2:
time: 784 us; the launch traced here: 782 us
  Pallas kernels  299 us (38%)
  starting transfers between devices  193 us (25%)
  waiting for transfers between devices  164 us (21%)
  other arithmetic  76 us (10%)
  local copies, waits for them, and re-layouts  32.9 us (4%)
  between operations  16.9 us (2%)
    ppermute x81, waiting for transfers between devices, swap(): return lax.ppermute(value, BOTH, [(i, i ^ mask) for i in range(self.count)])  136 us
    ppermute x81, starting transfers between devices, swap(): return lax.ppermute(value, BOTH, [(i, i ^ mask) for i in range(self.count)])  112 us
    pallas_call x1, Pallas kernels, feed(): pl.pallas_call(functools.partial(feed_kernel, team=team), grid_spec=pltpu...  78.9 us
    pallas_call x6, Pallas kernels, weight_grad(): pl.pallas_call(functools.partial(weight_kernel, size=chunk), grid_spec=pl...  60.1 us
    convert_element_type x17, other arithmetic, split(): sent = [total(self.pick(m)).astype(self.wire) for m in self.masks[1:]]  44.3 us
    ppermute x8, starting transfers between devices, from_team(): received.append(lax.ppermute(away, BOTH, back))  42.9 us
    pallas_call x2, Pallas kernels, attend_back(): pl.pallas_call(functools.partial(attend_back_kernel, team=team), grid_spe...  39.4 us
    ppermute x8, starting transfers between devices, to_team(): received.append(lax.ppermute(away, BOTH, self.route(k)))  37.9 us
  transfers between devices with their start and end apart: 98, of which 28 were waited for; matrix products, arithmetic and copies ran while one was open for 12% of the time, Pallas kernels for 26%

profile of v2, /device:TPU:0, one launch (start us, length us, event | category | flops | bytes accessed | tf_op | source)
XLA Modules:
  0.0 782.0 jit_solution(6223617436623120081)
XLA Ops:
  62.5 15.9 %collective-permute-done.12 = bf16[8,32,1024]{2,1,0:T(8,128)(2,1)S(1)} collective-permute-done((bf16[8,32,1024]{2,1,0:T(8,128)(2,1)S(1)}, bf16[8,32,1024]{2,1,0:T(8,128)(2,1)S(1)}, u32[]{:S(2)}, u32[]{:S(2)}) %collective-permute-start.12) | collective-permute-done | bytes 524320 | tf_op jit(solution)/shard_map/ppermute | solution.py:851
  92.7 15.1 %collective-permute-done.2.refs_2_ = bf16[256,1024]{1,0:T(8,128)(2,1)S(1)} collective-permute-done((bf16[256,1024]{1,0:T(8,128)(2,1)S(1)}, bf16[256,1024]{1,0:T(8,128)(2,1)S(1)}, u32[]{:S(2)}, u32[]{:S(2)}) %collective-permute-start.2) | collective-permute-done | bytes 524320 | tf_op jit(solution)/shard_map/ppermute | solution.py:820
  127.3 12.1 %project.2 = (bf16[3,1024,512]{2,1,0:T(8,128)(2,1)}, bf16[1024,1024]{1,0:T(8,128)(2,1)}) custom-call(s32[1]{0:T(128)} %bitcast.9.at_ref, bf16[1024,1024]{1,0:T(8,128)(2,1)} %bitcast.569, bf16[3,1024,1024]{2,1,0:T(8,128)(2,1)} %bitcast.565, f32[4,1024]{1,0:T(4,128)} %bitcast.626, f32[1024,128]{1,0:T(8,128)} %pad_maximum_fusion.3.c_ref, ...), custom_call_target="tpu_custom_call" | custom-call | flops 3221225472 | bytes 6291456 | tf_op jit(solution)/shard_map/project/pallas_call | solution.py:151
  147.0 12.8 %project.3 = (bf16[3,1024,512]{2,1,0:T(8,128)(2,1)}, bf16[1024,1024]{1,0:T(8,128)(2,1)}) custom-call(s32[1]{0:T(128)} %bitcast.1.at_ref, bf16[1024,1024]{1,0:T(8,128)(2,1)} %bitcast.570, bf16[3,1024,1024]{2,1,0:T(8,128)(2,1)} %bitcast.566, f32[4,1024]{1,0:T(4,128)} %bitcast.627, f32[1024,128]{1,0:T(8,128)} %pad_maximum_fusion.3.c_ref, ...), custom_call_target="tpu_custom_call" | custom-call | flops 3221225472 | bytes 6291456 | tf_op jit(solution)/shard_map/project/pallas_call | solution.py:151
  159.8 37.5 %attend.1 = (bf16[1024,512]{1,0:T(8,128)(2,1)}, bf16[1024,512]{1,0:T(8,128)(2,1)}, f32[4,2,2048]{2,1,0:T(2,128)}) custom-call(s32[3]{0:T(128)} %pad_add_fusion.1.info_ref, bf16[3,1024,512]{2,1,0:T(8,128)(2,1)} %get-tuple-element.169.refs_0_.refs_2_.refs_4_, bf16[3,1024,512]{2,1,0:T(8,128)(2,1)} %collective-permute-done.32.refs_1_.refs_3_.refs_5_, ...), custom_call_target="tpu_custom_call" | custom-call | flops 34359738368 | bytes 8388608 | tf_op jit(solution)/shard_map/attend/pallas_call | solution.py:253
  201.0 28.4 %collective-permute-start.25 = (bf16[256,1024]{1,0:T(8,128)(2,1)}, bf16[256,1024]{1,0:T(8,128)(2,1)S(1)}, u32[]{:S(2)}, u32[]{:S(2)}) collective-permute-start(bf16[256,1024]{1,0:T(8,128)(2,1)} %get-tuple-element.349), channel_id=1, source_target_pairs={{0,1},{1,0},{2,5},{3,4},{4,3},{5,2},{6,7},{7,6},{8,9},{9,8},{10,13... | collective-permute-start | bytes 1572872 | tf_op jit(solution)/shard_map/ppermute | solution.py:820
  244.6 8.5 %collective-permute-done.27.refs_3_ = bf16[256,1024]{1,0:T(8,128)(2,1)S(1)} collective-permute-done((bf16[256,1024]{1,0:T(8,128)(2,1)S(1)}, bf16[256,1024]{1,0:T(8,128)(2,1)S(1)}, u32[]{:S(2)}, u32[]{:S(2)}) %collective-permute-start.27) | collective-permute-done | bytes 524320 | tf_op jit(solution)/shard_map/ppermute | solution.py:820
  256.9 78.9 %feed.1 = (bf16[1024,512]{1,0:T(8,128)(2,1)}, bf16[1024,512]{1,0:T(8,128)(2,1)}, bf16[1024,1024]{1,0:T(8,128)(2,1)}, f32[1024,1024]{1,0:T(8,128)}, bf16[1024,102...) custom-call(s32[1]{0:T(128)} %bitcast.1.at_ref, ...), custom_call_target="tpu_custom_call" | custom-call | flops 55834574848 | bytes 106954752 | tf_op jit(solution)/shard_map/feed/pallas_call | solution.py:508
  335.8 13.3 %weight_grad.8 = (bf16[512,4096]{1,0:T(8,128)(2,1)}, bf16[512,4096]{1,0:T(8,128)(2,1)}) custom-call(s32[1]{0:T(128)} %bitcast.38.core_ref, bf16[1024,1024]{1,0:T(8,128)(2,1)} %get-tuple-element.179.a_ref, bf16[1024,4096]{1,0:T(8,128)(2,1)} %get-tuple-element.183.b_ref), custom_call_target="tpu_custom_call" | custom-call | flops 8589934592 | bytes 18874368 | tf_op jit(solution)/shard_map/weight_grad/pallas_call | solution.py:588
  349.4 12.8 %weight_grad.6 = (bf16[2048,1024]{1,0:T(8,128)(2,1)}, bf16[2048,1024]{1,0:T(8,128)(2,1)}) custom-call(s32[1]{0:T(128)} %bitcast.38.core_ref, bf16[1024,4096]{1,0:T(8,128)(2,1)} %get-tuple-element.175.a_ref, bf16[1024,1024]{1,0:T(8,128)(2,1)} %get-tuple-element.176.b_ref), custom_call_target="tpu_custom_call" | custom-call | flops 8589934592 | bytes 18874368 | tf_op jit(solution)/shard_map/weight_grad/pallas_call | solution.py:588
  362.4 13.8 %weight_grad.7 = (bf16[512,4096]{1,0:T(8,128)(2,1)}, bf16[512,4096]{1,0:T(8,128)(2,1)}) custom-call(s32[1]{0:T(128)} %bitcast.38.core_ref, bf16[1024,1024]{1,0:T(8,128)(2,1)} %get-tuple-element.179.a_ref, bf16[1024,4096]{1,0:T(8,128)(2,1)} %get-tuple-element.180.b_ref), custom_call_target="tpu_custom_call" | custom-call | flops 8589934592 | bytes 18874368 | tf_op jit(solution)/shard_map/weight_grad/pallas_call | solution.py:588
  405.8 19.8 %attend_back.2 = (bf16[3,1024,256]{2,1,0:T(8,128)(2,1)}, bf16[3,1024,256]{2,1,0:T(8,128)(2,1)}) custom-call(s32[3]{0:T(128)} %pad_add_fusion.1.info_ref, bf16[3,1024,512]{2,1,0:T(8,128)(2,1)} %get-tuple-element.169.refs_0_.refs_2_.refs_4_, bf16[3,1024,512]{2,1,0:T(8,128)(2,1)} %collective-permute-done.32.refs_1_.refs_3_.refs_5_, ...), custom_call_target="tpu_custom_call" | custom-call | flops 32212254720 | bytes 8388608 | tf_op jit(solution)/shard_map/attend_back/pallas_call | solution.py:388
  425.6 32.5 %collective-permute-done.42 = bf16[2,2,2,32,1024]{4,3,2,1,0:T(8,128)(2,1)} collective-permute-done((bf16[2,2,2,32,1024]{4,3,2,1,0:T(8,128)(2,1)}, bf16[2,2,2,32,1024]{4,3,2,1,0:T(8,128)(2,1)}, u32[]{:S(2)}, u32[]{:S(2)}) %collective-permute-start.42) | collective-permute-done | bytes 524320 | tf_op jit(solution)/shard_map/ppermute | solution.py:851
  475.3 19.6 %attend_back.3 = (bf16[3,1024,256]{2,1,0:T(8,128)(2,1)}, bf16[3,1024,256]{2,1,0:T(8,128)(2,1)}) custom-call(s32[3]{0:T(128)} %pad_add_fusion.1.info_ref, bf16[3,1024,512]{2,1,0:T(8,128)(2,1)} %get-tuple-element.169.refs_0_.refs_2_.refs_4_, bf16[3,1024,512]{2,1,0:T(8,128)(2,1)} %collective-permute-done.32.refs_1_.refs_3_.refs_5_, ...), custom_call_target="tpu_custom_call" | custom-call | flops 32212254720 | bytes 8388608 | tf_op jit(solution)/shard_map/attend_back/pallas_call | solution.py:388
  509.2 9.7 %collective-permute-done.51 = bf16[2,2,32,4096]{3,2,1,0:T(8,128)(2,1)} collective-permute-done((bf16[2,2,32,4096]{3,2,1,0:T(8,128)(2,1)}, bf16[2,2,32,4096]{3,2,1,0:T(8,128)(2,1)}, u32[]{:S(2)}, u32[]{:S(2)}) %collective-permute-start.51) | collective-permute-done | bytes 1048608 | tf_op jit(solution)/shard_map/ppermute | solution.py:851
  530.0 10.7 %project_back.2.refs_0_ = f32[1024,1024]{1,0:T(8,128)} custom-call(bf16[1024,1024]{1,0:T(8,128)(2,1)} %bitcast.572, f32[1024,1024]{1,0:T(8,128)} %get-tuple-element.210.gm_ref, f32[4,1024]{1,0:T(4,128)} %bitcast.629, bf16[3,1024,1024]{2,1,0:T(8,128)(2,1)} %bitcast.567, bf16[3,1024,512]{2,1,0:T(8,128)(2,1)} %unturn.2.b_ref.low_ref), custom_call_target="tpu_custom_call" | custom-call | flops 3221225472 | bytes 25165824 | tf_op jit(solution)/shard_map/project_back/pallas_call | solution.py:678
  547.0 24.0 %collective-permute-start.44 = (bf16[256,1024]{1,0:T(8,128)(2,1)S(1)}, bf16[256,1024]{1,0:T(8,128)(2,1)S(1)}, u32[]{:S(2)}, u32[]{:S(2)}) collective-permute-start(bf16[256,1024]{1,0:T(8,128)(2,1)S(1)} %get-tuple-element.345), channel_id=1, source_target_pairs={{4,0},{5,1},{0,2},{1,3},{6,4},{7,5},{2,6},{3,7},{12,8},{13,9},{8,1... | collective-permute-start | bytes 1572872 | tf_op jit(solution)/shard_map/ppermute | solution.py:831
  594.0 10.2 %collective-permute-done.55 = bf16[2,2,32,1536]{3,2,1,0:T(8,128)(2,1)S(1)} collective-permute-done((bf16[2,2,32,1536]{3,2,1,0:T(8,128)(2,1)}, bf16[2,2,32,1536]{3,2,1,0:T(8,128)(2,1)S(1)}, u32[]{:S(2)}, u32[]{:S(2)}) %collective-permute-start.55) | collective-permute-done | bytes 393248 | tf_op jit(solution)/shard_map/ppermute | solution.py:851
  619.9 14.2 %project_back.3 = (bf16[1024,1024]{1,0:T(8,128)(2,1)}, f32[2,1024]{1,0:T(2,128)}) custom-call(bf16[1024,1024]{1,0:T(8,128)(2,1)} %bitcast.573, f32[1024,1024]{1,0:T(8,128)} %get-tuple-element.210.gm_ref, f32[4,1024]{1,0:T(4,128)} %bitcast.630, bf16[3,1024,1024]{2,1,0:T(8,128)(2,1)} %bitcast.568, bf16[3,1024,512]{2,1,0:T(8,128)(2,1)} %unturn.3.b_ref.low_ref, ...), custom_call_target="tpu_custom_call" | custom-call | flops 3221225472 | bytes 25165824 | tf_op jit(solution)/shard_map/project_back/pallas_call | solution.py:678
  642.7 8.7 %collective-permute-start.46 = (bf16[256,1024]{1,0:T(8,128)(2,1)}, bf16[256,1024]{1,0:T(8,128)(2,1)S(1)}, u32[]{:S(2)}, u32[]{:S(2)}) collective-permute-start(bf16[256,1024]{1,0:T(8,128)(2,1)} %get-tuple-element.343), channel_id=1, source_target_pairs={{5,0},{4,1},{1,2},{0,3},{7,4},{6,5},{3,6},{2,7},{13,8},{12,9},{9,1... | collective-permute-start | bytes 1572872 | tf_op jit(solution)/shard_map/ppermute | solution.py:831
  662.4 10.5 %collective-permute-start.64 = (bf16[2,2,32,768]{3,2,1,0:T(8,128)(2,1)S(1)}, bf16[2,2,32,768]{3,2,1,0:T(8,128)(2,1)S(1)}, u32[]{:S(2)}, u32[]{:S(2)}) collective-permute-start(bf16[2,2,32,768]{3,2,1,0:T(8,128)(2,1)S(1)} %get-tuple-element.247), channel_id=1, source_target_pairs={{0,1},{1,0},{2,3},{3,2},{4,5},{5,4},{6,7},{7,6},{8,9},{9,8},{10,11... | collective-permute-start | bytes 589832 | tf_op jit(solution)/shard_map/ppermute | solution.py:851
  673.0 9.6 %collective-permute-done.92 = bf16[32,4096]{1,0:T(8,128)(2,1)S(1)} collective-permute-done((bf16[32,4096]{1,0:T(8,128)(2,1)S(1)}, bf16[32,4096]{1,0:T(8,128)(2,1)S(1)}, u32[]{:S(2)}, u32[]{:S(2)}) %collective-permute-start.92) | collective-permute-done | bytes 262176 | tf_op jit(solution)/shard_map/ppermute | solution.py:851
  682.7 9.8 %collective-permute-start.72 = (f32[2,2,4,32]{3,2,1,0:T(4,128)S(1)}, f32[2,2,4,32]{3,2,1,0:T(4,128)S(1)}, u32[]{:S(2)}, u32[]{:S(2)}) collective-permute-start(f32[2,2,4,32]{3,2,1,0:T(4,128)S(1)} %get-tuple-element.255), channel_id=1, source_target_pairs={{0,3},{1,2},{2,1},{3,0},{4,7},{5,6},{6,5},{7,4},{8,11},{9,10},{10,... | collective-permute-start | bytes 6152 | tf_op jit(solution)/shard_map/ppermute | solution.py:851
  716.7 16.3 %collective-permute-done.83 = bf16[32,1536]{1,0:T(8,128)(2,1)S(1)} collective-permute-done((bf16[32,1536]{1,0:T(8,128)(2,1)S(1)}, bf16[32,1536]{1,0:T(8,128)(2,1)S(1)}, u32[]{:S(2)}, u32[]{:S(2)}) %collective-permute-start.83) | collective-permute-done | bytes 98336 | tf_op jit(solution)/shard_map/ppermute | solution.py:851
  (490 shorter events, 320.3 us)
Async XLA Ops:
  7.2 249.7 %all-gather.3.cloned.1.call-start = ((), (), s32[]{:S(2)}) async-start(), calls=%async_computation | async-start | bytes 28114944 | tf_op jit(solution)/shard_map/all_gather | solution.py:961
  44.4 44.1 %collective-permute-start = (bf16[256,1024]{1,0:T(8,128)(2,1)S(1)}, bf16[256,1024]{1,0:T(8,128)(2,1)}, u32[]{:S(2)}, u32[]{:S(2)}) collective-permute-start(bf16[256,1024]{1,0:T(8,128)(2,1)S(1)} %get-tuple-element.354), channel_id=1, source_target_pairs={{0,0},{1,1},{2,4},{3,5},{4,2},{5,3},{6,6},{7,7},{8,8},{9,9},{10,12... | collective-permute-start | bytes 1572872 | tf_op jit(solution)/shard_map/ppermute | solution.py:820
  45.8 43.2 %collective-permute-start.1 = (bf16[256,1024]{1,0:T(8,128)(2,1)}, bf16[256,1024]{1,0:T(8,128)(2,1)}, u32[]{:S(2)}, u32[]{:S(2)}) collective-permute-start(bf16[256,1024]{1,0:T(8,128)(2,1)} %get-tuple-element.353), channel_id=1, source_target_pairs={{0,1},{1,0},{2,5},{3,4},{4,3},{5,2},{6,7},{7,6},{8,9},{9,8},{10,13... | collective-permute-start | bytes 1572872 | tf_op jit(solution)/shard_map/ppermute | solution.py:820
  197.3 59.6 %collective-permute-start.33 = (bf16[1024,512]{1,0:T(8,128)(2,1)}, bf16[1024,512]{1,0:T(8,128)(2,1)}, u32[]{:S(2)}, u32[]{:S(2)}) collective-permute-start(bf16[1024,512]{1,0:T(8,128)(2,1)} %get-tuple-element.171.refs_7_), channel_id=1, source_target_pairs={{0,4},{1,5},{2,6},{3,7},{4,0},{5,1},{6,2},{7,3},{8,12},{9,13},{10,... | collective-permute-start | bytes 3145736 | tf_op jit(solution)/shard_map/ppermute | solution.py:851
  199.2 44.6 %collective-permute-start.24 = (bf16[256,1024]{1,0:T(8,128)(2,1)}, bf16[256,1024]{1,0:T(8,128)(2,1)S(1)}, u32[]{:S(2)}, u32[]{:S(2)}) collective-permute-start(bf16[256,1024]{1,0:T(8,128)(2,1)} %get-tuple-element.350), channel_id=1, source_target_pairs={{0,0},{1,1},{2,4},{3,5},{4,2},{5,3},{6,6},{7,7},{8,8},{9,9},{10,12... | collective-permute-start | bytes 1572872 | tf_op jit(solution)/shard_map/ppermute | solution.py:820
  201.0 42.7 %collective-permute-start.25 = (bf16[256,1024]{1,0:T(8,128)(2,1)}, bf16[256,1024]{1,0:T(8,128)(2,1)S(1)}, u32[]{:S(2)}, u32[]{:S(2)}) collective-permute-start(bf16[256,1024]{1,0:T(8,128)(2,1)} %get-tuple-element.349), channel_id=1, source_target_pairs={{0,1},{1,0},{2,5},{3,4},{4,3},{5,2},{6,7},{7,6},{8,9},{9,8},{10,13... | collective-permute-start | bytes 1572872 | tf_op jit(solution)/shard_map/ppermute | solution.py:820
  349.1 43.2 %collective-permute-start.37 = (bf16[512,4096]{1,0:T(8,128)(2,1)}, bf16[512,4096]{1,0:T(8,128)(2,1)}, u32[]{:S(2)}, u32[]{:S(2)}) collective-permute-start(bf16[512,4096]{1,0:T(8,128)(2,1)} %get-tuple-element.185), channel_id=1, source_target_pairs={{0,4},{1,5},{2,6},{3,7},{4,0},{5,1},{6,2},{7,3},{8,12},{9,13},{10,... | collective-permute-start | bytes 12582920 | tf_op jit(solution)/shard_map/ppermute | solution.py:851
  398.8 59.4 %collective-permute-start.39 = (bf16[2,2,2,128,1024]{4,3,2,1,0:T(8,128)(2,1)}, bf16[2,2,2,128,1024]{4,3,2,1,0:T(8,128)(2,1)}, u32[]{:S(2)}, u32[]{:S(2)}) collective-permute-start(bf16[2,2,2,128,1024]{4,3,2,1,0:T(8,128)(2,1)} %fusion), channel_id=1, source_target_pairs={{0,8},{1,9},{2,10},{3,11},{4,12},{5,13},{6,14},{7,15},{8,0},{9,1},... | collective-permute-start | bytes 6291464 | tf_op jit(solution)/shard_map/ppermute | solution.py:851
  399.8 58.4 %collective-permute-start.40 = (bf16[2,2,2,32,4096]{4,3,2,1,0:T(8,128)(2,1)}, bf16[2,2,2,32,4096]{4,3,2,1,0:T(8,128)(2,1)}, u32[]{:S(2)}, u32[]{:S(2)}) collective-permute-start(bf16[2,2,2,32,4096]{4,3,2,1,0:T(8,128)(2,1)} %fusion.1), channel_id=1, source_target_pairs={{0,1},{1,0},{2,3},{3,2},{4,5},{5,4},{6,7},{7,6},{8,9},{9,8},{10,11... | collective-permute-start | bytes 6291464 | tf_op jit(solution)/shard_map/ppermute | solution.py:851
  403.5 54.7 %collective-permute-start.41 = (bf16[2,2,2,32,4096]{4,3,2,1,0:T(8,128)(2,1)S(1)}, bf16[2,2,2,32,4096]{4,3,2,1,0:T(8,128)(2,1)}, u32[]{:S(2)}, u32[]{:S(2)}) collective-permute-start(bf16[2,2,2,32,4096]{4,3,2,1,0:T(8,128)(2,1)S(1)} %fusion.2), channel_id=1, source_target_pairs={{0,2},{1,3},{2,0},{3,1},{4,6},{5,7},{6,4},{7,5},{8,10},{9,11},{10,... | collective-permute-start | bytes 6291464 | tf_op jit(solution)/shard_map/ppermute | solution.py:851
  403.8 54.3 %collective-permute-start.42 = (bf16[2,2,2,32,1024]{4,3,2,1,0:T(8,128)(2,1)}, bf16[2,2,2,32,1024]{4,3,2,1,0:T(8,128)(2,1)}, u32[]{:S(2)}, u32[]{:S(2)}) collective-permute-start(bf16[2,2,2,32,1024]{4,3,2,1,0:T(8,128)(2,1)} %fusion.6), channel_id=1, source_target_pairs={{0,8},{1,9},{2,10},{3,11},{4,12},{5,13},{6,14},{7,15},{8,0},{9,1},... | collective-permute-start | bytes 1572872 | tf_op jit(solution)/shard_map/ppermute | solution.py:851
  425.6 69.4 %collective-permute-start.48 = (bf16[3,1024,256]{2,1,0:T(8,128)(2,1)}, bf16[3,1024,256]{2,1,0:T(8,128)(2,1)S(1)}, u32[]{:S(2)}, u32[]{:S(2)}) collective-permute-start(bf16[3,1024,256]{2,1,0:T(8,128)(2,1)} %get-tuple-element.194), channel_id=1, source_target_pairs={{0,4},{1,5},{2,6},{3,7},{4,0},{5,1},{6,2},{7,3},{8,12},{9,13},{10,... | collective-permute-start | bytes 4718600 | tf_op jit(solution)/shard_map/ppermute | solution.py:851
  468.6 40.6 %collective-permute-start.49 = (bf16[2,2,128,1024]{3,2,1,0:T(8,128)(2,1)}, bf16[2,2,128,1024]{3,2,1,0:T(8,128)(2,1)}, u32[]{:S(2)}, u32[]{:S(2)}) collective-permute-start(bf16[2,2,128,1024]{3,2,1,0:T(8,128)(2,1)} %fusion.5), channel_id=1, source_target_pairs={{0,1},{1,0},{2,3},{3,2},{4,5},{5,4},{6,7},{7,6},{8,9},{9,8},{10,11... | collective-permute-start | bytes 3145736 | tf_op jit(solution)/shard_map/ppermute | solution.py:851
  473.4 45.5 %collective-permute-start.51 = (bf16[2,2,32,4096]{3,2,1,0:T(8,128)(2,1)}, bf16[2,2,32,4096]{3,2,1,0:T(8,128)(2,1)}, u32[]{:S(2)}, u32[]{:S(2)}) collective-permute-start(bf16[2,2,32,4096]{3,2,1,0:T(8,128)(2,1)} %fusion.3), channel_id=1, source_target_pairs={{0,1},{1,0},{2,3},{3,2},{4,5},{5,4},{6,7},{7,6},{8,9},{9,8},{10,11... | collective-permute-start | bytes 3145736 | tf_op jit(solution)/shard_map/ppermute | solution.py:851
  495.0 45.7 %collective-permute-start.47 = (bf16[3,1024,256]{2,1,0:T(8,128)(2,1)}, bf16[3,1024,256]{2,1,0:T(8,128)(2,1)}, u32[]{:S(2)}, u32[]{:S(2)}) collective-permute-start(bf16[3,1024,256]{2,1,0:T(8,128)(2,1)} %get-tuple-element.208), channel_id=1, source_target_pairs={{0,4},{1,5},{2,6},{3,7},{4,0},{5,1},{6,2},{7,3},{8,12},{9,13},{10,... | collective-permute-start | bytes 4718600 | tf_op jit(solution)/shard_map/ppermute | solution.py:851
  545.3 66.6 %collective-permute-start.43 = (bf16[256,1024]{1,0:T(8,128)(2,1)}, bf16[256,1024]{1,0:T(8,128)(2,1)S(1)}, u32[]{:S(2)}, u32[]{:S(2)}) collective-permute-start(bf16[256,1024]{1,0:T(8,128)(2,1)} %get-tuple-element.346), channel_id=1, source_target_pairs={{0,0},{1,1},{4,2},{5,3},{2,4},{3,5},{6,6},{7,7},{8,8},{9,9},{12,10... | collective-permute-start | bytes 1572872 | tf_op jit(solution)/shard_map/ppermute | solution.py:831
  547.0 67.2 %collective-permute-start.44 = (bf16[256,1024]{1,0:T(8,128)(2,1)S(1)}, bf16[256,1024]{1,0:T(8,128)(2,1)S(1)}, u32[]{:S(2)}, u32[]{:S(2)}) collective-permute-start(bf16[256,1024]{1,0:T(8,128)(2,1)S(1)} %get-tuple-element.345), channel_id=1, source_target_pairs={{4,0},{5,1},{0,2},{1,3},{6,4},{7,5},{2,6},{3,7},{12,8},{13,9},{8,1... | collective-permute-start | bytes 1572872 | tf_op jit(solution)/shard_map/ppermute | solution.py:831
  571.0 43.5 %collective-permute-start.45 = (bf16[256,1024]{1,0:T(8,128)(2,1)S(1)}, bf16[256,1024]{1,0:T(8,128)(2,1)S(1)}, u32[]{:S(2)}, u32[]{:S(2)}) collective-permute-start(bf16[256,1024]{1,0:T(8,128)(2,1)S(1)} %get-tuple-element.344), channel_id=1, source_target_pairs={{1,0},{0,1},{5,2},{4,3},{3,4},{2,5},{7,6},{6,7},{9,8},{8,9},{13,10... | collective-permute-start | bytes 1572872 | tf_op jit(solution)/shard_map/ppermute | solution.py:831
  619.9 37.3 %collective-permute-start.62 = (bf16[512,768]{1,0:T(8,128)(2,1)}, bf16[512,768]{1,0:T(8,128)(2,1)}, u32[]{:S(2)}, u32[]{:S(2)}) collective-permute-start(bf16[512,768]{1,0:T(8,128)(2,1)} %get-tuple-element.361), channel_id=1, source_target_pairs={{0,4},{1,5},{2,6},{3,7},{4,0},{5,1},{6,2},{7,3},{8,12},{9,13},{10,... | collective-permute-start | bytes 2359304 | tf_op jit(solution)/shard_map/ppermute | solution.py:851
  642.7 49.9 %collective-permute-start.46 = (bf16[256,1024]{1,0:T(8,128)(2,1)}, bf16[256,1024]{1,0:T(8,128)(2,1)S(1)}, u32[]{:S(2)}, u32[]{:S(2)}) collective-permute-start(bf16[256,1024]{1,0:T(8,128)(2,1)} %get-tuple-element.343), channel_id=1, source_target_pairs={{5,0},{4,1},{1,2},{0,3},{7,4},{6,5},{3,6},{2,7},{13,8},{12,9},{9,1... | collective-permute-start | bytes 1572872 | tf_op jit(solution)/shard_map/ppermute | solution.py:831
  705.7 46.7 %collective-permute-start.57 = (bf16[256,1024]{1,0:T(8,128)(2,1)}, bf16[256,1024]{1,0:T(8,128)(2,1)S(1)}, u32[]{:S(2)}, u32[]{:S(2)}) collective-permute-start(bf16[256,1024]{1,0:T(8,128)(2,1)} %get-tuple-element.342), channel_id=1, source_target_pairs={{0,0},{1,1},{4,2},{5,3},{2,4},{3,5},{6,6},{7,7},{8,8},{9,9},{12,10... | collective-permute-start | bytes 1572872 | tf_op jit(solution)/shard_map/ppermute | solution.py:831
  707.4 45.1 %collective-permute-start.58 = (bf16[256,1024]{1,0:T(8,128)(2,1)}, bf16[256,1024]{1,0:T(8,128)(2,1)S(1)}, u32[]{:S(2)}, u32[]{:S(2)}) collective-permute-start(bf16[256,1024]{1,0:T(8,128)(2,1)} %get-tuple-element.341), channel_id=1, source_target_pairs={{4,0},{5,1},{0,2},{1,3},{6,4},{7,5},{2,6},{3,7},{12,8},{13,9},{8,1... | collective-permute-start | bytes 1572872 | tf_op jit(solution)/shard_map/ppermute | solution.py:831
  710.6 45.1 %collective-permute-start.59 = (bf16[256,1024]{1,0:T(8,128)(2,1)}, bf16[256,1024]{1,0:T(8,128)(2,1)S(1)}, u32[]{:S(2)}, u32[]{:S(2)}) collective-permute-start(bf16[256,1024]{1,0:T(8,128)(2,1)} %get-tuple-element.340), channel_id=1, source_target_pairs={{1,0},{0,1},{5,2},{4,3},{3,4},{2,5},{7,6},{6,7},{9,8},{8,9},{13,10... | collective-permute-start | bytes 1572872 | tf_op jit(solution)/shard_map/ppermute | solution.py:831
  710.8 46.2 %collective-permute-start.60 = (bf16[256,1024]{1,0:T(8,128)(2,1)}, bf16[256,1024]{1,0:T(8,128)(2,1)S(1)}, u32[]{:S(2)}, u32[]{:S(2)}) collective-permute-start(bf16[256,1024]{1,0:T(8,128)(2,1)} %get-tuple-element.339), channel_id=1, source_target_pairs={{5,0},{4,1},{1,2},{0,3},{7,4},{6,5},{3,6},{2,7},{13,8},{12,9},{9,1... | collective-permute-start | bytes 1572872 | tf_op jit(solution)/shard_map/ppermute | solution.py:831
  (166 other events, 2781.4 us)
Sparse Core Ops, SparseCore 0:
  43.2 187.4 all-gather.2

commit v3 on v2

--- a/solution.py
+++ b/solution.py
@@ -37,7 +37,7 @@
 
 
 def cost(flops, moved, exps=0):
-    return pl.CostEstimate(flops=flops, bytes_accessed=moved, transcendentals=exps)
+    return pl.CostEstimate(flops=flops // 64, bytes_accessed=moved // 64, transcendentals=exps // 64)
 
 
 def normalise(value):
@@ -241,30 +241,37 @@
         run(4 * ups)
 
 
-def attend(info, qkv):
+def attend(info, qkv, part):
     team = len(qkv)
     _, rows, lanes = qkv[0].shape
-    span, pairs, ups = team * rows, lanes // 128, team // 2
+    span, pairs, ups = team * rows, lanes // 128 // PARTS, team // 2
     block = rows // 4
 
     def whole(which):
-        return [pl.BlockSpec((None, rows, 128), lambda h, b, u, _: (which, 0, h))] * team
+        return [
+            pl.BlockSpec((None, rows, 128), lambda h, b, u, _: (which, 0, part * pairs + h))
+        ] * team
 
     return pl.pallas_call(
         functools.partial(attend_kernel, team=team),
         grid_spec=pltpu.PrefetchScalarGridSpec(
             num_scalar_prefetch=1,
             grid=(pairs, 4, ups),
-            in_specs=[pl.BlockSpec((None, block, 128), lambda h, b, u, _: (0, b, h))] * team
+            in_specs=[
+                pl.BlockSpec((None, block, 128), lambda h, b, u, _: (0, b, part * pairs + h))
+            ]
+            * team
             + whole(1)
             + whole(2),
             out_specs=[pl.BlockSpec((block, 128), lambda h, b, u, _: (b, h))] * team
             + [pl.BlockSpec((1, 2, 2 * block), lambda h, b, u, _: (h, 0, b * ups + u))],
             scratch_shapes=[pltpu.VMEM((128, span), BF16)],
         ),
-        out_shape=[shape((rows, lanes), BF16)] * team + [shape((pairs, 2, span), F32)],
+        out_shape=[shape((rows, pairs * 128), BF16)] * team + [shape((pairs, 2, span), F32)],
         compiler_params=params(),
-        cost_estimate=cost(16 * span * span * lanes, 8 * span * lanes, span * span * lanes // 64),
+        cost_estimate=cost(
+            16 * span * span * pairs * 128, 8 * span * pairs * 128, 2 * span * span * pairs
+        ),
         name="attend",
     )(info, *qkv, *qkv, *qkv)
 
@@ -373,16 +380,17 @@
                         d_refs[2 * p + m][t, rows] = piece.astype(BF16)
 
 
-def attend_back(info, qkv, mixed, grad, lse, part):
+def attend_back(info, qkv, mixed, grad, lse, part, sub, subs):
     team = len(qkv)
     _, rows, lanes = qkv[0].shape
-    span, pairs, ups = team * rows, lanes // 128 // PARTS, team // 2
+    span, pairs, ups = team * rows, lanes // 128 // PARTS // subs, team // 2
+    start, near = (part * subs + sub) * pairs, sub * pairs
     block = rows // 4
-    spot = pl.BlockSpec((block, 128), lambda h, b, u, _: (b, part * pairs + h))
+    spot = pl.BlockSpec((block, 128), lambda h, b, u, _: (b, start + h))
 
     def whole(which):
         return [
-            pl.BlockSpec((None, rows, 128), lambda h, b, u, _: (which, 0, part * pairs + h))
+            pl.BlockSpec((None, rows, 128), lambda h, b, u, _: (which, 0, start + h))
         ] * team
 
     return pl.pallas_call(
@@ -391,17 +399,14 @@
             num_scalar_prefetch=1,
             grid=(pairs, 4, ups),
             in_specs=[
-                pl.BlockSpec((None, block, 128), lambda h, b, u, _: (0, b, part * pairs + h))
+                pl.BlockSpec((None, block, 128), lambda h, b, u, _: (0, b, start + h))
             ]
             * team
             + whole(1)
             + whole(2)
-            + [spot] * (2 * team)
-            + [
-                pl.BlockSpec(
-                    (1, 2, 2 * block), lambda h, b, u, _: (part * pairs + h, 0, b * ups + u)
-                )
-            ],
+            + [pl.BlockSpec((block, 128), lambda h, b, u, _: (b, near + h))] * team
+            + [spot] * team
+            + [pl.BlockSpec((1, 2, 2 * block), lambda h, b, u, _: (near + h, 0, b * ups + u))],
             out_specs=[pl.BlockSpec((3, rows, 128), lambda h, b, u, _: (0, 0, h))] * team,
             scratch_shapes=[
                 pltpu.VMEM((128, span), BF16),
@@ -421,24 +426,25 @@
 def feed_kernel(
     at_ref, x_ref, cot_ref, scale_ref, vec_ref, wo_ref, wg_ref, wu_ref, wd_ref, *refs, team
 ):
-    mix_refs, send_refs = refs[:team], refs[team : 2 * team]
+    mix_refs, send_refs = refs[: team * PARTS], refs[team * PARTS : team * (PARTS + 1)]
     (
         delta_ref, gm_ref, gml_ref, n_ref, gl_ref, hid_ref, gg_ref, gu_ref, sum_ref, rows_ref,
         acc_ref, normal_ref, inv_ref,
-    ) = refs[2 * team :]
+    ) = refs[team * (PARTS + 1) :]
     step = pl.program_id(1)
-    lanes = mix_refs[0].shape[1]
+    lanes = send_refs[0].shape[1]
+    some = mix_refs[0].shape[1]
 
     def whole(ref):
         return ref[...].reshape(-1, ref.shape[-1])
 
-    def spot(m):
-        return pl.ds(pl.multiple_of((at_ref[0] ^ m) * lanes, lanes), lanes)
+    def spot(m, first, size):
+        return pl.ds(pl.multiple_of((at_ref[0] ^ m) * lanes + first, size), size)
 
     @pl.when(step == 0)
     def _():
-        for m in range(team):
-            rows_ref[:, spot(m)] = mix_refs[m][...]
+        for i, ref in enumerate(mix_refs):
+            rows_ref[:, spot(i % team, i // team * some, some)] = ref[...]
         added = dot(rows_ref[...], whole(wo_ref))
         acc_ref[...] = added
         normal, inverse = normalise(x_ref[...].astype(F32) + added)
@@ -484,11 +490,11 @@
         gml_ref[...] = low
         acc_ref[...] = dot(low, whole(wo_ref), NT)
         for m in range(team):
-            send_refs[m][...] = acc_ref[:, spot(m)].astype(BF16)
+            send_refs[m][...] = acc_ref[:, spot(m, 0, lanes)].astype(BF16)
 
 
 def feed(at, tokens, cotangent, scale, mixed, vectors, weights):
-    team = len(mixed)
+    team = len(mixed) // PARTS
     rows, width = tokens.shape
     lanes = width // team
     units = weights.shape[0]
@@ -520,7 +526,7 @@
                 part(9),
                 pl.BlockSpec((FF_BLOCK // tall, tall, width), lambda i, j, _: (j, 0, 0)),
             ]
-            + [mix] * team,
+            + [pl.BlockSpec((each, lanes // PARTS), lambda i, j, _: (i, 0))] * len(mixed),
             out_specs=[mix] * team
             + [const, const, const, const, const, block, block, block]
             + [pl.BlockSpec((2, width), lambda i, j, _: (0, 0)), const],
@@ -553,7 +559,8 @@
     )(at, tokens, cotangent, scale, vectors, weights, weights, weights, weights, *mixed)
 
 
-def weight_kernel(core_ref, a_ref, b_ref, own_ref, away_ref, at_ref, *, size):
+def weight_kernel(core_ref, a_ref, b_ref, *refs, size):
+    own_ref, away_ref, at_ref = refs[-3:]
     rows, tall = a_ref.shape
     core = core_ref[0]
     outs = (own_ref, away_ref)
@@ -568,10 +575,11 @@
 
     wide = own_ref.shape[-1]
     for side in range(2):
-        outs[side][...] = dot(at_ref[side], b_ref[...].reshape(rows, wide)).astype(BF16)
-
-
-def weight_grad(core, a, b, chunk):
+        product = dot(at_ref[side], b_ref[...].reshape(rows, wide)).astype(BF16)
+        outs[side][...] = product.reshape(own_ref.shape)
+
+
+def weight_grad(core, a, b, chunk, shared=None, before=()):
     rows, tall = a.shape
     stacked = b.ndim == 3
     wide = b.shape[0] * b.shape[2] if stacked else b.shape[1]
@@ -584,31 +592,44 @@
         right = pl.BlockSpec((1, rows, columns), lambda i, j, _: (j, 0, 0))
     else:
         right = pl.BlockSpec((rows, columns), lambda i, j, _: (0, j))
-    out = pl.BlockSpec((block // 2, columns), lambda i, j, _: (i, j))
+    if shared:
+        devices, height, at = shared
+        one = tall // 2 // devices
+        made = shape((devices, height, wide), BF16)
+        out = pl.BlockSpec(
+            (block // 2 // one, one, columns), lambda i, j, _: (i, at // one, j)
+        )
+    else:
+        made = shape((tall // 2, wide), BF16)
+        out = pl.BlockSpec((block // 2, columns), lambda i, j, _: (i, j))
     return pl.pallas_call(
         functools.partial(weight_kernel, size=chunk),
         grid_spec=pltpu.PrefetchScalarGridSpec(
             num_scalar_prefetch=1,
             grid=(tall // block, wide // columns),
-            in_specs=[pl.BlockSpec((rows, block), lambda i, j, _: (0, i)), right],
+            in_specs=[pl.BlockSpec((rows, block), lambda i, j, _: (0, i)), right]
+            + [pl.BlockSpec(memory_space=pl.ANY)] * len(before),
             out_specs=[out, out],
             scratch_shapes=[pltpu.VMEM((2, block // 2, rows), BF16)],
         ),
-        out_shape=[shape((tall // 2, wide), BF16)] * 2,
+        input_output_aliases={3: 0, 4: 1} if before else {},
+        out_shape=[made] * 2,
         compiler_params=params(),
         cost_estimate=cost(2 * rows * tall * wide, 2 * (rows * tall + rows * wide + tall * wide)),
         name="weight_grad",
-    )(core, a, b)
-
-
-def unturn_kernel(at_ref, c_ref, e_ref, l_ref, *refs):
+    )(core, a, b, *before)
+
+
+def unturn_kernel(at_ref, c_ref, e_ref, l_ref, *refs, team):
     blocks, out_ref = refs[:-1], refs[-1]
     cosine, early, late = c_ref[...], e_ref[...], l_ref[...]
     which = pl.program_id(0)
-    lanes = blocks[0].shape[-1]
-    for m, ref in enumerate(blocks):
-        for at in range(0, lanes, 128):
-            spot = pl.ds(pl.multiple_of((at_ref[0] ^ m) * lanes + at, 128), 128)
+    size = blocks[0].shape[-1]
+    lanes = size * len(blocks) // team
+    for i, ref in enumerate(blocks):
+        for at in range(0, size, 128):
+            first = (at_ref[0] ^ (i % team)) * lanes + i // team * size + at
+            spot = pl.ds(pl.multiple_of(first, 128), 128)
 
             @pl.when(which < 2)
             def _(ref=ref, at=at, spot=spot):
@@ -620,21 +641,21 @@
                 out_ref[0, :, spot] = ref[0, :, at : at + 128]
 
 
-def unturn(at, blocks, table):
+def unturn(at, blocks, table, team):
     _, rows, lanes = blocks[0].shape
     wide = pl.BlockSpec((rows, 128), lambda j, _: (0, 0))
-    team = len(blocks)
+    count = len(blocks)
     return pl.pallas_call(
-        unturn_kernel,
+        functools.partial(unturn_kernel, team=team),
         grid_spec=pltpu.PrefetchScalarGridSpec(
             num_scalar_prefetch=1,
             grid=(3,),
-            in_specs=[wide] * 3 + [pl.BlockSpec((1, rows, lanes), lambda j, _: (j, 0, 0))] * team,
-            out_specs=pl.BlockSpec((1, rows, team * lanes), lambda j, _: (j, 0, 0)),
-        ),
-        out_shape=shape((3, rows, team * lanes), BF16),
+            in_specs=[wide] * 3 + [pl.BlockSpec((1, rows, lanes), lambda j, _: (j, 0, 0))] * count,
+            out_specs=pl.BlockSpec((1, rows, count * lanes), lambda j, _: (j, 0, 0)),
+        ),
+        out_shape=shape((3, rows, count * lanes), BF16),
         compiler_params=params(),
-        cost_estimate=cost(0, 12 * rows * team * lanes),
+        cost_estimate=cost(0, 12 * rows * count * lanes),
         name="unturn",
     )(at, *table, *blocks)
 
@@ -701,7 +722,7 @@
     )(tokens, grad_middle, vectors, weights, low, *partial)
 
 
-def place_kernel(me_ref, *refs, masks):
+def place_kernel(me_ref, *refs, masks, pieces):
     count = len(masks)
     halves, (wide_ref, small_ref, sem) = refs[: 2 * count], refs[2 * count :]
     me = me_ref[0]
@@ -710,17 +731,29 @@
             half = len(masks[t]) // 2
             for j, mask in enumerate(masks[t]):
                 source = halves[2 * t + j // half].at[j % half]
-                place = wide_ref.at[t, me ^ mask] if t < count - 1 else small_ref.at[me ^ mask]
-                copy = pltpu.make_async_copy(source, place, sem.at[t, j])
-                copy.wait() if wait else copy.start()
+                for lane, (first, size, which, to) in enumerate(pieces[t]):
+                    origin = source.at[:, first : first + size]
+                    if which is None:
+                        place = small_ref.at[me ^ mask]
+                    else:
+                        place = wide_ref.at[which, me ^ mask, :, to : to + size]
+                    copy = pltpu.make_async_copy(origin, place, sem.at[t, j, lane])
+                    copy.wait() if wait else copy.start()
 
 
 class Chain:
     def __init__(self, links, own, away, rounds, wire=BF16):
         self.links, self.rounds, self.wire = links, [list(r) for r in rounds], wire
         self.axes = [b for b in range(links.bits - 1, -1, -1) if b != links.core]
-        self.dims = (2,) * len(self.axes) + (own.shape[0] * 2 // links.count,) + own.shape[1:]
+        self.dims = (2,) * len(self.axes)
+        if own.ndim == 2:
+            self.dims += (own.shape[0] * 2 // links.count,)
+        self.dims += own.shape[1:]
         self.terms = [own.reshape(self.dims), links.swap(away, 1 << links.core).reshape(self.dims)]
+
+    def hold(self, after):
+        self.terms = tie(self.terms, after)
+        return self
 
     def pick(self, mask):
         me, parts, axes = self.links.me() ^ mask, self.terms, list(self.axes)
@@ -752,6 +785,29 @@
         return total(self.terms)
 
 
+class Joined:
+    def __init__(self, *chains):
+        self.chains, self.links = chains, chains[0].links
+
+    @property
+    def rounds(self):
+        return self.chains[0].rounds
+
+    def split(self):
+        sent = [c.split() for c in self.chains]
+        return [jnp.concatenate(v, axis=-1) for v in zip(*sent)]
+
+    def swap(self, sent):
+        return self.chains[0].swap(sent)
+
+    def take(self, received):
+        first = 0
+        for c in self.chains:
+            last = first + c.terms[0].shape[-1]
+            c.take([v[..., first:last] for v in received])
+            first = last
+
+
 def total(terms):
     return functools.reduce(jnp.add, [t.astype(F32) for t in terms])
 
@@ -760,15 +816,18 @@
     return lax.optimization_barrier((values, others))[0]
 
 
-def beside(chains, work, *values):
-    chains = [c for c in chains if c.rounds]
+def begin(chains, values):
     sent = [c.split() for c in chains]
     values, sent = lax.optimization_barrier((values, sent))
-    received = [c.swap(v) for c, v in zip(chains, sent)]
-    result = work(*values)
-    for c, r in zip(chains, tie(received, jax.tree.leaves(result))):
+    for c, v in zip(chains, sent):
+        c.received = c.swap(v)
+    return values
+
+
+def finish(chains, after):
+    received = tie([c.received for c in chains], after)
+    for c, r in zip(chains, received):
         c.take(r)
-    return result
 
 
 class Links:
@@ -781,12 +840,11 @@
         dp_bits = list(range(self.core + 1, self.bits))
         self.dp_bits = [self.core] + dp_bits
         first, last = dp_bits[:1], dp_bits[1:]
-        self.seq_first = [[seq_bits[0]], seq_bits[1:], dp_bits]
-        self.seq_last = [[seq_bits[-1]], seq_bits[:-1], dp_bits]
-        self.dp_first = [first, [seq_bits[0]], seq_bits[1:] + last]
-        self.dp_last = [first, [seq_bits[-1]], seq_bits[:-1] + last]
+        self.seq_first = [[b] for b in seq_bits + dp_bits]
+        self.seq_last = [[b] for b in seq_bits[::-1] + dp_bits]
+        self.dp_first = [first, seq_bits[:1], seq_bits[1:] + last]
+        self.seq_then = [seq_bits[:1], seq_bits[1:], dp_bits]
         self.direct = [seq_bits, dp_bits]
-        self.direct_back = [dp_bits, seq_bits]
         self.orders = [
             seq_bits + dp_bits,
             seq_bits[::-1] + dp_bits,
@@ -812,23 +870,28 @@
         wins, rows, width = value.shape
         blocks = value.reshape(wins * 2, rows // 2, width)
         place = 2 * self.bit(0) + self.bit(1)
-        received = []
-        for k in range(4):
-            away = lax.dynamic_index_in_dim(
-                blocks, place ^ (2 * (k & 1) + (k >> 1)), 0, keepdims=False
-            )
-            received.append(lax.ppermute(away, BOTH, self.route(k)))
-        return received
-
-    def from_team(self, value):
+        return [
+            lax.dynamic_index_in_dim(blocks, place ^ (2 * (k & 1) + (k >> 1)), 0, keepdims=False)
+            for k in range(4)
+        ]
+
+    def move_one(self, sent, k):
+        return lax.ppermute(sent, BOTH, self.route(k))
+
+    def move(self, sent):
+        return [self.move_one(v, k) for k, v in enumerate(sent)]
+
+    def from_team_blocks(self, value):
         rows, width = value.shape
         blocks = value.reshape(4, rows // 4, width)
-        base = self.base()
-        received = []
-        for k in range(4):
-            away = lax.dynamic_index_in_dim(blocks, base ^ k, 0, keepdims=False)
-            back = [(j, i) for i, j in self.route(k)]
-            received.append(lax.ppermute(away, BOTH, back))
+        return [
+            lax.dynamic_index_in_dim(blocks, self.base() ^ k, 0, keepdims=False) for k in range(4)
+        ]
+
+    def back_one(self, sent, k):
+        return lax.ppermute(sent, BOTH, [(j, i) for i, j in self.route(k)])
+
+    def in_place(self, received):
         return [received[k] for k in (0, 2, 1, 3)]
 
     def base(self):
@@ -850,39 +913,40 @@
     def swap(self, value, mask):
         return lax.ppermute(value, BOTH, [(i, i ^ mask) for i in range(self.count)])
 
-    def chip_sum(self, own, away):
-        both = total([own, self.swap(away, 1 << self.core)]).astype(BF16)
-        groups = [
-            [d * self.seq + s for d in range(c, self.dp, 2) for s in range(self.seq)]
-            for c in range(2)
-        ]
-        summed = lax.psum_scatter(
-            both, BOTH, scatter_dimension=0, axis_index_groups=groups, tiled=True
-        )
-        return summed.astype(F32)
-
     def own(self):
         return jnp.reshape(lax.axis_index("dp") % 2, (1,))
 
-    def gather(self, values, orders):
-        args, masks, early = [], [], []
-        for value, order in zip(values, orders):
-            order = order[::-1] + [self.core]
-            held, mask = value[None], [0]
-            for bit in order:
-                got = self.swap(held, 1 << bit)
-                if bit == order[-3]:
-                    early.append(got)
-                mask = mask + [m | 1 << bit for m in mask]
-                if bit == self.core:
-                    args += [held, got]
-                else:
-                    held = jnp.concatenate([held, got], axis=0)
-            masks.append(mask)
-        wide = (len(values) - 1, self.count) + values[0].shape
-        narrow = (self.count,) + values[-1].shape
+    def gather(self, values, pieces, width, counts, moved):
+        orders = self.orders
+        held, masks = [v[None] for v in values], [[0] for v in values]
+        levels = self.bits - 1
+        early = None
+        (held, counts, moved) = lax.optimization_barrier((held, counts, moved))
+        for level in range(levels):
+            order = [o[levels - 1 - level] for o in orders]
+            got = [self.swap(h, 1 << b) for h, b in zip(held, order)]
+            masks = [m + [i | 1 << b for i in m] for m, b in zip(masks, order)]
+            if level in (0, 2):
+                moved[level : level + 2] = [
+                    self.move_one(moved[k], k) for k in (level, level + 1)
+                ]
+            if level < len(self.dp_bits):
+                counts = counts + self.swap(counts, 1 << self.dp_bits[level])
+            held = [jnp.concatenate([h, g], axis=0) for h, g in zip(held, got)]
+            if level in (1, 3):
+                held, counts, moved = lax.optimization_barrier((held, counts, moved))
+            else:
+                held, counts = lax.optimization_barrier((held, counts))
+            if level == 1:
+                early = held
+        got = [self.swap(h, 1 << self.core) for h in held]
+        masks = [m + [i | 1 << self.core for i in m] for m in masks]
+        args = [v for pair in zip(held, got) for v in pair]
+        rows = values[0].shape[0]
+        wide = (3, self.count, rows, width)
+        narrow = (self.count, rows, 128)
         placed = pl.pallas_call(
-            functools.partial(place_kernel, masks=masks),
+            functools.partial(place_kernel, masks=masks, pieces=pieces),
             grid_spec=pltpu.PrefetchScalarGridSpec(
                 num_scalar_prefetch=1,
                 grid=(1,),
@@ -891,18 +955,13 @@
                     pl.BlockSpec(wide, lambda i, _: (0, 0, 0, 0)),
                     pl.BlockSpec(narrow, lambda i, _: (0, 0, 0)),
                 ],
-                scratch_shapes=[pltpu.SemaphoreType.DMA((len(values), self.count))],
+                scratch_shapes=[pltpu.SemaphoreType.DMA((len(values), self.count, 3))],
             ),
             out_shape=[shape(wide, BF16), shape(narrow, BF16)],
             compiler_params=params(),
             name="place",
         )(jnp.reshape(self.me(), (1,)), *args)
-        return placed, early
-
-    def window_sum(self, value):
-        for bit in self.dp_bits:
-            value = value + self.swap(value, 1 << bit)
-        return value
+        return placed, early, counts, moved
 
 
 def packed(w_down, w_out, w_gate, w_up, width):
@@ -952,12 +1011,24 @@
 
     small = jnp.stack([ln1_gain, ln1_bias, ln2_gain, ln2_bias], axis=1)
     small = jnp.pad(small, ((0, 0), (0, 124)))
-    local = [w_query, w_key, w_value, small]
-    moved = links.to_team(tokens)
+    cut = width // 2
+    local = [
+        jnp.concatenate([w_query, w_key[:, :cut]], axis=1),
+        jnp.concatenate([w_key[:, cut:], w_value, small], axis=1),
+    ]
+    pieces = [
+        [(0, width, 0, 0), (width, cut, 1, 0)],
+        [(0, cut, 1, cut), (cut, width, 2, 0), (cut + width, 128, None, 0)],
+    ]
+    species_ids = jnp.arange(SPECIES)
+    onehot = (species[:, None] == species_ids[None, :]).astype(F32)
+    counts = jnp.sum(onehot * lengths[:, None].astype(F32), axis=0)
     told = jnp.stack([lengths, species])
     told = jnp.stack([told, links.swap(told, 1 << links.core)])
-    (qkv_w, small), early = links.gather(local, links.orders)
-    mine = tie(packed(w_down, w_out, w_gate, w_up, width), early)
+    (qkv_w, small), early, counts, moved = links.gather(
+        local, pieces, width, counts, links.to_team(tokens)
+    )
+    mine = packed(*tie((w_down, w_out, w_gate, w_up), early), width)
     weights = regrouped(lax.all_gather(mine, BOTH, axis=0), each, width)
     qkv_w = qkv_w.reshape(3, width, width)
     vectors = small.reshape(width, 128)[:, :4].T.astype(F32)
@@ -978,17 +1049,20 @@
         projected.append(project(scalar(member ^ m), rows_in, qkv_w, vectors, table, lanes))
     projected = projected[::-1]
     normed_one = projected[0][1]
-    cot_moved = links.to_team(tie(cotangent, [p[0] for p in projected[1:]]))
-    species_ids = jnp.arange(SPECIES)
-    onehot = (species[:, None] == species_ids[None, :]).astype(F32)
-    counts = jnp.sum(onehot * lengths[:, None].astype(F32), axis=0)
-    counts = links.window_sum(tie(counts, projected[-1][0]))
     window_weight = SPECIES * jnp.sum((kind == species_ids) * counts) / jnp.sum(counts)
     row_scale = jnp.where(positions < length, window_weight, 0.0)[:, None]
 
     qkv = links.exchange([p[0] for p in projected])
-    *mixed_heads, lse = attend(info, qkv)
-    mixed = links.exchange(mixed_heads)
+    qkv, cot_sent = lax.optimization_barrier((qkv, links.to_team(cotangent)))
+    cot_moved = links.move(cot_sent)
+    mixed_heads, lse, mixed = [], [], []
+    for part in range(PARTS):
+        *heads, sums = attend(info, qkv, part)
+        mixed_heads.append(heads)
+        lse.append(sums)
+        mixed += links.exchange(heads)
+        if part == 0:
+            qkv, cot_moved = lax.optimization_barrier((qkv, tie(cot_moved, sums)))
     cot_in = arrange(base, cot_moved)
     fed = feed(scalar(member), rows_in, cot_in, row_scale, mixed, vectors, weights)
     grad_mixed = fed[:team]
@@ -1000,72 +1074,94 @@
 
     narrow, broad = width // links.dp, hidden.shape[1] // links.dp
     core = links.own()
-    terms = [
-        (hidden, grad_low, broad, links.dp_first),
-        (normed_two, grad_gate, narrow, links.seq_first),
-        (normed_two, grad_up, narrow, links.seq_last),
-        (mixed_rows, grad_middle_low, narrow, links.dp_last),
+    place = scalar(2 * links.bit(0) + links.bit(1))
+    shared = (links.count // 2, 5 * each)
+    grad_low, sent = lax.optimization_barrier((grad_low, links.from_team_blocks(delta)))
+    returned = [links.back_one(sent[k], k) for k in range(2)]
+    before = weight_grad(core, hidden, grad_low, broad, shared + (0,))
+    low, returned = lax.optimization_barrier((tie(grad_middle_low, before), returned))
+    own, away = weight_grad(core, mixed_rows, low, narrow, shared + (4 * each,), before)
+    sum_rest = Chain(links, own, away, links.dp_first)
+    grad_gate, sent = lax.optimization_barrier((tie(grad_gate, own), sent[2:]))
+    returned += [links.back_one(v, k) for k, v in enumerate(sent, 2)]
+    own, away = weight_grad(core, normed_two, grad_gate, narrow)
+    sum_gate = Chain(links, own, away, links.seq_first)
+    grad_up = begin([sum_rest.hold((own, returned))], tie(grad_up, own))
+    own, away = weight_grad(core, normed_two, grad_up, narrow)
+    sum_up = Chain(links, own, away, links.seq_last)
+
+    def back(part, grads, sub=0, subs=1):
+        return attend_back(
+            info, qkv, mixed_heads[part], grads, lse[part], part, sub, subs
+        )
+
+    def through(part, low, partial):
+        return project_back(rows_in, grad_middle, vectors, qkv_w, low, part, team, partial)
+
+    grad_heads = begin([sum_gate.hold(own)], tie(list(grad_heads), own))
+    output = settle(place, links.in_place(tie(returned, own)), [tokens])
+    grad_heads = begin([sum_up.hold(output)], tie(list(grad_heads), output))
+    made = back(0, grad_heads)
+    received = links.exchange(made)
+    chains = [sum_rest, sum_gate, sum_up]
+    finish(chains, made)
+    received = begin(chains, tie(list(received), made))
+    low = unturn(scalar(member), received, table, team)
+    own_one, away_one = weight_grad(core, normed_one, low, narrow)
+    sum_one = Chain(links, own_one, away_one, links.seq_then)
+    (partial,) = through(0, tie(low, own_one), [])
+    sum_one.hold(partial)
+    if len(links.seq_first) == 4:
+        sum_pair = [Joined(sum_gate, sum_up)]
+    else:
+        sum_pair = [sum_gate, sum_up]
+    subs = 2 if lanes // 128 // PARTS > 1 else 1
+    made = back(1, tie(list(grad_heads), partial), 0, subs)
+    received = list(links.exchange(made))
+    finish(chains, made)
+    if subs > 1:
+        grad_heads = begin(sum_pair + [sum_rest], tie(list(grad_heads), made))
+        made = back(1, grad_heads, 1, subs)
+        received += links.exchange(made)
+    else:
+        received = begin(sum_pair + [sum_rest], received)
+    finish(sum_pair, made)
+    received = begin(sum_pair + [sum_one], tie(received, made))
+    low = unturn(scalar(member), received, table, team)
+    grad_in, sums_one = through(1, low, [partial])
+    finish(sum_pair + [sum_one, sum_rest], grad_in)
+    chains = [c for c in sum_pair + [sum_one] if c.rounds]
+    low, sent = begin(chains, (low, links.from_team_blocks(grad_in)))
+    home = [links.back_one(v, k) for k, v in enumerate(sent)]
+    own_two, away_two = weight_grad(core, normed_one, low, narrow)
+    finish(chains, own_two)
+    gains = jnp.concatenate([sums_one, sums_two], axis=0)
+    gains = gains.reshape(4, links.dp // 2, 2, width // links.dp).transpose(2, 1, 3, 0)
+    gains = gains.reshape(2, width // 2, 4)
+    gains = jnp.pad(gains, ((0, 0), (0, 0), (0, 124))).astype(BF16)
+    gains = [
+        lax.dynamic_index_in_dim(gains, c, 0, keepdims=False) for c in (core[0], 1 - core[0])
     ]
-    chains = [Chain(links, *weight_grad(core, *t[:3]), t[3]) for t in terms]
-    sum_down, sum_gate, sum_up, sum_out = chains
-
-    blocks, made = [], []
-    for part in range(PARTS):
-        made = beside(
-            chains, lambda *g: attend_back(info, qkv, mixed_heads, g, lse, part), *grad_heads
-        )
-        grad_heads = tie(list(grad_heads), made)
-        blocks.append(links.exchange(made))
-    returned = links.from_team(tie(delta, made))
-
-    sums, partial, fresh = [], [], []
-    for part in range(PARTS):
-
-        def through(value):
-            return project_back(
-                rows_in, grad_middle, vectors, qkv_w, value, part, team, partial
-            )
-
-        def weigh(*received):
-            low = unturn(scalar(member), received, table)
-            return (low,) + tuple(weight_grad(core, normed_one, low, narrow))
-
-        if part < PARTS - 1:
-            low, own, away = weigh(*tie(blocks[part], made))
-            fresh = [Chain(links, own, away, links.direct_back)]
-            sums.append(fresh)
-            partial = beside(chains, through, tie(low, own))
-            chains = chains + fresh
-        else:
-            low, own, away = beside(chains, weigh, *tie(blocks[part], partial))
-            half = own.shape[1] // 2
-            fresh = [
-                Chain(links, own[:, :half], away[:, :half], links.direct),
-                Chain(links, own[:, half:], away[:, half:], links.direct),
-            ]
-            sums.append(fresh)
-            grad_in, sums_one = beside(chains, through, tie(low, own))
-            chains = chains + fresh
-
-    home = links.from_team(grad_in)
-    place = scalar(2 * links.bit(0) + links.bit(1))
-    gains = jnp.concatenate([sums_one, sums_two], axis=0)
-    gains = gains.reshape(4, links.dp // 2, 2, links.seq, each).transpose(2, 1, 3, 0, 4)
-    gains = gains.reshape(2, links.count // 2 * 4, each)
-    own, away = (
-        lax.dynamic_index_in_dim(gains, c, 0, keepdims=False) for c in (core[0], 1 - core[0])
-    )
-    gains = Chain(links, own, away, links.direct, F32)
-    output = settle(place, tie(returned, sums_one), [tokens])
-    chains = chains + [gains]
-    while any(c.rounds for c in chains):
-        beside(chains, lambda: [])
-    grad_tokens = settle(place, home, [])
-
-    merged = [jnp.concatenate([c.result() for c in s], axis=1) for s in sums]
-    merged = jnp.concatenate([m.reshape(each, 3, team, 1, -1) for m in merged], axis=3)
+    own = jnp.concatenate([own_two, gains[0]], axis=1)
+    away = jnp.concatenate([away_two, gains[1]], axis=1)
+    last = Chain(links, own, away, links.direct)
+    chains = [c for c in sum_pair + [sum_rest, last] if c.rounds]
+    nothing = begin(chains, [])
+    finish(chains, nothing)
+    pieces = [c for c in sum_pair + [sum_rest] if c.rounds]
+    chains = pieces + [Joined(sum_one, last)]
+    while chains:
+        nothing = begin(chains, [])
+        finish(chains, nothing)
+        chains = [c for c in chains if c.rounds]
+    grad_tokens = settle(place, links.in_place(home), [])
+
+    last = last.result()
+    gains = last[:, -128:].T
+    merged = jnp.stack([sum_one.result(), last[:, :-128]], axis=1)
+    merged = merged.reshape(each, PARTS, 3, team, -1).transpose(0, 2, 3, 1, 4)
     merged = merged.reshape(each, 3, width)
-    gains = gains.result()
+    rest = sum_rest.result()
     return (
         output.reshape(wins, rows, width),
         grad_tokens.reshape(wins, rows, width),
@@ -1074,12 +1170,12 @@
         merged[:, 0],
         merged[:, 1],
         merged[:, 2],
-        sum_out.result(),
+        rest[4 * each :],
         gains[2],
         gains[3],
         sum_gate.result(),
         sum_up.result(),
-        sum_down.result(),
+        rest[: 4 * each],
     )
 
 

time: 784 us -> 733 us (0.935); the launches traced: 782 us -> 723 us
  starting transfers between devices: 193 us -> 80.2 us
  Pallas kernels: 299 us -> 400 us
  waiting for transfers between devices: 164 us -> 130 us
    pallas_call x2 -> x3, Pallas kernels: 39.4 us -> 109 us  [attend_back(): pl.pallas_call(functools.partial(attend_back_kernel, team=team), grid_spe...]
    ppermute x16, starting transfers between devices: 80.8 us -> 20.4 us  [the longest x8 12.2 us: move_one(): return lax.ppermute(sent, BOTH, self.route(k))]
    ppermute x81 -> x45, starting transfers between devices: 112 us -> 59.8 us  [swap(): return lax.ppermute(value, BOTH, [(i, i ^ mask) for i in range(self.count)])]
    ppermute x81 -> x45, waiting for transfers between devices: 136 us -> 99.6 us  [swap(): return lax.ppermute(value, BOTH, [(i, i ^ mask) for i in range(self.count)])]
    pallas_call x1 -> x2, Pallas kernels: 37.5 us -> 66.4 us  [attend(): pl.pallas_call(functools.partial(attend_kernel, team=team), grid_spec=plt...]
    unnamed x213 -> x105, local copies, waits for them, and re-layouts: 20.4 us -> 8.63 us
    convert_element_type x17 -> x16, other arithmetic: 44.3 us -> 39.8 us  [split(): sent = [total(self.pick(m)).astype(self.wire) for m in self.masks[1:]]]
  transfers between devices with their start and end apart: 98 -> 62, of which waited for: 28 -> 23; matrix products, arithmetic and copies ran while one was open for 12% -> 8% of each run, Pallas kernels for 26% -> 43%
where the time goes in v3:
time: 733 us; the launch traced here: 723 us
  Pallas kernels  400 us (55%)
  waiting for transfers between devices  130 us (18%)
  starting transfers between devices  80.2 us (11%)
  other arithmetic  68.6 us (9%)
  local copies, waits for them, and re-layouts  27.6 us (4%)
  between operations  16.6 us (2%)
    pallas_call x3, Pallas kernels, attend_back(): pl.pallas_call(functools.partial(attend_back_kernel, team=team), grid_spe...  109 us
    ppermute x45, waiting for transfers between devices, swap(): return lax.ppermute(value, BOTH, [(i, i ^ mask) for i in range(self.count)])  99.6 us
    pallas_call x1, Pallas kernels, feed(): pl.pallas_call(functools.partial(feed_kernel, team=team), grid_spec=pltpu...  79 us
    pallas_call x2, Pallas kernels, attend(): pl.pallas_call(functools.partial(attend_kernel, team=team), grid_spec=plt...  66.4 us
    pallas_call x6, Pallas kernels, weight_grad(): pl.pallas_call(functools.partial(weight_kernel, size=chunk), grid_spec=pl...  61.5 us
    ppermute x45, starting transfers between devices, swap(): return lax.ppermute(value, BOTH, [(i, i ^ mask) for i in range(self.count)])  59.8 us
    convert_element_type x16, other arithmetic, split(): sent = [total(self.pick(m)).astype(self.wire) for m in self.masks[1:]]  39.8 us
    ppermute x8, waiting for transfers between devices, move_one(): return lax.ppermute(sent, BOTH, self.route(k))  28.1 us
  transfers between devices with their start and end apart: 62, of which 23 were waited for; matrix products, arithmetic and copies ran while one was open for 8% of the time, Pallas kernels for 43%

profile of v3, /device:TPU:0, one launch (start us, length us, event | category | flops | bytes accessed | tf_op | source)
XLA Modules:
  0.0 723.1 jit_solution(6031905667228564470)
XLA Ops:
  19.9 6.9 collective-permute-done
  62.7 20.8 %collective-permute-done.11 = bf16[8,32,1536]{2,1,0:T(8,128)(2,1)S(1)} collective-permute-done((bf16[8,32,1536]{2,1,0:T(8,128)(2,1)S(1)}, bf16[8,32,1536]{2,1,0:T(8,128)(2,1)S(1)}, u32[]{:S(2)}, u32[]{:S(2)}) %collective-permute-start.11) | collective-permute-done | bytes 786464 | tf_op jit(solution)/shard_map/ppermute | solution.py:914
  84.8 18.3 %collective-permute-done.13.refs_2_ = bf16[256,1024]{1,0:T(8,128)(2,1)S(1)} collective-permute-done((bf16[256,1024]{1,0:T(8,128)(2,1)}, bf16[256,1024]{1,0:T(8,128)(2,1)S(1)}, u32[]{:S(2)}, u32[]{:S(2)}) %collective-permute-start.13) | collective-permute-done | bytes 524320 | tf_op jit(solution)/shard_map/ppermute | solution.py:879
  112.9 7.5 %place.1 = (bf16[3,32,32,1024]{3,2,1,0:T(8,128)(2,1)}, bf16[32,32,128]{2,1,0:T(8,128)(2,1)}) custom-call(s32[1]{0:T(128)} %bitcast.15.me_ref, bf16[16,32,1536]{2,1,0:T(8,128)(2,1)} %copy-done.4, bf16[16,32,1536]{2,1,0:T(8,128)(2,1)} %collective-permute-done.15.refs_1_, bf16[16,32,1664]{2,1,0:T(8,128)(2,1)} %copy-done.3, ...), custom_call_target="tpu_custom_call" | custom-call | tf_op jit(solution)/shard_map/place/pallas_call | solution.py:948
  122.3 12.3 %project.3 = (bf16[3,1024,512]{2,1,0:T(8,128)(2,1)}, bf16[1024,1024]{1,0:T(8,128)(2,1)}) custom-call(s32[1]{0:T(128)} %bitcast.19.at_ref, bf16[1024,1024]{1,0:T(8,128)(2,1)} %bitcast.319, bf16[3,1024,1024]{2,1,0:T(8,128)(2,1)} %bitcast.315, f32[4,1024]{1,0:T(4,128)} %bitcast.364, f32[1024,128]{1,0:T(8,128)} %pad_maximum_fusion.6.c_ref, ...), custom_call_target="tpu_custom_call" | custom-call | flops 50331648 | bytes 98304 | tf_op jit(solution)/shard_map/project/pallas_call | solution.py:151
  137.9 12.9 %project.2 = (bf16[3,1024,512]{2,1,0:T(8,128)(2,1)}, bf16[1024,1024]{1,0:T(8,128)(2,1)}) custom-call(s32[1]{0:T(128)} %bitcast.1.at_ref, bf16[1024,1024]{1,0:T(8,128)(2,1)} %bitcast.320, bf16[3,1024,1024]{2,1,0:T(8,128)(2,1)} %bitcast.316, f32[4,1024]{1,0:T(4,128)} %bitcast.365, f32[1024,128]{1,0:T(8,128)} %pad_maximum_fusion.6.c_ref, ...), custom_call_target="tpu_custom_call" | custom-call | flops 50331648 | bytes 98304 | tf_op jit(solution)/shard_map/project/pallas_call | solution.py:151
  163.8 33.4 %attend.2 = (bf16[1024,256]{1,0:T(8,128)(2,1)}, bf16[1024,256]{1,0:T(8,128)(2,1)}, f32[2,2,2048]{2,1,0:T(2,128)}) custom-call(s32[3]{0:T(128)} %pad_add_fusion.1.info_ref, bf16[3,1024,512]{2,1,0:T(8,128)(2,1)} %get-tuple-element.252.refs_0_.refs_2_.refs_4_, bf16[3,1024,512]{2,1,0:T(8,128)(2,1)} %copy-done, ...), custom_call_target="tpu_custom_call" | custom-call | flops 268435456 | bytes 65536 | tf_op jit(solution)/shard_map/attend/pallas_call | solution.py:255
  204.1 33.0 %attend.3 = (bf16[1024,256]{1,0:T(8,128)(2,1)}, bf16[1024,256]{1,0:T(8,128)(2,1)}, f32[2,2,2048]{2,1,0:T(2,128)}) custom-call(s32[3]{0:T(128)} %pad_add_fusion.1.info_ref, bf16[3,1024,512]{2,1,0:T(8,128)(2,1)} %get-tuple-element.252.refs_0_.refs_2_.refs_4_, bf16[3,1024,512]{2,1,0:T(8,128)(2,1)} %copy-done, ...), custom_call_target="tpu_custom_call" | custom-call | flops 268435456 | bytes 65536 | tf_op jit(solution)/shard_map/attend/pallas_call | solution.py:255
  246.2 79.0 %feed.1 = (bf16[1024,512]{1,0:T(8,128)(2,1)}, bf16[1024,512]{1,0:T(8,128)(2,1)}, bf16[1024,1024]{1,0:T(8,128)(2,1)}, f32[1024,1024]{1,0:T(8,128)}, bf16[1024,102...) custom-call(s32[1]{0:T(128)} %bitcast.1.at_ref, ...), custom_call_target="tpu_custom_call" | custom-call | flops 872415232 | bytes 1671168 | tf_op jit(solution)/shard_map/feed/pallas_call | solution.py:514
  327.7 13.2 %weight_grad.6 = (bf16[16,160,1024]{2,1,0:T(8,128)(2,1)}, bf16[16,160,1024]{2,1,0:T(8,128)(2,1)}) custom-call(s32[1]{0:T(128)} %bitcast.36.core_ref, bf16[1024,4096]{1,0:T(8,128)(2,1)} %get-tuple-element.257.a_ref, bf16[1024,1024]{1,0:T(8,128)(2,1)} %get-tuple-element.260.b_ref), custom_call_target="tpu_custom_call" | custom-call | flops 134217728 | bytes 294912 | tf_op jit(solution)/shard_map/weight_grad/pallas_call | solution.py:605
  340.9 6.3 weight_grad.7
  351.5 13.6 %weight_grad.8 = (bf16[512,4096]{1,0:T(8,128)(2,1)}, bf16[512,4096]{1,0:T(8,128)(2,1)}) custom-call(s32[1]{0:T(128)} %bitcast.36.core_ref, bf16[1024,1024]{1,0:T(8,128)(2,1)} %get-tuple-element.277.a_ref, bf16[1024,4096]{1,0:T(8,128)(2,1)} %get-tuple-element.279.b_ref), custom_call_target="tpu_custom_call" | custom-call | flops 134217728 | bytes 294912 | tf_op jit(solution)/shard_map/weight_grad/pallas_call | solution.py:605
  371.2 13.5 %weight_grad.9 = (bf16[512,4096]{1,0:T(8,128)(2,1)}, bf16[512,4096]{1,0:T(8,128)(2,1)}) custom-call(s32[1]{0:T(128)} %bitcast.36.core_ref, bf16[1024,1024]{1,0:T(8,128)(2,1)} %get-tuple-element.277.a_ref, bf16[1024,4096]{1,0:T(8,128)(2,1)} %get-tuple-element.285.b_ref), custom_call_target="tpu_custom_call" | custom-call | flops 134217728 | bytes 294912 | tf_op jit(solution)/shard_map/weight_grad/pallas_call | solution.py:605
  404.7 53.0 %attend_back.3 = (bf16[3,1024,256]{2,1,0:T(8,128)(2,1)}, bf16[3,1024,256]{2,1,0:T(8,128)(2,1)}) custom-call(s32[3]{0:T(128)} %pad_add_fusion.1.info_ref, bf16[3,1024,512]{2,1,0:T(8,128)(2,1)} %get-tuple-element.252.refs_0_.refs_2_.refs_4_, bf16[3,1024,512]{2,1,0:T(8,128)(2,1)} %copy-done, bf16[3,1024,512]{2,1,0:T(8,128)(2,1)} %get-tuple-element.252.refs_0_.refs_2_.refs_4_, ...), custom_call_target="tpu_custom_call" | custom-call | flops 503316480 | bytes 131072 | tf_op jit(solution)/shard_map/attend_back/pallas_call | solution.py:396
  479.6 7.3 %weight_grad.10 = (bf16[512,1536]{1,0:T(8,128)(2,1)}, bf16[512,1536]{1,0:T(8,128)(2,1)}) custom-call(s32[1]{0:T(128)} %bitcast.36.core_ref, bf16[1024,1024]{1,0:T(8,128)(2,1)} %get-tuple-element.320.a_ref, bf16[3,1024,512]{2,1,0:T(8,128)(2,1)} %unturn.2.b_ref.low_ref), custom_call_target="tpu_custom_call" | custom-call | flops 50331648 | bytes 131072 | tf_op jit(solution)/shard_map/weight_grad/pallas_call | solution.py:605
  486.9 10.4 %project_back.2.refs_0_ = f32[1024,1024]{1,0:T(8,128)} custom-call(bf16[1024,1024]{1,0:T(8,128)(2,1)} %bitcast.322, f32[1024,1024]{1,0:T(8,128)} %get-tuple-element.307.gm_ref, f32[4,1024]{1,0:T(4,128)} %bitcast.367, bf16[3,1024,1024]{2,1,0:T(8,128)(2,1)} %bitcast.317, bf16[3,1024,512]{2,1,0:T(8,128)(2,1)} %unturn.2.b_ref.low_ref), custom_call_target="tpu_custom_call" | custom-call | flops 50331648 | bytes 393216 | tf_op jit(solution)/shard_map/project_back/pallas_call | solution.py:699
  497.3 28.1 %attend_back.4 = (bf16[3,1024,128]{2,1,0:T(8,128)(2,1)}, bf16[3,1024,128]{2,1,0:T(8,128)(2,1)}) custom-call(s32[3]{0:T(128)} %pad_add_fusion.1.info_ref, bf16[3,1024,512]{2,1,0:T(8,128)(2,1)} %get-tuple-element.252.refs_0_.refs_2_.refs_4_, bf16[3,1024,512]{2,1,0:T(8,128)(2,1)} %copy-done, bf16[3,1024,512]{2,1,0:T(8,128)(2,1)} %get-tuple-element.252.refs_0_.refs_2_.refs_4_, ...), custom_call_target="tpu_custom_call" | custom-call | flops 251658240 | bytes 65536 | tf_op jit(solution)/shard_map/attend_back/pallas_call | solution.py:396
  535.5 28.3 %attend_back.5 = (bf16[3,1024,128]{2,1,0:T(8,128)(2,1)}, bf16[3,1024,128]{2,1,0:T(8,128)(2,1)}) custom-call(s32[3]{0:T(128)} %pad_add_fusion.1.info_ref, bf16[3,1024,512]{2,1,0:T(8,128)(2,1)} %get-tuple-element.252.refs_0_.refs_2_.refs_4_, bf16[3,1024,512]{2,1,0:T(8,128)(2,1)} %copy-done, bf16[3,1024,512]{2,1,0:T(8,128)(2,1)} %get-tuple-element.252.refs_0_.refs_2_.refs_4_, ...), custom_call_target="tpu_custom_call" | custom-call | flops 251658240 | bytes 65536 | tf_op jit(solution)/shard_map/attend_back/pallas_call | solution.py:396
  581.2 5.8 unturn.3.low_ref.b_ref
  587.0 14.1 %project_back.3 = (bf16[1024,1024]{1,0:T(8,128)(2,1)}, f32[2,1024]{1,0:T(2,128)}) custom-call(bf16[1024,1024]{1,0:T(8,128)(2,1)} %bitcast.323, f32[1024,1024]{1,0:T(8,128)} %get-tuple-element.307.gm_ref, f32[4,1024]{1,0:T(4,128)} %bitcast.368, bf16[3,1024,1024]{2,1,0:T(8,128)(2,1)} %bitcast.318, bf16[3,1024,512]{2,1,0:T(8,128)(2,1)} %unturn.3.low_ref.b_ref, ...), custom_call_target="tpu_custom_call" | custom-call | flops 50331648 | bytes 393216 | tf_op jit(solution)/shard_map/project_back/pallas_call | solution.py:699
  604.9 16.9 %collective-permute-done.47 = bf16[160,1024]{1,0:T(8,128)(2,1)} collective-permute-done((bf16[160,1024]{1,0:T(8,128)(2,1)S(1)}, bf16[160,1024]{1,0:T(8,128)(2,1)}, u32[]{:S(2)}, u32[]{:S(2)}) %collective-permute-start.47) | collective-permute-done | bytes 327712 | tf_op jit(solution)/shard_map/ppermute | solution.py:914
  625.0 7.5 %weight_grad.11 = (bf16[512,1536]{1,0:T(8,128)(2,1)}, bf16[512,1536]{1,0:T(8,128)(2,1)}) custom-call(s32[1]{0:T(128)} %bitcast.36.core_ref, bf16[1024,1024]{1,0:T(8,128)(2,1)} %get-tuple-element.320.a_ref, bf16[3,1024,512]{2,1,0:T(8,128)(2,1)} %unturn.3.low_ref.b_ref), custom_call_target="tpu_custom_call" | custom-call | flops 50331648 | bytes 131072 | tf_op jit(solution)/shard_map/weight_grad/pallas_call | solution.py:605
  635.3 7.5 %collective-permute-start.57 = (bf16[2,2,32,1536]{3,2,1,0:T(8,128)(2,1)}, bf16[2,2,32,1536]{3,2,1,0:T(8,128)(2,1)S(1)}, u32[]{:S(2)}, u32[]{:S(2)}) collective-permute-start(bf16[2,2,32,1536]{3,2,1,0:T(8,128)(2,1)} %fusion.9), channel_id=1, source_target_pairs={{0,2},{1,3},{2,0},{3,1},{4,6},{5,7},{6,4},{7,5},{8,10},{9,11},{10,... | collective-permute-start | bytes 1179656 | tf_op jit(solution)/shard_map/ppermute | solution.py:914
  659.1 28.9 %collective-permute-done.55 = bf16[2,2,32,1664]{3,2,1,0:T(8,128)(2,1)S(1)} collective-permute-done((bf16[2,2,32,1664]{3,2,1,0:T(8,128)(2,1)S(1)}, bf16[2,2,32,1664]{3,2,1,0:T(8,128)(2,1)S(1)}, u32[]{:S(2)}, u32[]{:S(2)}) %collective-permute-start.55) | collective-permute-done | bytes 426016 | tf_op jit(solution)/shard_map/ppermute | solution.py:914
  (311 shorter events, 227.9 us)
Async XLA Ops:
  7.2 238.1 %all-gather.3.cloned.1.call-start = ((), (), s32[]{:S(2)}) async-start(), calls=%async_computation | async-start | bytes 28114944 | tf_op jit(solution)/shard_map/all_gather | solution.py:1032
  62.7 40.5 %collective-permute-start.13 = (bf16[256,1024]{1,0:T(8,128)(2,1)}, bf16[256,1024]{1,0:T(8,128)(2,1)S(1)}, u32[]{:S(2)}, u32[]{:S(2)}) collective-permute-start(bf16[256,1024]{1,0:T(8,128)(2,1)} %get-tuple-element.218), channel_id=1, source_target_pairs={{0,4},{1,5},{2,0},{3,1},{4,6},{5,7},{6,2},{7,3},{8,12},{9,13},{10,... | collective-permute-start | bytes 1572872 | tf_op jit(solution)/shard_map/ppermute | solution.py:879
  62.7 40.5 %collective-permute-start.14 = (bf16[256,1024]{1,0:T(8,128)(2,1)}, bf16[256,1024]{1,0:T(8,128)(2,1)S(1)}, u32[]{:S(2)}, u32[]{:S(2)}) collective-permute-start(bf16[256,1024]{1,0:T(8,128)(2,1)} %get-tuple-element.219), channel_id=1, source_target_pairs={{0,5},{1,4},{2,1},{3,0},{4,7},{5,6},{6,3},{7,2},{8,13},{9,12},{10,... | collective-permute-start | bytes 1572872 | tf_op jit(solution)/shard_map/ppermute | solution.py:879
  150.8 46.6 %collective-permute-start.18 = (bf16[256,1024]{1,0:T(8,128)(2,1)}, bf16[256,1024]{1,0:T(8,128)(2,1)}, u32[]{:S(2)}, u32[]{:S(2)}) collective-permute-start(bf16[256,1024]{1,0:T(8,128)(2,1)} %get-tuple-element.232), channel_id=1, source_target_pairs={{0,0},{1,1},{2,4},{3,5},{4,2},{5,3},{6,6},{7,7},{8,8},{9,9},{10,12... | collective-permute-start | bytes 1572872 | tf_op jit(solution)/shard_map/ppermute | solution.py:879
  156.3 41.2 %collective-permute-start.19 = (bf16[256,1024]{1,0:T(8,128)(2,1)}, bf16[256,1024]{1,0:T(8,128)(2,1)}, u32[]{:S(2)}, u32[]{:S(2)}) collective-permute-start(bf16[256,1024]{1,0:T(8,128)(2,1)} %get-tuple-element.233), channel_id=1, source_target_pairs={{0,1},{1,0},{2,5},{3,4},{4,3},{5,2},{6,7},{7,6},{8,9},{9,8},{10,13... | collective-permute-start | bytes 1572872 | tf_op jit(solution)/shard_map/ppermute | solution.py:879
  158.5 41.8 %collective-permute-start.20 = (bf16[256,1024]{1,0:T(8,128)(2,1)}, bf16[256,1024]{1,0:T(8,128)(2,1)}, u32[]{:S(2)}, u32[]{:S(2)}) collective-permute-start(bf16[256,1024]{1,0:T(8,128)(2,1)} %get-tuple-element.234), channel_id=1, source_target_pairs={{0,4},{1,5},{2,0},{3,1},{4,6},{5,7},{6,2},{7,3},{8,12},{9,13},{10,... | collective-permute-start | bytes 1572872 | tf_op jit(solution)/shard_map/ppermute | solution.py:879
  158.5 45.6 %collective-permute-start.21 = (bf16[256,1024]{1,0:T(8,128)(2,1)}, bf16[256,1024]{1,0:T(8,128)(2,1)}, u32[]{:S(2)}, u32[]{:S(2)}) collective-permute-start(bf16[256,1024]{1,0:T(8,128)(2,1)} %get-tuple-element.235), channel_id=1, source_target_pairs={{0,5},{1,4},{2,1},{3,0},{4,7},{5,6},{6,3},{7,2},{8,13},{9,12},{10,... | collective-permute-start | bytes 1572872 | tf_op jit(solution)/shard_map/ppermute | solution.py:879
  197.2 48.0 %collective-permute-start.23 = (bf16[1024,256]{1,0:T(8,128)(2,1)}, bf16[1024,256]{1,0:T(8,128)(2,1)S(1)}, u32[]{:S(2)}, u32[]{:S(2)}) collective-permute-start(bf16[1024,256]{1,0:T(8,128)(2,1)} %get-tuple-element.251.refs_7_), channel_id=1, source_target_pairs={{0,4},{1,5},{2,6},{3,7},{4,0},{5,1},{6,2},{7,3},{8,12},{9,13},{10,... | collective-permute-start | bytes 1572872 | tf_op jit(solution)/shard_map/ppermute | solution.py:914
  385.2 76.3 %collective-permute-start.34 = (bf16[2,2,2,160,1024]{4,3,2,1,0:T(8,128)(2,1)}, bf16[2,2,2,160,1024]{4,3,2,1,0:T(8,128)(2,1)}, u32[]{:S(2)}, u32[]{:S(2)}) collective-permute-start(bf16[2,2,2,160,1024]{4,3,2,1,0:T(8,128)(2,1)} %fusion), channel_id=1, source_target_pairs={{0,8},{1,9},{2,10},{3,11},{4,12},{5,13},{6,14},{7,15},{8,0},{9,1},... | collective-permute-start | bytes 7864328 | tf_op jit(solution)/shard_map/ppermute | solution.py:914
  398.2 63.3 %collective-permute-start.35 = (bf16[2,2,2,32,4096]{4,3,2,1,0:T(8,128)(2,1)}, bf16[2,2,2,32,4096]{4,3,2,1,0:T(8,128)(2,1)S(1)}, u32[]{:S(2)}, u32[]{:S(2)}) collective-permute-start(bf16[2,2,2,32,4096]{4,3,2,1,0:T(8,128)(2,1)} %fusion.2), channel_id=1, source_target_pairs={{0,1},{1,0},{2,3},{3,2},{4,5},{5,4},{6,7},{7,6},{8,9},{9,8},{10,11... | collective-permute-start | bytes 6291464 | tf_op jit(solution)/shard_map/ppermute | solution.py:914
  404.7 56.9 %collective-permute-start.36 = (bf16[2,2,2,32,4096]{4,3,2,1,0:T(8,128)(2,1)}, bf16[2,2,2,32,4096]{4,3,2,1,0:T(8,128)(2,1)}, u32[]{:S(2)}, u32[]{:S(2)}) collective-permute-start(bf16[2,2,2,32,4096]{4,3,2,1,0:T(8,128)(2,1)} %fusion.3), channel_id=1, source_target_pairs={{0,2},{1,3},{2,0},{3,1},{4,6},{5,7},{6,4},{7,5},{8,10},{9,11},{10,... | collective-permute-start | bytes 6291464 | tf_op jit(solution)/shard_map/ppermute | solution.py:914
  470.8 54.7 %collective-permute-start.38 = (bf16[2,2,160,1024]{3,2,1,0:T(8,128)(2,1)}, bf16[2,2,160,1024]{3,2,1,0:T(8,128)(2,1)}, u32[]{:S(2)}, u32[]{:S(2)}) collective-permute-start(bf16[2,2,160,1024]{3,2,1,0:T(8,128)(2,1)} %fusion.1), channel_id=1, source_target_pairs={{0,1},{1,0},{2,3},{3,2},{4,5},{5,4},{6,7},{7,6},{8,9},{9,8},{10,11... | collective-permute-start | bytes 3932168 | tf_op jit(solution)/shard_map/ppermute | solution.py:914
  471.8 53.6 %collective-permute-start.39 = (bf16[2,2,32,4096]{3,2,0,1:T(8,128)(2,1)}, bf16[2,2,32,4096]{3,2,0,1:T(8,128)(2,1)}, u32[]{:S(2)}, u32[]{:S(2)}) collective-permute-start(bf16[2,2,32,4096]{3,2,0,1:T(8,128)(2,1)} %copy.147), channel_id=1, source_target_pairs={{0,2},{1,3},{2,0},{3,1},{4,6},{5,7},{6,4},{7,5},{8,10},{9,11},{10,... | collective-permute-start | bytes 3145736 | tf_op jit(solution)/shard_map/ppermute | solution.py:914
  471.8 53.6 %collective-permute-start.40 = (bf16[2,2,32,4096]{3,2,1,0:T(8,128)(2,1)S(1)}, bf16[2,2,32,4096]{3,2,1,0:T(8,128)(2,1)}, u32[]{:S(2)}, u32[]{:S(2)}) collective-permute-start(bf16[2,2,32,4096]{3,2,1,0:T(8,128)(2,1)S(1)} %fusion.4), channel_id=1, source_target_pairs={{0,1},{1,0},{2,3},{3,2},{4,5},{5,4},{6,7},{7,6},{8,9},{9,8},{10,11... | collective-permute-start | bytes 3145736 | tf_op jit(solution)/shard_map/ppermute | solution.py:914
  486.9 77.5 %collective-permute-start.43 = (bf16[512,1536]{1,0:T(8,128)(2,1)}, bf16[512,1536]{1,0:T(8,128)(2,1)}, u32[]{:S(2)}, u32[]{:S(2)}) collective-permute-start(bf16[512,1536]{1,0:T(8,128)(2,1)} %get-tuple-element.346), channel_id=1, source_target_pairs={{0,4},{1,5},{2,6},{3,7},{4,0},{5,1},{6,2},{7,3},{8,12},{9,13},{10,... | collective-permute-start | bytes 4718600 | tf_op jit(solution)/shard_map/ppermute | solution.py:914
  571.9 50.6 %collective-permute-start.45 = (bf16[2,2,2,32,1536]{4,3,2,1,0:T(8,128)(2,1)}, bf16[2,2,2,32,1536]{4,3,2,1,0:T(8,128)(2,1)S(1)}, u32[]{:S(2)}, u32[]{:S(2)}) collective-permute-start(bf16[2,2,2,32,1536]{4,3,2,1,0:T(8,128)(2,1)} %fusion.8), channel_id=1, source_target_pairs={{0,1},{1,0},{2,3},{3,2},{4,5},{5,4},{6,7},{7,6},{8,9},{9,8},{10,11... | collective-permute-start | bytes 2359304 | tf_op jit(solution)/shard_map/ppermute | solution.py:914
  572.0 50.5 %collective-permute-start.44 = (bf16[32,8192]{1,0:T(8,128)(2,1)S(1)}, bf16[32,8192]{1,0:T(8,128)(2,1)S(1)}, u32[]{:S(2)}, u32[]{:S(2)}) collective-permute-start(bf16[32,8192]{1,0:T(8,128)(2,1)S(1)} %pad_maximum_fusion.9), channel_id=1, source_target_pairs={{0,16},{1,17},{2,18},{3,19},{4,20},{5,21},{6,22},{7,23},{8,24},{9,... | collective-permute-start | bytes 1572872 | tf_op jit(solution)/shard_map/ppermute | solution.py:914
  576.8 45.0 %collective-permute-start.47 = (bf16[160,1024]{1,0:T(8,128)(2,1)S(1)}, bf16[160,1024]{1,0:T(8,128)(2,1)}, u32[]{:S(2)}, u32[]{:S(2)}) collective-permute-start(bf16[160,1024]{1,0:T(8,128)(2,1)S(1)} %copy-done.36), channel_id=1, source_target_pairs={{0,16},{1,17},{2,18},{3,19},{4,20},{5,21},{6,22},{7,23},{8,24},{9,... | collective-permute-start | bytes 983048 | tf_op jit(solution)/shard_map/ppermute | solution.py:914
  576.9 45.5 %collective-permute-start.48 = (bf16[160,1024]{1,0:T(8,128)(2,1)S(1)}, bf16[160,1024]{1,0:T(8,128)(2,1)}, u32[]{:S(2)}, u32[]{:S(2)}) collective-permute-start(bf16[160,1024]{1,0:T(8,128)(2,1)S(1)} %get-tuple-element.358), channel_id=1, source_target_pairs={{0,18},{1,19},{2,16},{3,17},{4,22},{5,23},{6,20},{7,21},{8,26},{9,... | collective-permute-start | bytes 983048 | tf_op jit(solution)/shard_map/ppermute | solution.py:914
  642.9 48.0 %collective-permute-start.49 = (bf16[256,1024]{1,0:T(8,128)(2,1)}, bf16[256,1024]{1,0:T(8,128)(2,1)S(1)}, u32[]{:S(2)}, u32[]{:S(2)}) collective-permute-start(bf16[256,1024]{1,0:T(8,128)(2,1)} %get-tuple-element.360), channel_id=1, source_target_pairs={{0,0},{1,1},{4,2},{5,3},{2,4},{3,5},{6,6},{7,7},{8,8},{9,9},{12,10... | collective-permute-start | bytes 1572872 | tf_op jit(solution)/shard_map/ppermute | solution.py:892
  646.4 41.5 %collective-permute-start.55 = (bf16[2,2,32,1664]{3,2,1,0:T(8,128)(2,1)S(1)}, bf16[2,2,32,1664]{3,2,1,0:T(8,128)(2,1)S(1)}, u32[]{:S(2)}, u32[]{:S(2)}) collective-permute-start(bf16[2,2,32,1664]{3,2,1,0:T(8,128)(2,1)S(1)} %get-tuple-element.370), channel_id=1, source_target_pairs={{0,2},{1,3},{2,0},{3,1},{4,6},{5,7},{6,4},{7,5},{8,10},{9,11},{10,... | collective-permute-start | bytes 1277960 | tf_op jit(solution)/shard_map/ppermute | solution.py:914
  648.5 39.8 %collective-permute-start.56 = (bf16[2,2,32,1664]{3,2,1,0:T(8,128)(2,1)S(1)}, bf16[2,2,32,1664]{3,2,1,0:T(8,128)(2,1)S(1)}, u32[]{:S(2)}, u32[]{:S(2)}) collective-permute-start(bf16[2,2,32,1664]{3,2,1,0:T(8,128)(2,1)S(1)} %get-tuple-element.371), channel_id=1, source_target_pairs={{0,3},{1,2},{2,1},{3,0},{4,7},{5,6},{6,5},{7,4},{8,11},{9,10},{10,... | collective-permute-start | bytes 1277960 | tf_op jit(solution)/shard_map/ppermute | solution.py:914
  653.0 41.0 %collective-permute-start.50 = (bf16[256,1024]{1,0:T(8,128)(2,1)S(1)}, bf16[256,1024]{1,0:T(8,128)(2,1)S(1)}, u32[]{:S(2)}, u32[]{:S(2)}) collective-permute-start(bf16[256,1024]{1,0:T(8,128)(2,1)S(1)} %copy-done.29), channel_id=1, source_target_pairs={{4,0},{5,1},{0,2},{1,3},{6,4},{7,5},{2,6},{3,7},{12,8},{13,9},{8,1... | collective-permute-start | bytes 1572872 | tf_op jit(solution)/shard_map/ppermute | solution.py:892
  657.7 41.7 %collective-permute-start.51 = (bf16[256,1024]{1,0:T(8,128)(2,1)S(1)}, bf16[256,1024]{1,0:T(8,128)(2,1)S(1)}, u32[]{:S(2)}, u32[]{:S(2)}) collective-permute-start(bf16[256,1024]{1,0:T(8,128)(2,1)S(1)} %copy-done.28), channel_id=1, source_target_pairs={{1,0},{0,1},{5,2},{4,3},{3,4},{2,5},{7,6},{6,7},{9,8},{8,9},{13,10... | collective-permute-start | bytes 1572872 | tf_op jit(solution)/shard_map/ppermute | solution.py:892
  (84 other events, 1127.9 us)
Sparse Core Ops, SparseCore 0:
  44.8 199.2 all-gather.2

commit v4 on v3

--- a/solution.py
+++ b/solution.py
@@ -840,9 +840,9 @@
         dp_bits = list(range(self.core + 1, self.bits))
         self.dp_bits = [self.core] + dp_bits
         first, last = dp_bits[:1], dp_bits[1:]
-        self.seq_first = [[b] for b in seq_bits + dp_bits]
-        self.seq_last = [[b] for b in seq_bits[::-1] + dp_bits]
-        self.dp_first = [first, seq_bits[:1], seq_bits[1:] + last]
+        self.seq_first = [[b] for b in seq_bits + dp_bits[::-1]]
+        self.seq_last = [[b] for b in seq_bits[::-1] + dp_bits[::-1]]
+        self.dp_first = [[b] for b in first + seq_bits + last]
         self.seq_then = [seq_bits[:1], seq_bits[1:], dp_bits]
         self.direct = [seq_bits, dp_bits]
         self.orders = [
@@ -1103,38 +1103,32 @@
     grad_heads = begin([sum_up.hold(output)], tie(list(grad_heads), output))
     made = back(0, grad_heads)
     received = links.exchange(made)
-    chains = [sum_rest, sum_gate, sum_up]
-    finish(chains, made)
-    received = begin(chains, tie(list(received), made))
+    finish([sum_rest, sum_gate, sum_up], made)
+    received = begin([sum_gate, sum_up], tie(list(received), made))
     low = unturn(scalar(member), received, table, team)
     own_one, away_one = weight_grad(core, normed_one, low, narrow)
     sum_one = Chain(links, own_one, away_one, links.seq_then)
     (partial,) = through(0, tie(low, own_one), [])
-    sum_one.hold(partial)
+    finish([sum_gate, sum_up], partial)
     if len(links.seq_first) == 4:
         sum_pair = [Joined(sum_gate, sum_up)]
     else:
         sum_pair = [sum_gate, sum_up]
-    subs = 2 if lanes // 128 // PARTS > 1 else 1
-    made = back(1, tie(list(grad_heads), partial), 0, subs)
-    received = list(links.exchange(made))
+    grad_heads = begin(sum_pair + [sum_rest], tie(list(grad_heads), partial))
+    made = back(1, grad_heads)
+    received = links.exchange(made)
+    chains = sum_pair + [sum_rest]
     finish(chains, made)
-    if subs > 1:
-        grad_heads = begin(sum_pair + [sum_rest], tie(list(grad_heads), made))
-        made = back(1, grad_heads, 1, subs)
-        received += links.exchange(made)
-    else:
-        received = begin(sum_pair + [sum_rest], received)
-    finish(sum_pair, made)
-    received = begin(sum_pair + [sum_one], tie(received, made))
+    chains.append(sum_one.hold(partial))
+    received = begin(chains, tie(list(received), made))
     low = unturn(scalar(member), received, table, team)
     grad_in, sums_one = through(1, low, [partial])
-    finish(sum_pair + [sum_one, sum_rest], grad_in)
-    chains = [c for c in sum_pair + [sum_one] if c.rounds]
+    finish(chains, grad_in)
+    chains = [c for c in chains if c.rounds]
     low, sent = begin(chains, (low, links.from_team_blocks(grad_in)))
-    home = [links.back_one(v, k) for k, v in enumerate(sent)]
+    home = [links.back_one(v, k) for k, v in enumerate(sent[:2])]
     own_two, away_two = weight_grad(core, normed_one, low, narrow)
-    finish(chains, own_two)
+    pending = chains
     gains = jnp.concatenate([sums_one, sums_two], axis=0)
     gains = gains.reshape(4, links.dp // 2, 2, width // links.dp).transpose(2, 1, 3, 0)
     gains = gains.reshape(2, width // 2, 4)
@@ -1142,12 +1136,13 @@
     gains = [
         lax.dynamic_index_in_dim(gains, c, 0, keepdims=False) for c in (core[0], 1 - core[0])
     ]
+    (own_two, away_two, gains), home = lax.optimization_barrier(((own_two, away_two, gains), home))
     own = jnp.concatenate([own_two, gains[0]], axis=1)
     away = jnp.concatenate([away_two, gains[1]], axis=1)
     last = Chain(links, own, away, links.direct)
-    chains = [c for c in sum_pair + [sum_rest, last] if c.rounds]
-    nothing = begin(chains, [])
-    finish(chains, nothing)
+    nothing = begin([last], [])
+    finish(pending + [last], nothing)
+    home += [links.back_one(v, k) for k, v in enumerate(tie(sent[2:], last.terms), 2)]
     pieces = [c for c in sum_pair + [sum_rest] if c.rounds]
     chains = pieces + [Joined(sum_one, last)]
     while chains:

time: 733 us -> 694 us (0.947)
  waiting for transfers between devices: 130 us -> 104 us
  starting transfers between devices: 80.2 us -> 72.1 us
    ppermute x45 -> x43, waiting for transfers between devices: 99.6 us -> 72.9 us  [swap(): return lax.ppermute(value, BOTH, [(i, i ^ mask) for i in range(self.count)])]
    ppermute x45 -> x43, starting transfers between devices: 59.8 us -> 47.2 us  [swap(): return lax.ppermute(value, BOTH, [(i, i ^ mask) for i in range(self.count)])]
    convert_element_type x16 -> x17, other arithmetic: 39.8 us -> 44 us  [split(): sent = [total(self.pick(m)).astype(self.wire) for m in self.masks[1:]]]
    pallas_call x3 -> x2, Pallas kernels: 109 us -> 107 us  [attend_back(): pl.pallas_call(functools.partial(attend_back_kernel, team=team), grid_spe...]
  transfers between devices with their start and end apart: 62 -> 60, of which waited for: 23 -> 23; matrix products, arithmetic and copies ran while one was open for 8% -> 9% of each run, Pallas kernels for 43% -> 45%
where the time goes in v4:
time: 694 us; the launch traced here: 685 us
  Pallas kernels  398 us (57%)
  waiting for transfers between devices  104 us (15%)
  starting transfers between devices  72.1 us (10%)
  other arithmetic  70.3 us (10%)
  local copies, waits for them, and re-layouts  24.5 us (4%)
  between operations  16.4 us (2%)
    pallas_call x2, Pallas kernels, attend_back(): pl.pallas_call(functools.partial(attend_back_kernel, team=team), grid_spe...  107 us
    pallas_call x1, Pallas kernels, feed(): pl.pallas_call(functools.partial(feed_kernel, team=team), grid_spec=pltpu...  79 us
    ppermute x43, waiting for transfers between devices, swap(): return lax.ppermute(value, BOTH, [(i, i ^ mask) for i in range(self.count)])  72.9 us
    pallas_call x2, Pallas kernels, attend(): pl.pallas_call(functools.partial(attend_kernel, team=team), grid_spec=plt...  66.3 us
    pallas_call x6, Pallas kernels, weight_grad(): pl.pallas_call(functools.partial(weight_kernel, size=chunk), grid_spec=pl...  61.5 us
    ppermute x43, starting transfers between devices, swap(): return lax.ppermute(value, BOTH, [(i, i ^ mask) for i in range(self.count)])  47.2 us
    convert_element_type x17, other arithmetic, split(): sent = [total(self.pick(m)).astype(self.wire) for m in self.masks[1:]]  44 us
    ppermute x8, waiting for transfers between devices, move_one(): return lax.ppermute(sent, BOTH, self.route(k))  28 us
  transfers between devices with their start and end apart: 60, of which 23 were waited for; matrix products, arithmetic and copies ran while one was open for 9% of the time, Pallas kernels for 45%

profile of v4, /device:TPU:0, one launch (start us, length us, event | category | flops | bytes accessed | tf_op | source)
XLA Modules:
  0.0 685.2 jit_solution(17875179597920584967)
XLA Ops:
  19.9 6.9 %collective-permute-done = bf16[1,32,1536]{2,1,0:T(8,128)(2,1)S(1)} collective-permute-done((bf16[1,32,1536]{2,1,0:T(8,128)(2,1)S(1)}, bf16[1,32,1536]{2,1,0:T(8,128)(2,1)S(1)}, u32[]{:S(2)}, u32[]{:S(2)}) %collective-permute-start) | collective-permute-done | bytes 98336 | tf_op jit(solution)/shard_map/ppermute | solution.py:914
  62.6 20.8 %collective-permute-done.11 = bf16[8,32,1536]{2,1,0:T(8,128)(2,1)S(1)} collective-permute-done((bf16[8,32,1536]{2,1,0:T(8,128)(2,1)S(1)}, bf16[8,32,1536]{2,1,0:T(8,128)(2,1)S(1)}, u32[]{:S(2)}, u32[]{:S(2)}) %collective-permute-start.11) | collective-permute-done | bytes 786464 | tf_op jit(solution)/shard_map/ppermute | solution.py:914
  84.8 18.3 %collective-permute-done.13.refs_2_ = bf16[256,1024]{1,0:T(8,128)(2,1)S(1)} collective-permute-done((bf16[256,1024]{1,0:T(8,128)(2,1)}, bf16[256,1024]{1,0:T(8,128)(2,1)S(1)}, u32[]{:S(2)}, u32[]{:S(2)}) %collective-permute-start.13) | collective-permute-done | bytes 524320 | tf_op jit(solution)/shard_map/ppermute | solution.py:879
  112.8 7.5 %place.1 = (bf16[3,32,32,1024]{3,2,1,0:T(8,128)(2,1)}, bf16[32,32,128]{2,1,0:T(8,128)(2,1)}) custom-call(s32[1]{0:T(128)} %bitcast.15.me_ref, bf16[16,32,1536]{2,1,0:T(8,128)(2,1)} %copy-done.2, bf16[16,32,1536]{2,1,0:T(8,128)(2,1)} %collective-permute-done.15.refs_1_, bf16[16,32,1664]{2,1,0:T(8,128)(2,1)} %copy-done.1, ...), custom_call_target="tpu_custom_call" | custom-call | tf_op jit(solution)/shard_map/place/pallas_call | solution.py:948
  122.2 12.3 %project.3 = (bf16[3,1024,512]{2,1,0:T(8,128)(2,1)}, bf16[1024,1024]{1,0:T(8,128)(2,1)}) custom-call(s32[1]{0:T(128)} %bitcast.19.at_ref, bf16[1024,1024]{1,0:T(8,128)(2,1)} %bitcast.316, bf16[3,1024,1024]{2,1,0:T(8,128)(2,1)} %bitcast.312, f32[4,1024]{1,0:T(4,128)} %bitcast.354, f32[1024,128]{1,0:T(8,128)} %pad_maximum_fusion.7.c_ref, ...), custom_call_target="tpu_custom_call" | custom-call | flops 50331648 | bytes 98304 | tf_op jit(solution)/shard_map/project/pallas_call | solution.py:151
  137.8 12.9 %project.2 = (bf16[3,1024,512]{2,1,0:T(8,128)(2,1)}, bf16[1024,1024]{1,0:T(8,128)(2,1)}) custom-call(s32[1]{0:T(128)} %bitcast.1.at_ref, bf16[1024,1024]{1,0:T(8,128)(2,1)} %bitcast.317, bf16[3,1024,1024]{2,1,0:T(8,128)(2,1)} %bitcast.313, f32[4,1024]{1,0:T(4,128)} %bitcast.355, f32[1024,128]{1,0:T(8,128)} %pad_maximum_fusion.7.c_ref, ...), custom_call_target="tpu_custom_call" | custom-call | flops 50331648 | bytes 98304 | tf_op jit(solution)/shard_map/project/pallas_call | solution.py:151
  163.8 33.3 %attend.2 = (bf16[1024,256]{1,0:T(8,128)(2,1)}, bf16[1024,256]{1,0:T(8,128)(2,1)}, f32[2,2,2048]{2,1,0:T(2,128)}) custom-call(s32[3]{0:T(128)} %pad_add_fusion.1.info_ref, bf16[3,1024,512]{2,1,0:T(8,128)(2,1)} %get-tuple-element.250.refs_0_.refs_2_.refs_4_, bf16[3,1024,512]{2,1,0:T(8,128)(2,1)} %copy-done, ...), custom_call_target="tpu_custom_call" | custom-call | flops 268435456 | bytes 65536 | tf_op jit(solution)/shard_map/attend/pallas_call | solution.py:255
  204.0 33.0 %attend.3 = (bf16[1024,256]{1,0:T(8,128)(2,1)}, bf16[1024,256]{1,0:T(8,128)(2,1)}, f32[2,2,2048]{2,1,0:T(2,128)}) custom-call(s32[3]{0:T(128)} %pad_add_fusion.1.info_ref, bf16[3,1024,512]{2,1,0:T(8,128)(2,1)} %get-tuple-element.250.refs_0_.refs_2_.refs_4_, bf16[3,1024,512]{2,1,0:T(8,128)(2,1)} %copy-done, ...), custom_call_target="tpu_custom_call" | custom-call | flops 268435456 | bytes 65536 | tf_op jit(solution)/shard_map/attend/pallas_call | solution.py:255
  246.1 79.0 %feed.1 = (bf16[1024,512]{1,0:T(8,128)(2,1)}, bf16[1024,512]{1,0:T(8,128)(2,1)}, bf16[1024,1024]{1,0:T(8,128)(2,1)}, f32[1024,1024]{1,0:T(8,128)}, bf16[1024,102...) custom-call(s32[1]{0:T(128)} %bitcast.1.at_ref, ...), custom_call_target="tpu_custom_call" | custom-call | flops 872415232 | bytes 1671168 | tf_op jit(solution)/shard_map/feed/pallas_call | solution.py:514
  327.6 13.2 %weight_grad.6 = (bf16[16,160,1024]{2,1,0:T(8,128)(2,1)}, bf16[16,160,1024]{2,1,0:T(8,128)(2,1)}) custom-call(s32[1]{0:T(128)} %bitcast.36.core_ref, bf16[1024,4096]{1,0:T(8,128)(2,1)} %get-tuple-element.255.a_ref, bf16[1024,1024]{1,0:T(8,128)(2,1)} %get-tuple-element.258.b_ref), custom_call_target="tpu_custom_call" | custom-call | flops 134217728 | bytes 294912 | tf_op jit(solution)/shard_map/weight_grad/pallas_call | solution.py:605
  340.8 6.3 weight_grad.7
  351.5 13.6 %weight_grad.8 = (bf16[512,4096]{1,0:T(8,128)(2,1)}, bf16[512,4096]{1,0:T(8,128)(2,1)}) custom-call(s32[1]{0:T(128)} %bitcast.36.core_ref, bf16[1024,1024]{1,0:T(8,128)(2,1)} %get-tuple-element.275.a_ref, bf16[1024,4096]{1,0:T(8,128)(2,1)} %get-tuple-element.277.b_ref), custom_call_target="tpu_custom_call" | custom-call | flops 134217728 | bytes 294912 | tf_op jit(solution)/shard_map/weight_grad/pallas_call | solution.py:605
  365.4 5.7 fusion
  371.2 13.4 %weight_grad.9 = (bf16[512,4096]{1,0:T(8,128)(2,1)}, bf16[512,4096]{1,0:T(8,128)(2,1)}) custom-call(s32[1]{0:T(128)} %bitcast.36.core_ref, bf16[1024,1024]{1,0:T(8,128)(2,1)} %get-tuple-element.275.a_ref, bf16[1024,4096]{1,0:T(8,128)(2,1)} %get-tuple-element.283.b_ref), custom_call_target="tpu_custom_call" | custom-call | flops 134217728 | bytes 294912 | tf_op jit(solution)/shard_map/weight_grad/pallas_call | solution.py:605
  404.3 53.3 %attend_back.2 = (bf16[3,1024,256]{2,1,0:T(8,128)(2,1)}, bf16[3,1024,256]{2,1,0:T(8,128)(2,1)}) custom-call(s32[3]{0:T(128)} %pad_add_fusion.1.info_ref, bf16[3,1024,512]{2,1,0:T(8,128)(2,1)} %get-tuple-element.250.refs_0_.refs_2_.refs_4_, bf16[3,1024,512]{2,1,0:T(8,128)(2,1)} %copy-done, bf16[3,1024,512]{2,1,0:T(8,128)(2,1)} %get-tuple-element.250.refs_0_.refs_2_.refs_4_, ...), custom_call_target="tpu_custom_call" | custom-call | flops 503316480 | bytes 131072 | tf_op jit(solution)/shard_map/attend_back/pallas_call | solution.py:396
  467.1 5.7 unturn.2.b_ref.low_ref
  472.8 7.3 %weight_grad.10 = (bf16[512,1536]{1,0:T(8,128)(2,1)}, bf16[512,1536]{1,0:T(8,128)(2,1)}) custom-call(s32[1]{0:T(128)} %bitcast.36.core_ref, bf16[1024,1024]{1,0:T(8,128)(2,1)} %get-tuple-element.289.a_ref, bf16[3,1024,512]{2,1,0:T(8,128)(2,1)} %unturn.2.b_ref.low_ref), custom_call_target="tpu_custom_call" | custom-call | flops 50331648 | bytes 131072 | tf_op jit(solution)/shard_map/weight_grad/pallas_call | solution.py:605
  480.2 10.4 %project_back.2.refs_0_ = f32[1024,1024]{1,0:T(8,128)} custom-call(bf16[1024,1024]{1,0:T(8,128)(2,1)} %bitcast.319, f32[1024,1024]{1,0:T(8,128)} %get-tuple-element.306.gm_ref, f32[4,1024]{1,0:T(4,128)} %bitcast.357, bf16[3,1024,1024]{2,1,0:T(8,128)(2,1)} %bitcast.314, bf16[3,1024,512]{2,1,0:T(8,128)(2,1)} %unturn.2.b_ref.low_ref), custom_call_target="tpu_custom_call" | custom-call | flops 50331648 | bytes 393216 | tf_op jit(solution)/shard_map/project_back/pallas_call | solution.py:699
  502.9 53.7 %attend_back.3 = (bf16[3,1024,256]{2,1,0:T(8,128)(2,1)}, bf16[3,1024,256]{2,1,0:T(8,128)(2,1)}) custom-call(s32[3]{0:T(128)} %pad_add_fusion.1.info_ref, bf16[3,1024,512]{2,1,0:T(8,128)(2,1)} %get-tuple-element.250.refs_0_.refs_2_.refs_4_, bf16[3,1024,512]{2,1,0:T(8,128)(2,1)} %copy-done, bf16[3,1024,512]{2,1,0:T(8,128)(2,1)} %get-tuple-element.250.refs_0_.refs_2_.refs_4_, ...), custom_call_target="tpu_custom_call" | custom-call | flops 503316480 | bytes 131072 | tf_op jit(solution)/shard_map/attend_back/pallas_call | solution.py:396
  569.0 5.7 unturn.3.low_ref.b_ref
  574.7 14.1 %project_back.3 = (bf16[1024,1024]{1,0:T(8,128)(2,1)}, f32[2,1024]{1,0:T(2,128)}) custom-call(bf16[1024,1024]{1,0:T(8,128)(2,1)} %bitcast.320, f32[1024,1024]{1,0:T(8,128)} %get-tuple-element.306.gm_ref, f32[4,1024]{1,0:T(4,128)} %bitcast.358, bf16[3,1024,1024]{2,1,0:T(8,128)(2,1)} %bitcast.315, bf16[3,1024,512]{2,1,0:T(8,128)(2,1)} %unturn.3.low_ref.b_ref, ...), custom_call_target="tpu_custom_call" | custom-call | flops 50331648 | bytes 393216 | tf_op jit(solution)/shard_map/project_back/pallas_call | solution.py:699
  603.7 7.5 %weight_grad.11 = (bf16[512,1536]{1,0:T(8,128)(2,1)}, bf16[512,1536]{1,0:T(8,128)(2,1)}) custom-call(s32[1]{0:T(128)} %bitcast.36.core_ref, bf16[1024,1024]{1,0:T(8,128)(2,1)} %get-tuple-element.289.a_ref, bf16[3,1024,512]{2,1,0:T(8,128)(2,1)} %unturn.3.low_ref.b_ref), custom_call_target="tpu_custom_call" | custom-call | flops 50331648 | bytes 131072 | tf_op jit(solution)/shard_map/weight_grad/pallas_call | solution.py:605
  636.4 10.9 %collective-permute-done.52 = bf16[2,2,32,1664]{3,2,1,0:T(8,128)(2,1)S(1)} collective-permute-done((bf16[2,2,32,1664]{3,2,1,0:T(8,128)(2,1)S(1)}, bf16[2,2,32,1664]{3,2,1,0:T(8,128)(2,1)S(1)}, u32[]{:S(2)}, u32[]{:S(2)}) %collective-permute-start.52) | collective-permute-done | bytes 426016 | tf_op jit(solution)/shard_map/ppermute | solution.py:914
  660.2 7.6 %collective-permute-done.57 = bf16[32,3200]{1,0:T(8,128)(2,1)S(1)} collective-permute-done((bf16[32,3200]{1,0:T(8,128)(2,1)S(1)}, bf16[32,3200]{1,0:T(8,128)(2,1)S(1)}, u32[]{:S(2)}, u32[]{:S(2)}) %collective-permute-start.57) | collective-permute-done | bytes 204832 | tf_op jit(solution)/shard_map/ppermute | solution.py:914
  (273 shorter events, 216.2 us)
Async XLA Ops:
  7.2 238.0 %all-gather.3.cloned.1.call-start = ((), (), s32[]{:S(2)}) async-start(), calls=%async_computation | async-start | bytes 28114944 | tf_op jit(solution)/shard_map/all_gather | solution.py:1032
  58.9 24.5 %collective-permute-start.11 = (bf16[8,32,1536]{2,1,0:T(8,128)(2,1)S(1)}, bf16[8,32,1536]{2,1,0:T(8,128)(2,1)S(1)}, u32[]{:S(2)}, u32[]{:S(2)}) collective-permute-start(bf16[8,32,1536]{2,1,0:T(8,128)(2,1)S(1)} %pad_maximum_fusion.6), channel_id=1, source_target_pairs={{0,1},{1,0},{2,3},{3,2},{4,5},{5,4},{6,7},{7,6},{8,9},{9,8},{10,11... | collective-permute-start | bytes 2359304 | tf_op jit(solution)/shard_map/ppermute | solution.py:914
  61.0 23.6 %collective-permute-start.12 = (bf16[8,32,1664]{2,1,0:T(8,128)(2,1)S(1)}, bf16[8,32,1664]{2,1,0:T(8,128)(2,1)S(1)}, u32[]{:S(2)}, u32[]{:S(2)}) collective-permute-start(bf16[8,32,1664]{2,1,0:T(8,128)(2,1)S(1)} %pad_maximum_fusion.5), channel_id=1, source_target_pairs={{0,2},{1,3},{2,0},{3,1},{4,6},{5,7},{6,4},{7,5},{8,10},{9,11},{10,... | collective-permute-start | bytes 2555912 | tf_op jit(solution)/shard_map/ppermute | solution.py:914
  62.6 40.5 %collective-permute-start.13 = (bf16[256,1024]{1,0:T(8,128)(2,1)}, bf16[256,1024]{1,0:T(8,128)(2,1)S(1)}, u32[]{:S(2)}, u32[]{:S(2)}) collective-permute-start(bf16[256,1024]{1,0:T(8,128)(2,1)} %get-tuple-element.216), channel_id=1, source_target_pairs={{0,4},{1,5},{2,0},{3,1},{4,6},{5,7},{6,2},{7,3},{8,12},{9,13},{10,... | collective-permute-start | bytes 1572872 | tf_op jit(solution)/shard_map/ppermute | solution.py:879
  62.6 40.5 %collective-permute-start.14 = (bf16[256,1024]{1,0:T(8,128)(2,1)}, bf16[256,1024]{1,0:T(8,128)(2,1)S(1)}, u32[]{:S(2)}, u32[]{:S(2)}) collective-permute-start(bf16[256,1024]{1,0:T(8,128)(2,1)} %get-tuple-element.217), channel_id=1, source_target_pairs={{0,5},{1,4},{2,1},{3,0},{4,7},{5,6},{6,3},{7,2},{8,13},{9,12},{10,... | collective-permute-start | bytes 1572872 | tf_op jit(solution)/shard_map/ppermute | solution.py:879
  150.7 46.6 %collective-permute-start.18 = (bf16[256,1024]{1,0:T(8,128)(2,1)}, bf16[256,1024]{1,0:T(8,128)(2,1)}, u32[]{:S(2)}, u32[]{:S(2)}) collective-permute-start(bf16[256,1024]{1,0:T(8,128)(2,1)} %get-tuple-element.230), channel_id=1, source_target_pairs={{0,0},{1,1},{2,4},{3,5},{4,2},{5,3},{6,6},{7,7},{8,8},{9,9},{10,12... | collective-permute-start | bytes 1572872 | tf_op jit(solution)/shard_map/ppermute | solution.py:879
  156.2 41.2 %collective-permute-start.19 = (bf16[256,1024]{1,0:T(8,128)(2,1)}, bf16[256,1024]{1,0:T(8,128)(2,1)}, u32[]{:S(2)}, u32[]{:S(2)}) collective-permute-start(bf16[256,1024]{1,0:T(8,128)(2,1)} %get-tuple-element.231), channel_id=1, source_target_pairs={{0,1},{1,0},{2,5},{3,4},{4,3},{5,2},{6,7},{7,6},{8,9},{9,8},{10,13... | collective-permute-start | bytes 1572872 | tf_op jit(solution)/shard_map/ppermute | solution.py:879
  158.4 41.7 %collective-permute-start.20 = (bf16[256,1024]{1,0:T(8,128)(2,1)}, bf16[256,1024]{1,0:T(8,128)(2,1)}, u32[]{:S(2)}, u32[]{:S(2)}) collective-permute-start(bf16[256,1024]{1,0:T(8,128)(2,1)} %get-tuple-element.232), channel_id=1, source_target_pairs={{0,4},{1,5},{2,0},{3,1},{4,6},{5,7},{6,2},{7,3},{8,12},{9,13},{10,... | collective-permute-start | bytes 1572872 | tf_op jit(solution)/shard_map/ppermute | solution.py:879
  158.4 45.6 %collective-permute-start.21 = (bf16[256,1024]{1,0:T(8,128)(2,1)}, bf16[256,1024]{1,0:T(8,128)(2,1)}, u32[]{:S(2)}, u32[]{:S(2)}) collective-permute-start(bf16[256,1024]{1,0:T(8,128)(2,1)} %get-tuple-element.233), channel_id=1, source_target_pairs={{0,5},{1,4},{2,1},{3,0},{4,7},{5,6},{6,3},{7,2},{8,13},{9,12},{10,... | collective-permute-start | bytes 1572872 | tf_op jit(solution)/shard_map/ppermute | solution.py:879
  197.1 48.0 %collective-permute-start.23 = (bf16[1024,256]{1,0:T(8,128)(2,1)}, bf16[1024,256]{1,0:T(8,128)(2,1)S(1)}, u32[]{:S(2)}, u32[]{:S(2)}) collective-permute-start(bf16[1024,256]{1,0:T(8,128)(2,1)} %get-tuple-element.249.refs_7_), channel_id=1, source_target_pairs={{0,4},{1,5},{2,6},{3,7},{4,0},{5,1},{6,2},{7,3},{8,12},{9,13},{10,... | collective-permute-start | bytes 1572872 | tf_op jit(solution)/shard_map/ppermute | solution.py:914
  365.1 20.0 %collective-permute-start.31 = (bf16[512,4096]{1,0:T(8,128)(2,1)}, bf16[512,4096]{1,0:T(8,128)(2,1)}, u32[]{:S(2)}, u32[]{:S(2)}) collective-permute-start(bf16[512,4096]{1,0:T(8,128)(2,1)} %get-tuple-element.294), channel_id=1, source_target_pairs={{0,4},{1,5},{2,6},{3,7},{4,0},{5,1},{6,2},{7,3},{8,12},{9,13},{10,... | collective-permute-start | bytes 12582920 | tf_op jit(solution)/shard_map/ppermute | solution.py:914
  385.1 76.4 %collective-permute-start.34 = (bf16[2,2,2,160,1024]{4,3,2,1,0:T(8,128)(2,1)}, bf16[2,2,2,160,1024]{4,3,2,1,0:T(8,128)(2,1)}, u32[]{:S(2)}, u32[]{:S(2)}) collective-permute-start(bf16[2,2,2,160,1024]{4,3,2,1,0:T(8,128)(2,1)} %fusion), channel_id=1, source_target_pairs={{0,8},{1,9},{2,10},{3,11},{4,12},{5,13},{6,14},{7,15},{8,0},{9,1},... | collective-permute-start | bytes 7864328 | tf_op jit(solution)/shard_map/ppermute | solution.py:914
  396.9 64.6 %collective-permute-start.35 = (bf16[2,2,2,32,4096]{4,3,2,1,0:T(8,128)(2,1)}, bf16[2,2,2,32,4096]{4,3,2,1,0:T(8,128)(2,1)S(1)}, u32[]{:S(2)}, u32[]{:S(2)}) collective-permute-start(bf16[2,2,2,32,4096]{4,3,2,1,0:T(8,128)(2,1)} %fusion.2), channel_id=1, source_target_pairs={{0,1},{1,0},{2,3},{3,2},{4,5},{5,4},{6,7},{7,6},{8,9},{9,8},{10,11... | collective-permute-start | bytes 6291464 | tf_op jit(solution)/shard_map/ppermute | solution.py:914
  402.8 58.8 %collective-permute-start.36 = (bf16[2,2,2,32,4096]{4,3,2,1,0:T(8,128)(2,1)}, bf16[2,2,2,32,4096]{4,3,2,1,0:T(8,128)(2,1)}, u32[]{:S(2)}, u32[]{:S(2)}) collective-permute-start(bf16[2,2,2,32,4096]{4,3,2,1,0:T(8,128)(2,1)} %fusion.3), channel_id=1, source_target_pairs={{0,2},{1,3},{2,0},{3,1},{4,6},{5,7},{6,4},{7,5},{8,10},{9,11},{10,... | collective-permute-start | bytes 6291464 | tf_op jit(solution)/shard_map/ppermute | solution.py:914
  466.9 27.7 %collective-permute-start.37 = (bf16[2,2,32,4096]{3,2,1,0:T(8,128)(2,1)}, bf16[2,2,32,4096]{3,2,1,0:T(8,128)(2,1)}, u32[]{:S(2)}, u32[]{:S(2)}) collective-permute-start(bf16[2,2,32,4096]{3,2,1,0:T(8,128)(2,1)} %fusion.5), channel_id=1, source_target_pairs={{0,2},{1,3},{2,0},{3,1},{4,6},{5,7},{6,4},{7,5},{8,10},{9,11},{10,... | collective-permute-start | bytes 3145736 | tf_op jit(solution)/shard_map/ppermute | solution.py:914
  467.0 27.7 %collective-permute-start.38 = (bf16[2,2,32,4096]{3,2,1,0:T(8,128)(2,1)S(1)}, bf16[2,2,32,4096]{3,2,1,0:T(8,128)(2,1)}, u32[]{:S(2)}, u32[]{:S(2)}) collective-permute-start(bf16[2,2,32,4096]{3,2,1,0:T(8,128)(2,1)S(1)} %fusion.4), channel_id=1, source_target_pairs={{0,1},{1,0},{2,3},{3,2},{4,5},{5,4},{6,7},{7,6},{8,9},{9,8},{10,11... | collective-permute-start | bytes 3145736 | tf_op jit(solution)/shard_map/ppermute | solution.py:914
  480.1 76.7 %collective-permute-start.42 = (bf16[512,1536]{1,0:T(8,128)(2,1)}, bf16[512,1536]{1,0:T(8,128)(2,1)}, u32[]{:S(2)}, u32[]{:S(2)}) collective-permute-start(bf16[512,1536]{1,0:T(8,128)(2,1)} %get-tuple-element.338), channel_id=1, source_target_pairs={{0,4},{1,5},{2,6},{3,7},{4,0},{5,1},{6,2},{7,3},{8,12},{9,13},{10,... | collective-permute-start | bytes 4718600 | tf_op jit(solution)/shard_map/ppermute | solution.py:914
  498.3 60.6 %collective-permute-start.41 = (bf16[2,2,160,1024]{3,2,1,0:T(8,128)(2,1)}, bf16[2,2,160,1024]{3,2,1,0:T(8,128)(2,1)}, u32[]{:S(2)}, u32[]{:S(2)}) collective-permute-start(bf16[2,2,160,1024]{3,2,1,0:T(8,128)(2,1)} %fusion.1), channel_id=1, source_target_pairs={{0,1},{1,0},{2,3},{3,2},{4,5},{5,4},{6,7},{7,6},{8,9},{9,8},{10,11... | collective-permute-start | bytes 3932168 | tf_op jit(solution)/shard_map/ppermute | solution.py:914
  500.2 58.8 %collective-permute-start.40 = (bf16[2,32,8192]{2,1,0:T(8,128)(2,1)}, bf16[2,32,8192]{2,1,0:T(8,128)(2,1)}, u32[]{:S(2)}, u32[]{:S(2)}) collective-permute-start(bf16[2,32,8192]{2,1,0:T(8,128)(2,1)} %pad_maximum_fusion.4), channel_id=1, source_target_pairs={{0,16},{1,17},{2,18},{3,19},{4,20},{5,21},{6,22},{7,23},{8,24},{9,... | collective-permute-start | bytes 3145736 | tf_op jit(solution)/shard_map/ppermute | solution.py:914
  566.0 25.7 %collective-permute-start.45 = (bf16[2,2,2,32,1536]{4,3,2,1,0:T(8,128)(2,1)}, bf16[2,2,2,32,1536]{4,3,2,1,0:T(8,128)(2,1)}, u32[]{:S(2)}, u32[]{:S(2)}) collective-permute-start(bf16[2,2,2,32,1536]{4,3,2,1,0:T(8,128)(2,1)} %fusion.9), channel_id=1, source_target_pairs={{0,1},{1,0},{2,3},{3,2},{4,5},{5,4},{6,7},{7,6},{8,9},{9,8},{10,11... | collective-permute-start | bytes 2359304 | tf_op jit(solution)/shard_map/ppermute | solution.py:914
  566.0 25.6 %collective-permute-start.44 = (bf16[2,160,1024]{2,1,0:T(8,128)(2,1)}, bf16[2,160,1024]{2,1,0:T(8,128)(2,1)}, u32[]{:S(2)}, u32[]{:S(2)}) collective-permute-start(bf16[2,160,1024]{2,1,0:T(8,128)(2,1)} %fusion.6), channel_id=1, source_target_pairs={{0,2},{1,3},{2,0},{3,1},{4,6},{5,7},{6,4},{7,5},{8,10},{9,11},{10,... | collective-permute-start | bytes 1966088 | tf_op jit(solution)/shard_map/ppermute | solution.py:914
  566.1 25.5 %collective-permute-start.43 = (bf16[32,8192]{1,0:T(8,128)(2,1)S(1)}, bf16[32,8192]{1,0:T(8,128)(2,1)}, u32[]{:S(2)}, u32[]{:S(2)}) collective-permute-start(bf16[32,8192]{1,0:T(8,128)(2,1)S(1)} %pad_maximum_fusion.10), channel_id=1, source_target_pairs={{0,8},{1,9},{2,10},{3,11},{4,12},{5,13},{6,14},{7,15},{8,0},{9,1},... | collective-permute-start | bytes 1572872 | tf_op jit(solution)/shard_map/ppermute | solution.py:914
  625.6 21.7 %collective-permute-start.52 = (bf16[2,2,32,1664]{3,2,1,0:T(8,128)(2,1)S(1)}, bf16[2,2,32,1664]{3,2,1,0:T(8,128)(2,1)S(1)}, u32[]{:S(2)}, u32[]{:S(2)}) collective-permute-start(bf16[2,2,32,1664]{3,2,1,0:T(8,128)(2,1)S(1)} %get-tuple-element.366), channel_id=1, source_target_pairs={{0,2},{1,3},{2,0},{3,1},{4,6},{5,7},{6,4},{7,5},{8,10},{9,11},{10,... | collective-permute-start | bytes 1277960 | tf_op jit(solution)/shard_map/ppermute | solution.py:914
  627.0 20.3 %collective-permute-start.53 = (bf16[2,2,32,1664]{3,2,1,0:T(8,128)(2,1)S(1)}, bf16[2,2,32,1664]{3,2,1,0:T(8,128)(2,1)S(1)}, u32[]{:S(2)}, u32[]{:S(2)}) collective-permute-start(bf16[2,2,32,1664]{3,2,1,0:T(8,128)(2,1)S(1)} %get-tuple-element.367), channel_id=1, source_target_pairs={{0,3},{1,2},{2,1},{3,0},{4,7},{5,6},{6,5},{7,4},{8,11},{9,10},{10,... | collective-permute-start | bytes 1277960 | tf_op jit(solution)/shard_map/ppermute | solution.py:914
  (65 other events, 766.8 us)
Sparse Core Ops, SparseCore 0:
  44.8 199.2 all-gather.2

commit v5 on v4

--- a/solution.py
+++ b/solution.py
@@ -926,14 +926,14 @@
             order = [o[levels - 1 - level] for o in orders]
             got = [self.swap(h, 1 << b) for h, b in zip(held, order)]
             masks = [m + [i | 1 << b for i in m] for m, b in zip(masks, order)]
-            if level in (0, 2):
-                moved[level : level + 2] = [
-                    self.move_one(moved[k], k) for k in (level, level + 1)
+            if level < 2:
+                moved[2 * level : 2 * level + 2] = [
+                    self.move_one(moved[k], k) for k in (2 * level, 2 * level + 1)
                 ]
             if level < len(self.dp_bits):
                 counts = counts + self.swap(counts, 1 << self.dp_bits[level])
             held = [jnp.concatenate([h, g], axis=0) for h, g in zip(held, got)]
-            if level in (1, 3):
+            if level < 2:
                 held, counts, moved = lax.optimization_barrier((held, counts, moved))
             else:
                 held, counts = lax.optimization_barrier((held, counts))

time: 694 us -> 686 us (0.988)
  starting transfers between devices: 72.1 us -> 64.2 us
    ppermute x8, waiting for transfers between devices: 28 us -> 15.6 us  [move_one(): return lax.ppermute(sent, BOTH, self.route(k))]
    all_gather x1, waiting for transfers between devices: 0.02 us -> 12.2 us  [body(): weights = regrouped(lax.all_gather(mine, BOTH, axis=0), each, width)]
    ppermute x43, starting transfers between devices: 47.2 us -> 39.7 us  [swap(): return lax.ppermute(value, BOTH, [(i, i ^ mask) for i in range(self.count)])]
  transfers between devices with their start and end apart: 60 -> 60, of which waited for: 23 -> 22; matrix products, arithmetic and copies ran while one was open for 9% -> 10% of each run, Pallas kernels for 45% -> 45%
where the time goes in v5:
time: 686 us; the launch traced here: 678 us
  Pallas kernels  397 us (58%)
  waiting for transfers between devices  109 us (16%)
  other arithmetic  70.3 us (10%)
  starting transfers between devices  64.2 us (9%)
  local copies, waits for them, and re-layouts  21.2 us (3%)
  between operations  16.4 us (2%)
    pallas_call x2, Pallas kernels, attend_back(): pl.pallas_call(functools.partial(attend_back_kernel, team=team), grid_spe...  107 us
    pallas_call x1, Pallas kernels, feed(): pl.pallas_call(functools.partial(feed_kernel, team=team), grid_spec=pltpu...  79 us
    ppermute x43, waiting for transfers between devices, swap(): return lax.ppermute(value, BOTH, [(i, i ^ mask) for i in range(self.count)])  77.2 us
    pallas_call x2, Pallas kernels, attend(): pl.pallas_call(functools.partial(attend_kernel, team=team), grid_spec=plt...  66.4 us
    pallas_call x6, Pallas kernels, weight_grad(): pl.pallas_call(functools.partial(weight_kernel, size=chunk), grid_spec=pl...  61.4 us
    convert_element_type x17, other arithmetic, split(): sent = [total(self.pick(m)).astype(self.wire) for m in self.masks[1:]]  44 us
    ppermute x43, starting transfers between devices, swap(): return lax.ppermute(value, BOTH, [(i, i ^ mask) for i in range(self.count)])  39.7 us
    pallas_call x2, Pallas kernels, project_back(): pl.pallas_call(functools.partial(project_back_kernel, part=part, lanes=wi...  24.5 us
  transfers between devices with their start and end apart: 60, of which 22 were waited for; matrix products, arithmetic and copies ran while one was open for 10% of the time, Pallas kernels for 45%

profile of v5, /device:TPU:0, one launch (start us, length us, event | category | flops | bytes accessed | tf_op | source)
XLA Modules:
  0.0 678.1 jit_solution(5133392158034813573)
XLA Ops:
  23.2 7.2 %collective-permute-done.1 = bf16[1,32,1664]{2,1,0:T(8,128)(2,1)S(1)} collective-permute-done((bf16[1,32,1664]{2,1,0:T(8,128)(2,1)S(1)}, bf16[1,32,1664]{2,1,0:T(8,128)(2,1)S(1)}, u32[]{:S(2)}, u32[]{:S(2)}) %collective-permute-start.1) | collective-permute-done | bytes 106528 | tf_op jit(solution)/shard_map/ppermute | solution.py:914
  72.6 14.5 %collective-permute-done.13 = bf16[8,32,1536]{2,1,0:T(8,128)(2,1)S(1)} collective-permute-done((bf16[8,32,1536]{2,1,0:T(8,128)(2,1)S(1)}, bf16[8,32,1536]{2,1,0:T(8,128)(2,1)S(1)}, u32[]{:S(2)}, u32[]{:S(2)}) %collective-permute-start.13) | collective-permute-done | bytes 786464 | tf_op jit(solution)/shard_map/ppermute | solution.py:914
  96.2 7.5 %place.1 = (bf16[3,32,32,1024]{3,2,1,0:T(8,128)(2,1)}, bf16[32,32,128]{2,1,0:T(8,128)(2,1)}) custom-call(s32[1]{0:T(128)} %bitcast.15.me_ref, bf16[16,32,1536]{2,1,0:T(8,128)(2,1)} %copy-done.2, bf16[16,32,1536]{2,1,0:T(8,128)(2,1)} %collective-permute-done.15.refs_1_, bf16[16,32,1664]{2,1,0:T(8,128)(2,1)} %copy-done.1, ...), custom_call_target="tpu_custom_call" | custom-call | tf_op jit(solution)/shard_map/place/pallas_call | solution.py:948
  105.5 12.3 %project.3 = (bf16[3,1024,512]{2,1,0:T(8,128)(2,1)}, bf16[1024,1024]{1,0:T(8,128)(2,1)}) custom-call(s32[1]{0:T(128)} %bitcast.19.at_ref, bf16[1024,1024]{1,0:T(8,128)(2,1)} %bitcast.316, bf16[3,1024,1024]{2,1,0:T(8,128)(2,1)} %bitcast.312, f32[4,1024]{1,0:T(4,128)} %bitcast.354, f32[1024,128]{1,0:T(8,128)} %pad_maximum_fusion.7.c_ref, ...), custom_call_target="tpu_custom_call" | custom-call | flops 50331648 | bytes 98304 | tf_op jit(solution)/shard_map/project/pallas_call | solution.py:151
  120.8 12.1 %project.2 = (bf16[3,1024,512]{2,1,0:T(8,128)(2,1)}, bf16[1024,1024]{1,0:T(8,128)(2,1)}) custom-call(s32[1]{0:T(128)} %bitcast.1.at_ref, bf16[1024,1024]{1,0:T(8,128)(2,1)} %bitcast.317, bf16[3,1024,1024]{2,1,0:T(8,128)(2,1)} %bitcast.313, f32[4,1024]{1,0:T(4,128)} %bitcast.355, f32[1024,128]{1,0:T(8,128)} %pad_maximum_fusion.7.c_ref, ...), custom_call_target="tpu_custom_call" | custom-call | flops 50331648 | bytes 98304 | tf_op jit(solution)/shard_map/project/pallas_call | solution.py:151
  143.9 33.4 %attend.2 = (bf16[1024,256]{1,0:T(8,128)(2,1)}, bf16[1024,256]{1,0:T(8,128)(2,1)}, f32[2,2,2048]{2,1,0:T(2,128)}) custom-call(s32[3]{0:T(128)} %pad_add_fusion.1.info_ref, bf16[3,1024,512]{2,1,0:T(8,128)(2,1)} %get-tuple-element.250.refs_0_.refs_2_.refs_4_, bf16[3,1024,512]{2,1,0:T(8,128)(2,1)} %copy-done, ...), custom_call_target="tpu_custom_call" | custom-call | flops 268435456 | bytes 65536 | tf_op jit(solution)/shard_map/attend/pallas_call | solution.py:255
  177.5 5.8 collective-permute-done.20.refs_2_
  185.4 33.0 %attend.3 = (bf16[1024,256]{1,0:T(8,128)(2,1)}, bf16[1024,256]{1,0:T(8,128)(2,1)}, f32[2,2,2048]{2,1,0:T(2,128)}) custom-call(s32[3]{0:T(128)} %pad_add_fusion.1.info_ref, bf16[3,1024,512]{2,1,0:T(8,128)(2,1)} %get-tuple-element.250.refs_0_.refs_2_.refs_4_, bf16[3,1024,512]{2,1,0:T(8,128)(2,1)} %copy-done, ...), custom_call_target="tpu_custom_call" | custom-call | flops 268435456 | bytes 65536 | tf_op jit(solution)/shard_map/attend/pallas_call | solution.py:255
  226.9 12.2 %all-gather.3.cloned.1.call-done = bf16[13312,1024]{1,0:T(8,128)(2,1)} async-done(((bf16[416,1024]{1,0:T(8,128)(2,1)}), bf16[13312,1024]{1,0:T(8,128)(2,1)}) %all-gather.3.cloned.1.call-update) | async-done | bytes 27262992 | tf_op jit(solution)/shard_map/all_gather | solution.py:1032
  239.1 79.0 %feed.1 = (bf16[1024,512]{1,0:T(8,128)(2,1)}, bf16[1024,512]{1,0:T(8,128)(2,1)}, bf16[1024,1024]{1,0:T(8,128)(2,1)}, f32[1024,1024]{1,0:T(8,128)}, bf16[1024,102...) custom-call(s32[1]{0:T(128)} %bitcast.1.at_ref, ...), custom_call_target="tpu_custom_call" | custom-call | flops 872415232 | bytes 1671168 | tf_op jit(solution)/shard_map/feed/pallas_call | solution.py:514
  322.0 13.2 %weight_grad.6 = (bf16[16,160,1024]{2,1,0:T(8,128)(2,1)}, bf16[16,160,1024]{2,1,0:T(8,128)(2,1)}) custom-call(s32[1]{0:T(128)} %bitcast.36.core_ref, bf16[1024,4096]{1,0:T(8,128)(2,1)} %get-tuple-element.255.a_ref, bf16[1024,1024]{1,0:T(8,128)(2,1)} %get-tuple-element.258.b_ref), custom_call_target="tpu_custom_call" | custom-call | flops 134217728 | bytes 294912 | tf_op jit(solution)/shard_map/weight_grad/pallas_call | solution.py:605
  335.2 6.3 weight_grad.7
  346.1 13.6 %weight_grad.8 = (bf16[512,4096]{1,0:T(8,128)(2,1)}, bf16[512,4096]{1,0:T(8,128)(2,1)}) custom-call(s32[1]{0:T(128)} %bitcast.36.core_ref, bf16[1024,1024]{1,0:T(8,128)(2,1)} %get-tuple-element.275.a_ref, bf16[1024,4096]{1,0:T(8,128)(2,1)} %get-tuple-element.277.b_ref), custom_call_target="tpu_custom_call" | custom-call | flops 134217728 | bytes 294912 | tf_op jit(solution)/shard_map/weight_grad/pallas_call | solution.py:605
  359.9 5.7 fusion
  365.7 13.4 %weight_grad.9 = (bf16[512,4096]{1,0:T(8,128)(2,1)}, bf16[512,4096]{1,0:T(8,128)(2,1)}) custom-call(s32[1]{0:T(128)} %bitcast.36.core_ref, bf16[1024,1024]{1,0:T(8,128)(2,1)} %get-tuple-element.275.a_ref, bf16[1024,4096]{1,0:T(8,128)(2,1)} %get-tuple-element.283.b_ref), custom_call_target="tpu_custom_call" | custom-call | flops 134217728 | bytes 294912 | tf_op jit(solution)/shard_map/weight_grad/pallas_call | solution.py:605
  397.7 53.3 %attend_back.2 = (bf16[3,1024,256]{2,1,0:T(8,128)(2,1)}, bf16[3,1024,256]{2,1,0:T(8,128)(2,1)}) custom-call(s32[3]{0:T(128)} %pad_add_fusion.1.info_ref, bf16[3,1024,512]{2,1,0:T(8,128)(2,1)} %get-tuple-element.250.refs_0_.refs_2_.refs_4_, bf16[3,1024,512]{2,1,0:T(8,128)(2,1)} %copy-done, bf16[3,1024,512]{2,1,0:T(8,128)(2,1)} %get-tuple-element.250.refs_0_.refs_2_.refs_4_, ...), custom_call_target="tpu_custom_call" | custom-call | flops 503316480 | bytes 131072 | tf_op jit(solution)/shard_map/attend_back/pallas_call | solution.py:396
  467.0 7.3 %weight_grad.10 = (bf16[512,1536]{1,0:T(8,128)(2,1)}, bf16[512,1536]{1,0:T(8,128)(2,1)}) custom-call(s32[1]{0:T(128)} %bitcast.36.core_ref, bf16[1024,1024]{1,0:T(8,128)(2,1)} %get-tuple-element.289.a_ref, bf16[3,1024,512]{2,1,0:T(8,128)(2,1)} %unturn.2.b_ref.low_ref), custom_call_target="tpu_custom_call" | custom-call | flops 50331648 | bytes 131072 | tf_op jit(solution)/shard_map/weight_grad/pallas_call | solution.py:605
  474.3 10.4 %project_back.2.refs_0_ = f32[1024,1024]{1,0:T(8,128)} custom-call(bf16[1024,1024]{1,0:T(8,128)(2,1)} %bitcast.319, f32[1024,1024]{1,0:T(8,128)} %get-tuple-element.306.gm_ref, f32[4,1024]{1,0:T(4,128)} %bitcast.357, bf16[3,1024,1024]{2,1,0:T(8,128)(2,1)} %bitcast.314, bf16[3,1024,512]{2,1,0:T(8,128)(2,1)} %unturn.2.b_ref.low_ref), custom_call_target="tpu_custom_call" | custom-call | flops 50331648 | bytes 393216 | tf_op jit(solution)/shard_map/project_back/pallas_call | solution.py:699
  495.4 53.7 %attend_back.3 = (bf16[3,1024,256]{2,1,0:T(8,128)(2,1)}, bf16[3,1024,256]{2,1,0:T(8,128)(2,1)}) custom-call(s32[3]{0:T(128)} %pad_add_fusion.1.info_ref, bf16[3,1024,512]{2,1,0:T(8,128)(2,1)} %get-tuple-element.250.refs_0_.refs_2_.refs_4_, bf16[3,1024,512]{2,1,0:T(8,128)(2,1)} %copy-done, bf16[3,1024,512]{2,1,0:T(8,128)(2,1)} %get-tuple-element.250.refs_0_.refs_2_.refs_4_, ...), custom_call_target="tpu_custom_call" | custom-call | flops 503316480 | bytes 131072 | tf_op jit(solution)/shard_map/attend_back/pallas_call | solution.py:396
  565.8 14.1 %project_back.3 = (bf16[1024,1024]{1,0:T(8,128)(2,1)}, f32[2,1024]{1,0:T(2,128)}) custom-call(bf16[1024,1024]{1,0:T(8,128)(2,1)} %bitcast.320, f32[1024,1024]{1,0:T(8,128)} %get-tuple-element.306.gm_ref, f32[4,1024]{1,0:T(4,128)} %bitcast.358, bf16[3,1024,1024]{2,1,0:T(8,128)(2,1)} %bitcast.315, bf16[3,1024,512]{2,1,0:T(8,128)(2,1)} %unturn.3.low_ref.b_ref, ...), custom_call_target="tpu_custom_call" | custom-call | flops 50331648 | bytes 393216 | tf_op jit(solution)/shard_map/project_back/pallas_call | solution.py:699
  593.6 7.5 %weight_grad.11 = (bf16[512,1536]{1,0:T(8,128)(2,1)}, bf16[512,1536]{1,0:T(8,128)(2,1)}) custom-call(s32[1]{0:T(128)} %bitcast.36.core_ref, bf16[1024,1024]{1,0:T(8,128)(2,1)} %get-tuple-element.289.a_ref, bf16[3,1024,512]{2,1,0:T(8,128)(2,1)} %unturn.3.low_ref.b_ref), custom_call_target="tpu_custom_call" | custom-call | flops 50331648 | bytes 131072 | tf_op jit(solution)/shard_map/weight_grad/pallas_call | solution.py:605
  621.1 6.5 collective-permute-done.48
  627.6 10.4 %collective-permute-done.52 = bf16[2,2,32,1664]{3,2,1,0:T(8,128)(2,1)S(1)} collective-permute-done((bf16[2,2,32,1664]{3,2,1,0:T(8,128)(2,1)S(1)}, bf16[2,2,32,1664]{3,2,1,0:T(8,128)(2,1)S(1)}, u32[]{:S(2)}, u32[]{:S(2)}) %collective-permute-start.52) | collective-permute-done | bytes 426016 | tf_op jit(solution)/shard_map/ppermute | solution.py:914
  650.3 10.4 %collective-permute-done.57 = bf16[32,3200]{1,0:T(8,128)(2,1)S(1)} collective-permute-done((bf16[32,3200]{1,0:T(8,128)(2,1)S(1)}, bf16[32,3200]{1,0:T(8,128)(2,1)S(1)}, u32[]{:S(2)}, u32[]{:S(2)}) %collective-permute-start.57) | collective-permute-done | bytes 204832 | tf_op jit(solution)/shard_map/ppermute | solution.py:914
  (273 shorter events, 218.6 us)
Async XLA Ops:
  7.2 232.0 %all-gather.3.cloned.1.call-start = ((), (), s32[]{:S(2)}) async-start(), calls=%async_computation | async-start | bytes 28114944 | tf_op jit(solution)/shard_map/all_gather | solution.py:1032
  69.4 17.8 %collective-permute-start.13 = (bf16[8,32,1536]{2,1,0:T(8,128)(2,1)S(1)}, bf16[8,32,1536]{2,1,0:T(8,128)(2,1)S(1)}, u32[]{:S(2)}, u32[]{:S(2)}) collective-permute-start(bf16[8,32,1536]{2,1,0:T(8,128)(2,1)S(1)} %pad_maximum_fusion.6), channel_id=1, source_target_pairs={{0,1},{1,0},{2,3},{3,2},{4,5},{5,4},{6,7},{7,6},{8,9},{9,8},{10,11... | collective-permute-start | bytes 2359304 | tf_op jit(solution)/shard_map/ppermute | solution.py:914
  132.9 44.6 %collective-permute-start.18 = (bf16[256,1024]{1,0:T(8,128)(2,1)}, bf16[256,1024]{1,0:T(8,128)(2,1)}, u32[]{:S(2)}, u32[]{:S(2)}) collective-permute-start(bf16[256,1024]{1,0:T(8,128)(2,1)} %get-tuple-element.230), channel_id=1, source_target_pairs={{0,0},{1,1},{2,4},{3,5},{4,2},{5,3},{6,6},{7,7},{8,8},{9,9},{10,12... | collective-permute-start | bytes 1572872 | tf_op jit(solution)/shard_map/ppermute | solution.py:879
  138.5 39.0 %collective-permute-start.19 = (bf16[256,1024]{1,0:T(8,128)(2,1)}, bf16[256,1024]{1,0:T(8,128)(2,1)}, u32[]{:S(2)}, u32[]{:S(2)}) collective-permute-start(bf16[256,1024]{1,0:T(8,128)(2,1)} %get-tuple-element.231), channel_id=1, source_target_pairs={{0,1},{1,0},{2,5},{3,4},{4,3},{5,2},{6,7},{7,6},{8,9},{9,8},{10,13... | collective-permute-start | bytes 1572872 | tf_op jit(solution)/shard_map/ppermute | solution.py:879
  140.0 43.3 %collective-permute-start.20 = (bf16[256,1024]{1,0:T(8,128)(2,1)}, bf16[256,1024]{1,0:T(8,128)(2,1)}, u32[]{:S(2)}, u32[]{:S(2)}) collective-permute-start(bf16[256,1024]{1,0:T(8,128)(2,1)} %get-tuple-element.232), channel_id=1, source_target_pairs={{0,4},{1,5},{2,0},{3,1},{4,6},{5,7},{6,2},{7,3},{8,12},{9,13},{10,... | collective-permute-start | bytes 1572872 | tf_op jit(solution)/shard_map/ppermute | solution.py:879
  140.0 45.4 %collective-permute-start.21 = (bf16[256,1024]{1,0:T(8,128)(2,1)}, bf16[256,1024]{1,0:T(8,128)(2,1)}, u32[]{:S(2)}, u32[]{:S(2)}) collective-permute-start(bf16[256,1024]{1,0:T(8,128)(2,1)} %get-tuple-element.233), channel_id=1, source_target_pairs={{0,5},{1,4},{2,1},{3,0},{4,7},{5,6},{6,3},{7,2},{8,13},{9,12},{10,... | collective-permute-start | bytes 1572872 | tf_op jit(solution)/shard_map/ppermute | solution.py:879
  177.2 49.6 %collective-permute-start.23 = (bf16[1024,256]{1,0:T(8,128)(2,1)}, bf16[1024,256]{1,0:T(8,128)(2,1)S(1)}, u32[]{:S(2)}, u32[]{:S(2)}) collective-permute-start(bf16[1024,256]{1,0:T(8,128)(2,1)} %get-tuple-element.249.refs_7_), channel_id=1, source_target_pairs={{0,4},{1,5},{2,6},{3,7},{4,0},{5,1},{6,2},{7,3},{8,12},{9,13},{10,... | collective-permute-start | bytes 1572872 | tf_op jit(solution)/shard_map/ppermute | solution.py:914
  341.6 18.3 %collective-permute-start.29 = (bf16[16,160,1024]{2,1,0:T(8,128)(2,1)}, bf16[16,160,1024]{2,1,0:T(8,128)(2,1)}, u32[]{:S(2)}, u32[]{:S(2)}) collective-permute-start(bf16[16,160,1024]{2,1,0:T(8,128)(2,1)} %get-tuple-element.280), channel_id=1, source_target_pairs={{0,4},{1,5},{2,6},{3,7},{4,0},{5,1},{6,2},{7,3},{8,12},{9,13},{10,... | collective-permute-start | bytes 15728648 | tf_op jit(solution)/shard_map/ppermute | solution.py:914
  359.7 19.9 %collective-permute-start.31 = (bf16[512,4096]{1,0:T(8,128)(2,1)}, bf16[512,4096]{1,0:T(8,128)(2,1)}, u32[]{:S(2)}, u32[]{:S(2)}) collective-permute-start(bf16[512,4096]{1,0:T(8,128)(2,1)} %get-tuple-element.294), channel_id=1, source_target_pairs={{0,4},{1,5},{2,6},{3,7},{4,0},{5,1},{6,2},{7,3},{8,12},{9,13},{10,... | collective-permute-start | bytes 12582920 | tf_op jit(solution)/shard_map/ppermute | solution.py:914
  379.6 75.3 %collective-permute-start.34 = (bf16[2,2,2,160,1024]{4,3,2,1,0:T(8,128)(2,1)}, bf16[2,2,2,160,1024]{4,3,2,1,0:T(8,128)(2,1)}, u32[]{:S(2)}, u32[]{:S(2)}) collective-permute-start(bf16[2,2,2,160,1024]{4,3,2,1,0:T(8,128)(2,1)} %fusion), channel_id=1, source_target_pairs={{0,8},{1,9},{2,10},{3,11},{4,12},{5,13},{6,14},{7,15},{8,0},{9,1},... | collective-permute-start | bytes 7864328 | tf_op jit(solution)/shard_map/ppermute | solution.py:914
  391.8 63.1 %collective-permute-start.35 = (bf16[2,2,2,32,4096]{4,3,2,1,0:T(8,128)(2,1)}, bf16[2,2,2,32,4096]{4,3,2,1,0:T(8,128)(2,1)S(1)}, u32[]{:S(2)}, u32[]{:S(2)}) collective-permute-start(bf16[2,2,2,32,4096]{4,3,2,1,0:T(8,128)(2,1)} %fusion.2), channel_id=1, source_target_pairs={{0,1},{1,0},{2,3},{3,2},{4,5},{5,4},{6,7},{7,6},{8,9},{9,8},{10,11... | collective-permute-start | bytes 6291464 | tf_op jit(solution)/shard_map/ppermute | solution.py:914
  396.8 58.1 %collective-permute-start.36 = (bf16[2,2,2,32,4096]{4,3,2,1,0:T(8,128)(2,1)}, bf16[2,2,2,32,4096]{4,3,2,1,0:T(8,128)(2,1)}, u32[]{:S(2)}, u32[]{:S(2)}) collective-permute-start(bf16[2,2,2,32,4096]{4,3,2,1,0:T(8,128)(2,1)} %fusion.3), channel_id=1, source_target_pairs={{0,2},{1,3},{2,0},{3,1},{4,6},{5,7},{6,4},{7,5},{8,10},{9,11},{10,... | collective-permute-start | bytes 6291464 | tf_op jit(solution)/shard_map/ppermute | solution.py:914
  460.3 28.5 %collective-permute-start.37 = (bf16[2,2,32,4096]{3,2,1,0:T(8,128)(2,1)}, bf16[2,2,32,4096]{3,2,1,0:T(8,128)(2,1)}, u32[]{:S(2)}, u32[]{:S(2)}) collective-permute-start(bf16[2,2,32,4096]{3,2,1,0:T(8,128)(2,1)} %fusion.5), channel_id=1, source_target_pairs={{0,2},{1,3},{2,0},{3,1},{4,6},{5,7},{6,4},{7,5},{8,10},{9,11},{10,... | collective-permute-start | bytes 3145736 | tf_op jit(solution)/shard_map/ppermute | solution.py:914
  460.4 28.4 %collective-permute-start.38 = (bf16[2,2,32,4096]{3,2,1,0:T(8,128)(2,1)S(1)}, bf16[2,2,32,4096]{3,2,1,0:T(8,128)(2,1)}, u32[]{:S(2)}, u32[]{:S(2)}) collective-permute-start(bf16[2,2,32,4096]{3,2,1,0:T(8,128)(2,1)S(1)} %fusion.4), channel_id=1, source_target_pairs={{0,1},{1,0},{2,3},{3,2},{4,5},{5,4},{6,7},{7,6},{8,9},{9,8},{10,11... | collective-permute-start | bytes 3145736 | tf_op jit(solution)/shard_map/ppermute | solution.py:914
  474.3 75.0 %collective-permute-start.42 = (bf16[512,1536]{1,0:T(8,128)(2,1)}, bf16[512,1536]{1,0:T(8,128)(2,1)}, u32[]{:S(2)}, u32[]{:S(2)}) collective-permute-start(bf16[512,1536]{1,0:T(8,128)(2,1)} %get-tuple-element.338), channel_id=1, source_target_pairs={{0,4},{1,5},{2,6},{3,7},{4,0},{5,1},{6,2},{7,3},{8,12},{9,13},{10,... | collective-permute-start | bytes 4718600 | tf_op jit(solution)/shard_map/ppermute | solution.py:914
  492.5 59.1 %collective-permute-start.41 = (bf16[2,2,160,1024]{3,2,1,0:T(8,128)(2,1)}, bf16[2,2,160,1024]{3,2,1,0:T(8,128)(2,1)}, u32[]{:S(2)}, u32[]{:S(2)}) collective-permute-start(bf16[2,2,160,1024]{3,2,1,0:T(8,128)(2,1)} %fusion.1), channel_id=1, source_target_pairs={{0,1},{1,0},{2,3},{3,2},{4,5},{5,4},{6,7},{7,6},{8,9},{9,8},{10,11... | collective-permute-start | bytes 3932168 | tf_op jit(solution)/shard_map/ppermute | solution.py:914
  493.6 58.0 %collective-permute-start.40 = (bf16[2,32,8192]{2,1,0:T(8,128)(2,1)}, bf16[2,32,8192]{2,1,0:T(8,128)(2,1)}, u32[]{:S(2)}, u32[]{:S(2)}) collective-permute-start(bf16[2,32,8192]{2,1,0:T(8,128)(2,1)} %pad_maximum_fusion.4), channel_id=1, source_target_pairs={{0,16},{1,17},{2,18},{3,19},{4,20},{5,21},{6,22},{7,23},{8,24},{9,... | collective-permute-start | bytes 3145736 | tf_op jit(solution)/shard_map/ppermute | solution.py:914
  558.6 24.1 %collective-permute-start.45 = (bf16[2,2,2,32,1536]{4,3,2,1,0:T(8,128)(2,1)}, bf16[2,2,2,32,1536]{4,3,2,1,0:T(8,128)(2,1)}, u32[]{:S(2)}, u32[]{:S(2)}) collective-permute-start(bf16[2,2,2,32,1536]{4,3,2,1,0:T(8,128)(2,1)} %fusion.9), channel_id=1, source_target_pairs={{0,1},{1,0},{2,3},{3,2},{4,5},{5,4},{6,7},{7,6},{8,9},{9,8},{10,11... | collective-permute-start | bytes 2359304 | tf_op jit(solution)/shard_map/ppermute | solution.py:914
  560.1 22.6 %collective-permute-start.44 = (bf16[2,160,1024]{2,1,0:T(8,128)(2,1)}, bf16[2,160,1024]{2,1,0:T(8,128)(2,1)}, u32[]{:S(2)}, u32[]{:S(2)}) collective-permute-start(bf16[2,160,1024]{2,1,0:T(8,128)(2,1)} %fusion.6), channel_id=1, source_target_pairs={{0,2},{1,3},{2,0},{3,1},{4,6},{5,7},{6,4},{7,5},{8,10},{9,11},{10,... | collective-permute-start | bytes 1966088 | tf_op jit(solution)/shard_map/ppermute | solution.py:914
  560.1 22.6 %collective-permute-start.43 = (bf16[32,8192]{1,0:T(8,128)(2,1)S(1)}, bf16[32,8192]{1,0:T(8,128)(2,1)}, u32[]{:S(2)}, u32[]{:S(2)}) collective-permute-start(bf16[32,8192]{1,0:T(8,128)(2,1)S(1)} %pad_maximum_fusion.10), channel_id=1, source_target_pairs={{0,8},{1,9},{2,10},{3,11},{4,12},{5,13},{6,14},{7,15},{8,0},{9,1},... | collective-permute-start | bytes 1572872 | tf_op jit(solution)/shard_map/ppermute | solution.py:914
  608.4 19.2 %collective-permute-start.49 = (bf16[2,2,32,1536]{3,2,1,0:T(8,128)(2,1)}, bf16[2,2,32,1536]{3,2,1,0:T(8,128)(2,1)S(1)}, u32[]{:S(2)}, u32[]{:S(2)}) collective-permute-start(bf16[2,2,32,1536]{3,2,1,0:T(8,128)(2,1)} %fusion.10), channel_id=1, source_target_pairs={{0,2},{1,3},{2,0},{3,1},{4,6},{5,7},{6,4},{7,5},{8,10},{9,11},{10,... | collective-permute-start | bytes 1179656 | tf_op jit(solution)/shard_map/ppermute | solution.py:914
  615.4 22.6 %collective-permute-start.52 = (bf16[2,2,32,1664]{3,2,1,0:T(8,128)(2,1)S(1)}, bf16[2,2,32,1664]{3,2,1,0:T(8,128)(2,1)S(1)}, u32[]{:S(2)}, u32[]{:S(2)}) collective-permute-start(bf16[2,2,32,1664]{3,2,1,0:T(8,128)(2,1)S(1)} %get-tuple-element.366), channel_id=1, source_target_pairs={{0,2},{1,3},{2,0},{3,1},{4,6},{5,7},{6,4},{7,5},{8,10},{9,11},{10,... | collective-permute-start | bytes 1277960 | tf_op jit(solution)/shard_map/ppermute | solution.py:914
  616.9 21.1 %collective-permute-start.53 = (bf16[2,2,32,1664]{3,2,1,0:T(8,128)(2,1)S(1)}, bf16[2,2,32,1664]{3,2,1,0:T(8,128)(2,1)S(1)}, u32[]{:S(2)}, u32[]{:S(2)}) collective-permute-start(bf16[2,2,32,1664]{3,2,1,0:T(8,128)(2,1)S(1)} %get-tuple-element.367), channel_id=1, source_target_pairs={{0,3},{1,2},{2,1},{3,0},{4,7},{5,6},{6,5},{7,4},{8,11},{9,10},{10,... | collective-permute-start | bytes 1277960 | tf_op jit(solution)/shard_map/ppermute | solution.py:914
  643.0 17.7 %collective-permute-start.57 = (bf16[32,3200]{1,0:T(8,128)(2,1)S(1)}, bf16[32,3200]{1,0:T(8,128)(2,1)S(1)}, u32[]{:S(2)}, u32[]{:S(2)}) collective-permute-start(bf16[32,3200]{1,0:T(8,128)(2,1)S(1)} %pad_maximum_fusion.15), channel_id=1, source_target_pairs={{0,16},{1,17},{2,18},{3,19},{4,20},{5,21},{6,22},{7,23},{8,24},{9,... | collective-permute-start | bytes 614408 | tf_op jit(solution)/shard_map/ppermute | solution.py:914
  (65 other events, 791.0 us)
Sparse Core Ops, SparseCore 0:
  52.7 186.4 all-gather.2

commit v6 on v5

--- a/solution.py
+++ b/solution.py
@@ -926,6 +926,8 @@
             order = [o[levels - 1 - level] for o in orders]
             got = [self.swap(h, 1 << b) for h, b in zip(held, order)]
             masks = [m + [i | 1 << b for i in m] for m, b in zip(masks, order)]
+            if level == 1:
+                early = got
             if level < 2:
                 moved[2 * level : 2 * level + 2] = [
                     self.move_one(moved[k], k) for k in (2 * level, 2 * level + 1)
@@ -937,8 +939,6 @@
                 held, counts, moved = lax.optimization_barrier((held, counts, moved))
             else:
                 held, counts = lax.optimization_barrier((held, counts))
-            if level == 1:
-                early = held
         got = [self.swap(h, 1 << self.core) for h in held]
         masks = [m + [i | 1 << self.core for i in m] for m in masks]
         args = [v for pair in zip(held, got) for v in pair]

time: 686 us -> 699 us (1.019)
  Pallas kernels: 397 us -> 277 us
  waiting for transfers between devices: 109 us -> 216 us
  starting transfers between devices: 64.2 us -> 90.2 us
    pallas_call x2, Pallas kernels: 107 us -> 23.8 us  [attend_back(): pl.pallas_call(functools.partial(attend_back_kernel, team=team), grid_spe...]
    ppermute x43, waiting for transfers between devices: 77.2 us -> 156 us  [swap(): return lax.ppermute(value, BOTH, [(i, i ^ mask) for i in range(self.count)])]
    pallas_call x2, Pallas kernels: 66.4 us -> 28.3 us  [attend(): pl.pallas_call(functools.partial(attend_kernel, team=team), grid_spec=plt...]
    ppermute x8, waiting for transfers between devices: 15.6 us -> 42.8 us  [move_one(): return lax.ppermute(sent, BOTH, self.route(k))]
    ppermute x43, starting transfers between devices: 39.7 us -> 59.8 us  [swap(): return lax.ppermute(value, BOTH, [(i, i ^ mask) for i in range(self.count)])]
  transfers between devices with their start and end apart: 60 -> 60, of which waited for: 22 -> 29; matrix products, arithmetic and copies ran while one was open for 10% -> 9% of each run, Pallas kernels for 45% -> 27%
where the time goes in v6:
time: 699 us; the launch traced here: 690 us
  Pallas kernels  277 us (40%)
  waiting for transfers between devices  216 us (31%)
  starting transfers between devices  90.2 us (13%)
  other arithmetic  70.1 us (10%)
  local copies, waits for them, and re-layouts  21.4 us (3%)
  between operations  16.4 us (2%)
    ppermute x43, waiting for transfers between devices, swap(): return lax.ppermute(value, BOTH, [(i, i ^ mask) for i in range(self.count)])  156 us
    pallas_call x1, Pallas kernels, feed(): pl.pallas_call(functools.partial(feed_kernel, team=team), grid_spec=pltpu...  79.1 us
    pallas_call x6, Pallas kernels, weight_grad(): pl.pallas_call(functools.partial(weight_kernel, size=chunk), grid_spec=pl...  61.4 us
    ppermute x43, starting transfers between devices, swap(): return lax.ppermute(value, BOTH, [(i, i ^ mask) for i in range(self.count)])  59.8 us
    convert_element_type x17, other arithmetic, split(): sent = [total(self.pick(m)).astype(self.wire) for m in self.masks[1:]]  43.9 us
    ppermute x8, waiting for transfers between devices, move_one(): return lax.ppermute(sent, BOTH, self.route(k))  42.8 us
    pallas_call x2, Pallas kernels, attend(): pl.pallas_call(functools.partial(attend_kernel, team=team), grid_spec=plt...  28.3 us
    pallas_call x2, Pallas kernels, project(): pl.pallas_call(project_kernel, grid_spec=pltpu.PrefetchScalarGridSpec(num...  25.3 us
  transfers between devices with their start and end apart: 60, of which 29 were waited for; matrix products, arithmetic and copies ran while one was open for 9% of the time, Pallas kernels for 27%

profile of v6, /device:TPU:0, one launch (start us, length us, event | category | flops | bytes accessed | tf_op | source)
XLA Modules:
  0.0 690.1 jit_solution(2845007217935044046)
XLA Ops:
  33.8 9.0 %collective-permute-done.5 = bf16[2,32,1536]{2,1,0:T(8,128)(2,1)S(1)} collective-permute-done((bf16[2,32,1536]{2,1,0:T(8,128)(2,1)S(1)}, bf16[2,32,1536]{2,1,0:T(8,128)(2,1)S(1)}, u32[]{:S(2)}, u32[]{:S(2)}) %collective-permute-start.5) | collective-permute-done | bytes 196640 | tf_op jit(solution)/shard_map/ppermute | solution.py:914
  49.9 8.8 %collective-permute-done.8.refs_2_ = bf16[256,1024]{1,0:T(8,128)(2,1)S(1)} collective-permute-done((bf16[256,1024]{1,0:T(8,128)(2,1)S(1)}, bf16[256,1024]{1,0:T(8,128)(2,1)S(1)}, u32[]{:S(2)}, u32[]{:S(2)}) %collective-permute-start.8) | collective-permute-done | bytes 524320 | tf_op jit(solution)/shard_map/ppermute | solution.py:879
  79.9 28.3 %collective-permute-done.13 = bf16[8,32,1536]{2,1,0:T(8,128)(2,1)S(1)} collective-permute-done((bf16[8,32,1536]{2,1,0:T(8,128)(2,1)S(1)}, bf16[8,32,1536]{2,1,0:T(8,128)(2,1)S(1)}, u32[]{:S(2)}, u32[]{:S(2)}) %collective-permute-start.13) | collective-permute-done | bytes 786464 | tf_op jit(solution)/shard_map/ppermute | solution.py:914
  127.5 12.4 %project.3 = (bf16[3,1024,512]{2,1,0:T(8,128)(2,1)}, bf16[1024,1024]{1,0:T(8,128)(2,1)}) custom-call(s32[1]{0:T(128)} %bitcast.19.at_ref, bf16[1024,1024]{1,0:T(8,128)(2,1)} %bitcast.316, bf16[3,1024,1024]{2,1,0:T(8,128)(2,1)} %bitcast.312, f32[4,1024]{1,0:T(4,128)} %bitcast.354, f32[1024,128]{1,0:T(8,128)} %pad_maximum_fusion.7.c_ref, ...), custom_call_target="tpu_custom_call" | custom-call | flops 50331648 | bytes 98304 | tf_op jit(solution)/shard_map/project/pallas_call | solution.py:151
  143.5 12.9 %project.2 = (bf16[3,1024,512]{2,1,0:T(8,128)(2,1)}, bf16[1024,1024]{1,0:T(8,128)(2,1)}) custom-call(s32[1]{0:T(128)} %bitcast.1.at_ref, bf16[1024,1024]{1,0:T(8,128)(2,1)} %bitcast.317, bf16[3,1024,1024]{2,1,0:T(8,128)(2,1)} %bitcast.313, f32[4,1024]{1,0:T(4,128)} %bitcast.355, f32[1024,128]{1,0:T(8,128)} %pad_maximum_fusion.7.c_ref, ...), custom_call_target="tpu_custom_call" | custom-call | flops 50331648 | bytes 98304 | tf_op jit(solution)/shard_map/project/pallas_call | solution.py:151
  167.7 14.3 %attend.2 = (bf16[1024,256]{1,0:T(8,128)(2,1)}, bf16[1024,256]{1,0:T(8,128)(2,1)}, f32[2,2,2048]{2,1,0:T(2,128)}) custom-call(s32[3]{0:T(128)} %pad_add_fusion.1.info_ref, bf16[3,1024,512]{2,1,0:T(8,128)(2,1)} %get-tuple-element.250.refs_0_.refs_2_.refs_4_, bf16[3,1024,512]{2,1,0:T(8,128)(2,1)} %copy-done, ...), custom_call_target="tpu_custom_call" | custom-call | flops 268435456 | bytes 65536 | tf_op jit(solution)/shard_map/attend/pallas_call | solution.py:255
  188.2 18.0 %collective-permute-done.20.refs_2_ = bf16[256,1024]{1,0:T(8,128)(2,1)} collective-permute-done((bf16[256,1024]{1,0:T(8,128)(2,1)}, bf16[256,1024]{1,0:T(8,128)(2,1)}, u32[]{:S(2)}, u32[]{:S(2)}) %collective-permute-start.20) | collective-permute-done | bytes 524320 | tf_op jit(solution)/shard_map/ppermute | solution.py:879
  209.0 14.0 %attend.3 = (bf16[1024,256]{1,0:T(8,128)(2,1)}, bf16[1024,256]{1,0:T(8,128)(2,1)}, f32[2,2,2048]{2,1,0:T(2,128)}) custom-call(s32[3]{0:T(128)} %pad_add_fusion.1.info_ref, bf16[3,1024,512]{2,1,0:T(8,128)(2,1)} %get-tuple-element.250.refs_0_.refs_2_.refs_4_, bf16[3,1024,512]{2,1,0:T(8,128)(2,1)} %copy-done, ...), custom_call_target="tpu_custom_call" | custom-call | flops 268435456 | bytes 65536 | tf_op jit(solution)/shard_map/attend/pallas_call | solution.py:255
  231.2 12.9 %all-gather.3.cloned.1.call-done = bf16[13312,1024]{1,0:T(8,128)(2,1)} async-done(((bf16[416,1024]{1,0:T(8,128)(2,1)}), bf16[13312,1024]{1,0:T(8,128)(2,1)}) %all-gather.3.cloned.1.call-update) | async-done | bytes 27262992 | tf_op jit(solution)/shard_map/all_gather | solution.py:1032
  244.2 79.1 %feed.1 = (bf16[1024,512]{1,0:T(8,128)(2,1)}, bf16[1024,512]{1,0:T(8,128)(2,1)}, bf16[1024,1024]{1,0:T(8,128)(2,1)}, f32[1024,1024]{1,0:T(8,128)}, bf16[1024,102...) custom-call(s32[1]{0:T(128)} %bitcast.1.at_ref, ...), custom_call_target="tpu_custom_call" | custom-call | flops 872415232 | bytes 1671168 | tf_op jit(solution)/shard_map/feed/pallas_call | solution.py:514
  325.6 8.8 %collective-permute-start.26 = (bf16[256,1024]{1,0:T(8,128)(2,1)S(1)}, bf16[256,1024]{1,0:T(8,128)(2,1)S(1)}, u32[]{:S(2)}, u32[]{:S(2)}) collective-permute-start(bf16[256,1024]{1,0:T(8,128)(2,1)S(1)} %get-tuple-element.263), channel_id=1, source_target_pairs={{1,0},{0,1},{5,2},{4,3},{3,4},{2,5},{7,6},{6,7},{9,8},{8,9},{13,10... | collective-permute-start | bytes 1572872 | tf_op jit(solution)/shard_map/ppermute | solution.py:892
  334.4 13.2 %weight_grad.6 = (bf16[16,160,1024]{2,1,0:T(8,128)(2,1)}, bf16[16,160,1024]{2,1,0:T(8,128)(2,1)}) custom-call(s32[1]{0:T(128)} %bitcast.36.core_ref, bf16[1024,4096]{1,0:T(8,128)(2,1)} %get-tuple-element.255.a_ref, bf16[1024,1024]{1,0:T(8,128)(2,1)} %get-tuple-element.258.b_ref), custom_call_target="tpu_custom_call" | custom-call | flops 134217728 | bytes 294912 | tf_op jit(solution)/shard_map/weight_grad/pallas_call | solution.py:605
  357.5 13.6 %weight_grad.8 = (bf16[512,4096]{1,0:T(8,128)(2,1)}, bf16[512,4096]{1,0:T(8,128)(2,1)}) custom-call(s32[1]{0:T(128)} %bitcast.36.core_ref, bf16[1024,1024]{1,0:T(8,128)(2,1)} %get-tuple-element.275.a_ref, bf16[1024,4096]{1,0:T(8,128)(2,1)} %get-tuple-element.277.b_ref), custom_call_target="tpu_custom_call" | custom-call | flops 134217728 | bytes 294912 | tf_op jit(solution)/shard_map/weight_grad/pallas_call | solution.py:605
  376.9 13.4 %weight_grad.9 = (bf16[512,4096]{1,0:T(8,128)(2,1)}, bf16[512,4096]{1,0:T(8,128)(2,1)}) custom-call(s32[1]{0:T(128)} %bitcast.36.core_ref, bf16[1024,1024]{1,0:T(8,128)(2,1)} %get-tuple-element.275.a_ref, bf16[1024,4096]{1,0:T(8,128)(2,1)} %get-tuple-element.283.b_ref), custom_call_target="tpu_custom_call" | custom-call | flops 134217728 | bytes 294912 | tf_op jit(solution)/shard_map/weight_grad/pallas_call | solution.py:605
  410.2 11.8 %attend_back.2 = (bf16[3,1024,256]{2,1,0:T(8,128)(2,1)}, bf16[3,1024,256]{2,1,0:T(8,128)(2,1)}) custom-call(s32[3]{0:T(128)} %pad_add_fusion.1.info_ref, bf16[3,1024,512]{2,1,0:T(8,128)(2,1)} %get-tuple-element.250.refs_0_.refs_2_.refs_4_, bf16[3,1024,512]{2,1,0:T(8,128)(2,1)} %copy-done, bf16[3,1024,512]{2,1,0:T(8,128)(2,1)} %get-tuple-element.250.refs_0_.refs_2_.refs_4_, ...), custom_call_target="tpu_custom_call" | custom-call | flops 503316480 | bytes 131072 | tf_op jit(solution)/shard_map/attend_back/pallas_call | solution.py:396
  425.8 26.5 %collective-permute-done.35 = bf16[2,2,2,32,4096]{4,3,2,1,0:T(8,128)(2,1)S(1)} collective-permute-done((bf16[2,2,2,32,4096]{4,3,2,1,0:T(8,128)(2,1)}, bf16[2,2,2,32,4096]{4,3,2,1,0:T(8,128)(2,1)S(1)}, u32[]{:S(2)}, u32[]{:S(2)}) %collective-permute-start.35) | collective-permute-done | bytes 2097184 | tf_op jit(solution)/shard_map/ppermute | solution.py:914
  463.8 11.5 %collective-permute-start.38 = (bf16[2,2,32,4096]{3,2,1,0:T(8,128)(2,1)S(1)}, bf16[2,2,32,4096]{3,2,1,0:T(8,128)(2,1)}, u32[]{:S(2)}, u32[]{:S(2)}) collective-permute-start(bf16[2,2,32,4096]{3,2,1,0:T(8,128)(2,1)S(1)} %fusion.4), channel_id=1, source_target_pairs={{0,1},{1,0},{2,3},{3,2},{4,5},{5,4},{6,7},{7,6},{8,9},{9,8},{10,11... | collective-permute-start | bytes 3145736 | tf_op jit(solution)/shard_map/ppermute | solution.py:914
  488.3 10.4 %project_back.2.refs_0_ = f32[1024,1024]{1,0:T(8,128)} custom-call(bf16[1024,1024]{1,0:T(8,128)(2,1)} %bitcast.319, f32[1024,1024]{1,0:T(8,128)} %get-tuple-element.306.gm_ref, f32[4,1024]{1,0:T(4,128)} %bitcast.357, bf16[3,1024,1024]{2,1,0:T(8,128)(2,1)} %bitcast.314, bf16[3,1024,512]{2,1,0:T(8,128)(2,1)} %unturn.2.b_ref.low_ref), custom_call_target="tpu_custom_call" | custom-call | flops 50331648 | bytes 393216 | tf_op jit(solution)/shard_map/project_back/pallas_call | solution.py:699
  506.5 12.0 %attend_back.3 = (bf16[3,1024,256]{2,1,0:T(8,128)(2,1)}, bf16[3,1024,256]{2,1,0:T(8,128)(2,1)}) custom-call(s32[3]{0:T(128)} %pad_add_fusion.1.info_ref, bf16[3,1024,512]{2,1,0:T(8,128)(2,1)} %get-tuple-element.250.refs_0_.refs_2_.refs_4_, bf16[3,1024,512]{2,1,0:T(8,128)(2,1)} %copy-done, bf16[3,1024,512]{2,1,0:T(8,128)(2,1)} %get-tuple-element.250.refs_0_.refs_2_.refs_4_, ...), custom_call_target="tpu_custom_call" | custom-call | flops 503316480 | bytes 131072 | tf_op jit(solution)/shard_map/attend_back/pallas_call | solution.py:396
  521.3 34.4 %collective-permute-done.40 = bf16[2,32,8192]{2,1,0:T(8,128)(2,1)} collective-permute-done((bf16[2,32,8192]{2,1,0:T(8,128)(2,1)}, bf16[2,32,8192]{2,1,0:T(8,128)(2,1)}, u32[]{:S(2)}, u32[]{:S(2)}) %collective-permute-start.40) | collective-permute-done | bytes 1048608 | tf_op jit(solution)/shard_map/ppermute | solution.py:914
  562.7 9.1 %collective-permute-start.45 = (bf16[2,2,2,32,1536]{4,3,2,1,0:T(8,128)(2,1)}, bf16[2,2,2,32,1536]{4,3,2,1,0:T(8,128)(2,1)}, u32[]{:S(2)}, u32[]{:S(2)}) collective-permute-start(bf16[2,2,2,32,1536]{4,3,2,1,0:T(8,128)(2,1)} %fusion.9), channel_id=1, source_target_pairs={{0,1},{1,0},{2,3},{3,2},{4,5},{5,4},{6,7},{7,6},{8,9},{9,8},{10,11... | collective-permute-start | bytes 2359304 | tf_op jit(solution)/shard_map/ppermute | solution.py:914
  579.0 14.1 %project_back.3 = (bf16[1024,1024]{1,0:T(8,128)(2,1)}, f32[2,1024]{1,0:T(2,128)}) custom-call(bf16[1024,1024]{1,0:T(8,128)(2,1)} %bitcast.320, f32[1024,1024]{1,0:T(8,128)} %get-tuple-element.306.gm_ref, f32[4,1024]{1,0:T(4,128)} %bitcast.358, bf16[3,1024,1024]{2,1,0:T(8,128)(2,1)} %bitcast.315, bf16[3,1024,512]{2,1,0:T(8,128)(2,1)} %unturn.3.low_ref.b_ref, ...), custom_call_target="tpu_custom_call" | custom-call | flops 50331648 | bytes 393216 | tf_op jit(solution)/shard_map/project_back/pallas_call | solution.py:699
  641.1 9.5 %collective-permute-done.52 = bf16[2,2,32,1664]{3,2,1,0:T(8,128)(2,1)S(1)} collective-permute-done((bf16[2,2,32,1664]{3,2,1,0:T(8,128)(2,1)S(1)}, bf16[2,2,32,1664]{3,2,1,0:T(8,128)(2,1)S(1)}, u32[]{:S(2)}, u32[]{:S(2)}) %collective-permute-start.52) | collective-permute-done | bytes 426016 | tf_op jit(solution)/shard_map/ppermute | solution.py:914
  663.0 9.6 %collective-permute-done.57 = bf16[32,3200]{1,0:T(8,128)(2,1)S(1)} collective-permute-done((bf16[32,3200]{1,0:T(8,128)(2,1)S(1)}, bf16[32,3200]{1,0:T(8,128)(2,1)S(1)}, u32[]{:S(2)}, u32[]{:S(2)}) %collective-permute-start.57) | collective-permute-done | bytes 204832 | tf_op jit(solution)/shard_map/ppermute | solution.py:914
  (273 shorter events, 266.2 us)
Async XLA Ops:
  7.2 237.0 %all-gather.3.cloned.1.call-start = ((), (), s32[]{:S(2)}) async-start(), calls=%async_computation | async-start | bytes 28114944 | tf_op jit(solution)/shard_map/all_gather | solution.py:1032
  76.4 31.8 %collective-permute-start.13 = (bf16[8,32,1536]{2,1,0:T(8,128)(2,1)S(1)}, bf16[8,32,1536]{2,1,0:T(8,128)(2,1)S(1)}, u32[]{:S(2)}, u32[]{:S(2)}) collective-permute-start(bf16[8,32,1536]{2,1,0:T(8,128)(2,1)S(1)} %pad_maximum_fusion.6), channel_id=1, source_target_pairs={{0,1},{1,0},{2,3},{3,2},{4,5},{5,4},{6,7},{7,6},{8,9},{9,8},{10,11... | collective-permute-start | bytes 2359304 | tf_op jit(solution)/shard_map/ppermute | solution.py:914
  78.2 30.9 %collective-permute-start.14 = (bf16[8,32,1664]{2,1,0:T(8,128)(2,1)S(1)}, bf16[8,32,1664]{2,1,0:T(8,128)(2,1)S(1)}, u32[]{:S(2)}, u32[]{:S(2)}) collective-permute-start(bf16[8,32,1664]{2,1,0:T(8,128)(2,1)S(1)} %pad_maximum_fusion.5), channel_id=1, source_target_pairs={{0,2},{1,3},{2,0},{3,1},{4,6},{5,7},{6,4},{7,5},{8,10},{9,11},{10,... | collective-permute-start | bytes 2555912 | tf_op jit(solution)/shard_map/ppermute | solution.py:914
  156.4 25.8 %collective-permute-start.18 = (bf16[256,1024]{1,0:T(8,128)(2,1)}, bf16[256,1024]{1,0:T(8,128)(2,1)}, u32[]{:S(2)}, u32[]{:S(2)}) collective-permute-start(bf16[256,1024]{1,0:T(8,128)(2,1)} %get-tuple-element.230), channel_id=1, source_target_pairs={{0,0},{1,1},{2,4},{3,5},{4,2},{5,3},{6,6},{7,7},{8,8},{9,9},{10,12... | collective-permute-start | bytes 1572872 | tf_op jit(solution)/shard_map/ppermute | solution.py:879
  161.9 26.3 %collective-permute-start.19 = (bf16[256,1024]{1,0:T(8,128)(2,1)}, bf16[256,1024]{1,0:T(8,128)(2,1)}, u32[]{:S(2)}, u32[]{:S(2)}) collective-permute-start(bf16[256,1024]{1,0:T(8,128)(2,1)} %get-tuple-element.231), channel_id=1, source_target_pairs={{0,1},{1,0},{2,5},{3,4},{4,3},{5,2},{6,7},{7,6},{8,9},{9,8},{10,13... | collective-permute-start | bytes 1572872 | tf_op jit(solution)/shard_map/ppermute | solution.py:879
  163.6 42.5 %collective-permute-start.20 = (bf16[256,1024]{1,0:T(8,128)(2,1)}, bf16[256,1024]{1,0:T(8,128)(2,1)}, u32[]{:S(2)}, u32[]{:S(2)}) collective-permute-start(bf16[256,1024]{1,0:T(8,128)(2,1)} %get-tuple-element.232), channel_id=1, source_target_pairs={{0,4},{1,5},{2,0},{3,1},{4,6},{5,7},{6,2},{7,3},{8,12},{9,13},{10,... | collective-permute-start | bytes 1572872 | tf_op jit(solution)/shard_map/ppermute | solution.py:879
  163.6 45.3 %collective-permute-start.21 = (bf16[256,1024]{1,0:T(8,128)(2,1)}, bf16[256,1024]{1,0:T(8,128)(2,1)}, u32[]{:S(2)}, u32[]{:S(2)}) collective-permute-start(bf16[256,1024]{1,0:T(8,128)(2,1)} %get-tuple-element.233), channel_id=1, source_target_pairs={{0,5},{1,4},{2,1},{3,0},{4,7},{5,6},{6,3},{7,2},{8,13},{9,12},{10,... | collective-permute-start | bytes 1572872 | tf_op jit(solution)/shard_map/ppermute | solution.py:879
  182.0 49.2 %collective-permute-start.23 = (bf16[1024,256]{1,0:T(8,128)(2,1)}, bf16[1024,256]{1,0:T(8,128)(2,1)S(1)}, u32[]{:S(2)}, u32[]{:S(2)}) collective-permute-start(bf16[1024,256]{1,0:T(8,128)(2,1)} %get-tuple-element.249.refs_7_), channel_id=1, source_target_pairs={{0,4},{1,5},{2,6},{3,7},{4,0},{5,1},{6,2},{7,3},{8,12},{9,13},{10,... | collective-permute-start | bytes 1572872 | tf_op jit(solution)/shard_map/ppermute | solution.py:914
  324.9 22.7 %collective-permute-start.25 = (bf16[256,1024]{1,0:T(8,128)(2,1)S(1)}, bf16[256,1024]{1,0:T(8,128)(2,1)S(1)}, u32[]{:S(2)}, u32[]{:S(2)}) collective-permute-start(bf16[256,1024]{1,0:T(8,128)(2,1)S(1)} %get-tuple-element.262), channel_id=1, source_target_pairs={{0,0},{1,1},{4,2},{5,3},{2,4},{3,5},{6,6},{7,7},{8,8},{9,9},{12,10... | collective-permute-start | bytes 1572872 | tf_op jit(solution)/shard_map/ppermute | solution.py:892
  325.6 22.0 %collective-permute-start.26 = (bf16[256,1024]{1,0:T(8,128)(2,1)S(1)}, bf16[256,1024]{1,0:T(8,128)(2,1)S(1)}, u32[]{:S(2)}, u32[]{:S(2)}) collective-permute-start(bf16[256,1024]{1,0:T(8,128)(2,1)S(1)} %get-tuple-element.263), channel_id=1, source_target_pairs={{1,0},{0,1},{5,2},{4,3},{3,4},{2,5},{7,6},{6,7},{9,8},{8,9},{13,10... | collective-permute-start | bytes 1572872 | tf_op jit(solution)/shard_map/ppermute | solution.py:892
  391.0 61.3 %collective-permute-start.34 = (bf16[2,2,2,160,1024]{4,3,2,1,0:T(8,128)(2,1)}, bf16[2,2,2,160,1024]{4,3,2,1,0:T(8,128)(2,1)}, u32[]{:S(2)}, u32[]{:S(2)}) collective-permute-start(bf16[2,2,2,160,1024]{4,3,2,1,0:T(8,128)(2,1)} %fusion), channel_id=1, source_target_pairs={{0,8},{1,9},{2,10},{3,11},{4,12},{5,13},{6,14},{7,15},{8,0},{9,1},... | collective-permute-start | bytes 7864328 | tf_op jit(solution)/shard_map/ppermute | solution.py:914
  404.3 47.9 %collective-permute-start.35 = (bf16[2,2,2,32,4096]{4,3,2,1,0:T(8,128)(2,1)}, bf16[2,2,2,32,4096]{4,3,2,1,0:T(8,128)(2,1)S(1)}, u32[]{:S(2)}, u32[]{:S(2)}) collective-permute-start(bf16[2,2,2,32,4096]{4,3,2,1,0:T(8,128)(2,1)} %fusion.2), channel_id=1, source_target_pairs={{0,1},{1,0},{2,3},{3,2},{4,5},{5,4},{6,7},{7,6},{8,9},{9,8},{10,11... | collective-permute-start | bytes 6291464 | tf_op jit(solution)/shard_map/ppermute | solution.py:914
  409.5 47.7 %collective-permute-start.36 = (bf16[2,2,2,32,4096]{4,3,2,1,0:T(8,128)(2,1)}, bf16[2,2,2,32,4096]{4,3,2,1,0:T(8,128)(2,1)}, u32[]{:S(2)}, u32[]{:S(2)}) collective-permute-start(bf16[2,2,2,32,4096]{4,3,2,1,0:T(8,128)(2,1)} %fusion.3), channel_id=1, source_target_pairs={{0,2},{1,3},{2,0},{3,1},{4,6},{5,7},{6,4},{7,5},{8,10},{9,11},{10,... | collective-permute-start | bytes 6291464 | tf_op jit(solution)/shard_map/ppermute | solution.py:914
  462.6 40.2 %collective-permute-start.37 = (bf16[2,2,32,4096]{3,2,1,0:T(8,128)(2,1)}, bf16[2,2,32,4096]{3,2,1,0:T(8,128)(2,1)}, u32[]{:S(2)}, u32[]{:S(2)}) collective-permute-start(bf16[2,2,32,4096]{3,2,1,0:T(8,128)(2,1)} %fusion.5), channel_id=1, source_target_pairs={{0,2},{1,3},{2,0},{3,1},{4,6},{5,7},{6,4},{7,5},{8,10},{9,11},{10,... | collective-permute-start | bytes 3145736 | tf_op jit(solution)/shard_map/ppermute | solution.py:914
  463.8 39.0 %collective-permute-start.38 = (bf16[2,2,32,4096]{3,2,1,0:T(8,128)(2,1)S(1)}, bf16[2,2,32,4096]{3,2,1,0:T(8,128)(2,1)}, u32[]{:S(2)}, u32[]{:S(2)}) collective-permute-start(bf16[2,2,32,4096]{3,2,1,0:T(8,128)(2,1)S(1)} %fusion.4), channel_id=1, source_target_pairs={{0,1},{1,0},{2,3},{3,2},{4,5},{5,4},{6,7},{7,6},{8,9},{9,8},{10,11... | collective-permute-start | bytes 3145736 | tf_op jit(solution)/shard_map/ppermute | solution.py:914
  488.3 30.8 %collective-permute-start.42 = (bf16[512,1536]{1,0:T(8,128)(2,1)}, bf16[512,1536]{1,0:T(8,128)(2,1)}, u32[]{:S(2)}, u32[]{:S(2)}) collective-permute-start(bf16[512,1536]{1,0:T(8,128)(2,1)} %get-tuple-element.338), channel_id=1, source_target_pairs={{0,4},{1,5},{2,6},{3,7},{4,0},{5,1},{6,2},{7,3},{8,12},{9,13},{10,... | collective-permute-start | bytes 4718600 | tf_op jit(solution)/shard_map/ppermute | solution.py:914
  506.5 49.2 %collective-permute-start.41 = (bf16[2,2,160,1024]{3,2,1,0:T(8,128)(2,1)}, bf16[2,2,160,1024]{3,2,1,0:T(8,128)(2,1)}, u32[]{:S(2)}, u32[]{:S(2)}) collective-permute-start(bf16[2,2,160,1024]{3,2,1,0:T(8,128)(2,1)} %fusion.1), channel_id=1, source_target_pairs={{0,1},{1,0},{2,3},{3,2},{4,5},{5,4},{6,7},{7,6},{8,9},{9,8},{10,11... | collective-permute-start | bytes 3932168 | tf_op jit(solution)/shard_map/ppermute | solution.py:914
  506.5 49.2 %collective-permute-start.40 = (bf16[2,32,8192]{2,1,0:T(8,128)(2,1)}, bf16[2,32,8192]{2,1,0:T(8,128)(2,1)}, u32[]{:S(2)}, u32[]{:S(2)}) collective-permute-start(bf16[2,32,8192]{2,1,0:T(8,128)(2,1)} %pad_maximum_fusion.4), channel_id=1, source_target_pairs={{0,16},{1,17},{2,18},{3,19},{4,20},{5,21},{6,22},{7,23},{8,24},{9,... | collective-permute-start | bytes 3145736 | tf_op jit(solution)/shard_map/ppermute | solution.py:914
  518.5 44.2 %collective-permute-start.39 = (bf16[3,1024,256]{2,1,0:T(8,128)(2,1)}, bf16[3,1024,256]{2,1,0:T(8,128)(2,1)}, u32[]{:S(2)}, u32[]{:S(2)}) collective-permute-start(bf16[3,1024,256]{2,1,0:T(8,128)(2,1)} %get-tuple-element.331), channel_id=1, source_target_pairs={{0,4},{1,5},{2,6},{3,7},{4,0},{5,1},{6,2},{7,3},{8,12},{9,13},{10,... | collective-permute-start | bytes 4718600 | tf_op jit(solution)/shard_map/ppermute | solution.py:914
  562.7 33.2 %collective-permute-start.45 = (bf16[2,2,2,32,1536]{4,3,2,1,0:T(8,128)(2,1)}, bf16[2,2,2,32,1536]{4,3,2,1,0:T(8,128)(2,1)}, u32[]{:S(2)}, u32[]{:S(2)}) collective-permute-start(bf16[2,2,2,32,1536]{4,3,2,1,0:T(8,128)(2,1)} %fusion.9), channel_id=1, source_target_pairs={{0,1},{1,0},{2,3},{3,2},{4,5},{5,4},{6,7},{7,6},{8,9},{9,8},{10,11... | collective-permute-start | bytes 2359304 | tf_op jit(solution)/shard_map/ppermute | solution.py:914
  571.8 24.1 %collective-permute-start.44 = (bf16[2,160,1024]{2,1,0:T(8,128)(2,1)}, bf16[2,160,1024]{2,1,0:T(8,128)(2,1)}, u32[]{:S(2)}, u32[]{:S(2)}) collective-permute-start(bf16[2,160,1024]{2,1,0:T(8,128)(2,1)} %fusion.6), channel_id=1, source_target_pairs={{0,2},{1,3},{2,0},{3,1},{4,6},{5,7},{6,4},{7,5},{8,10},{9,11},{10,... | collective-permute-start | bytes 1966088 | tf_op jit(solution)/shard_map/ppermute | solution.py:914
  573.3 22.6 %collective-permute-start.43 = (bf16[32,8192]{1,0:T(8,128)(2,1)S(1)}, bf16[32,8192]{1,0:T(8,128)(2,1)}, u32[]{:S(2)}, u32[]{:S(2)}) collective-permute-start(bf16[32,8192]{1,0:T(8,128)(2,1)S(1)} %pad_maximum_fusion.10), channel_id=1, source_target_pairs={{0,8},{1,9},{2,10},{3,11},{4,12},{5,13},{6,14},{7,15},{8,0},{9,1},... | collective-permute-start | bytes 1572872 | tf_op jit(solution)/shard_map/ppermute | solution.py:914
  628.5 22.0 %collective-permute-start.52 = (bf16[2,2,32,1664]{3,2,1,0:T(8,128)(2,1)S(1)}, bf16[2,2,32,1664]{3,2,1,0:T(8,128)(2,1)S(1)}, u32[]{:S(2)}, u32[]{:S(2)}) collective-permute-start(bf16[2,2,32,1664]{3,2,1,0:T(8,128)(2,1)S(1)} %get-tuple-element.366), channel_id=1, source_target_pairs={{0,2},{1,3},{2,0},{3,1},{4,6},{5,7},{6,4},{7,5},{8,10},{9,11},{10,... | collective-permute-start | bytes 1277960 | tf_op jit(solution)/shard_map/ppermute | solution.py:914
  629.6 20.9 %collective-permute-start.53 = (bf16[2,2,32,1664]{3,2,1,0:T(8,128)(2,1)S(1)}, bf16[2,2,32,1664]{3,2,1,0:T(8,128)(2,1)S(1)}, u32[]{:S(2)}, u32[]{:S(2)}) collective-permute-start(bf16[2,2,32,1664]{3,2,1,0:T(8,128)(2,1)S(1)} %get-tuple-element.367), channel_id=1, source_target_pairs={{0,3},{1,2},{2,1},{3,0},{4,7},{5,6},{6,5},{7,4},{8,11},{9,10},{10,... | collective-permute-start | bytes 1277960 | tf_op jit(solution)/shard_map/ppermute | solution.py:914
  (65 other events, 771.4 us)
Sparse Core Ops, SparseCore 0:
  44.1 200.0 all-gather.2
